TPU v7x, 32 devices: a whole 2x2x4 slice. The times are simulated.
32 devices in a mesh: dp: 8 (over y, x, core), tensor: 4 (over z).
Axes of the slice: x: 2, y: 2, z: 4, core: 2. Of those that a mesh axis runs over, the one named last changes fastest.
Arguments:
- tokens: bfloat16 [8, 256, 768], P('dp', 'tensor'), may hold values from -6 to 6
- condition: bfloat16 [8, 768], P('dp'), may hold values from -6 to 6
- cotangent: bfloat16 [8, 256, 768], P('dp', 'tensor'), may hold values from -6 to 6
- mod_weight: bfloat16 [2, 768, 6, 768], P(None, 'dp', None, 'tensor'), may hold values from -1 to 1
- mod_bias: bfloat16 [2, 6, 12, 64], P(None, None, 'tensor', 'dp'), may hold values from -3 to 3
- qkv_weight: bfloat16 [2, 768, 3, 768], P(None, 'dp', None, 'tensor'), may hold values from -1 to 1
- qv_bias: bfloat16 [2, 2, 12, 64], P(None, None, 'tensor', 'dp'), may hold values from -3 to 3
- out_weight: bfloat16 [2, 768, 768], P(None, 'tensor', 'dp'), may hold values from -1 to 1
- out_bias: bfloat16 [2, 12, 64], P(None, 'tensor', 'dp'), may hold values from -2 to 2
- up_weight: bfloat16 [2, 768, 3072], P(None, 'dp', 'tensor'), may hold values from -1 to 1
- up_bias: bfloat16 [2, 4, 768], P(None, 'tensor', 'dp'), may hold values from -3 to 3
- down_weight: bfloat16 [2, 3072, 768], P(None, 'tensor', 'dp'), may hold values from -1 to 1
- down_bias: bfloat16 [2, 12, 64], P(None, 'tensor', 'dp'), may hold values from -2 to 2
Outputs:
- output: bfloat16 [8, 256, 768], P('dp', 'tensor')
- grad_tokens: float32 [8, 256, 768], P('dp', 'tensor')
- grad_condition: float32 [8, 768], P('dp')
- grad_mod_weight: float32 [2, 768, 6, 768], P(None, 'dp', None, 'tensor')
- grad_mod_bias: float32 [2, 6, 12, 64], P(None, None, 'tensor', 'dp')
- grad_qkv_weight: float32 [2, 768, 3, 768], P(None, 'dp', None, 'tensor')
- grad_qv_bias: float32 [2, 2, 12, 64], P(None, None, 'tensor', 'dp')
- grad_out_weight: float32 [2, 768, 768], P(None, 'tensor', 'dp')
- grad_out_bias: float32 [2, 12, 64], P(None, 'tensor', 'dp')
- grad_up_weight: float32 [2, 768, 3072], P(None, 'dp', 'tensor')
- grad_up_bias: float32 [2, 4, 768], P(None, 'tensor', 'dp')
- grad_down_weight: float32 [2, 3072, 768], P(None, 'tensor', 'dp')
- grad_down_bias: float32 [2, 12, 64], P(None, 'tensor', 'dp')
All inputs are finite; a program needn't handle non-finite values.
Results may differ from a plain program's by a relative error of at most 0.018.
Values may be sent and summed in bfloat16 or wider, within the bound.
No kernel may reach another device: no remote copies, remote signals or barrier semaphores. Data moves between devices by JAX's collectives and lax.ppermute only.
A program may use at most 128 MiB of HBM per device.

v0:
```python
import math

import jax
import jax.numpy as jnp
from jax import lax
from jax.sharding import PartitionSpec as P

D = 768
HD = 64


epsilon = 1e-06


def normalize(values):
    centered = values - jnp.mean(values, axis=-1, keepdims=True)
    inverse = lax.rsqrt(jnp.mean(centered * centered, axis=-1, keepdims=True) + epsilon)
    return (centered * inverse, inverse)


def norm_back(incoming, normed, inverse):
    average = jnp.mean(incoming, axis=-1, keepdims=True)
    along = jnp.mean(incoming * normed, axis=-1, keepdims=True)
    return inverse * (incoming - average - normed * along)


def body(
    tokens,
    condition,
    cotangent,
    mod_weight,
    mod_bias,
    qkv_weight,
    qv_bias,
    out_weight,
    out_bias,
    up_weight,
    up_bias,
    down_weight,
    down_bias,
):
    layers = mod_weight.shape[0]
    rank = lax.axis_index("tensor")
    local_cols = mod_weight.shape[3]
    local_heads = local_cols // HD
    local_units = up_weight.shape[2]
    local_rows = tokens.shape[1]
    full_rows = local_rows * lax.axis_size("tensor")
    latent_count = tokens.shape[0]
    mod_rows = mod_weight.shape[1]
    scaling = 1.0 / math.sqrt(HD)

    def place(columns):
        return lax.dynamic_update_slice(jnp.zeros((D,), jnp.float32), columns, (rank * local_cols,))

    def own_columns(full):
        return lax.dynamic_slice_in_dim(full, rank * local_cols, local_cols)

    def sum_rows(term_fn):
        return lax.psum_scatter(
            term_fn(0, full_rows).astype(jnp.bfloat16), "tensor", scatter_dimension=0, tiled=True
        ).astype(jnp.float32)

    def all_rows(values):
        return lax.all_gather(values, "tensor", axis=0, tiled=True)

    def split_heads(values):
        return values.reshape(values.shape[0], latent_count, local_heads, HD)

    residual = jnp.transpose(tokens, (1, 0, 2)).astype(jnp.float32)
    grad_flow = jnp.transpose(cotangent, (1, 0, 2)).astype(jnp.float32)
    cond_full = condition.astype(jnp.float32)
    cond_act = jax.nn.silu(cond_full).astype(jnp.bfloat16)
    cond_every = lax.all_gather(cond_act, "dp", axis=0, tiled=True)
    cond_slice = lax.dynamic_slice_in_dim(cond_every, lax.axis_index("dp") * mod_rows, mod_rows, 1)
    cond_pieces = jnp.zeros((cond_every.shape[0], mod_rows), jnp.float32)
    saved = []
    for layer in range(layers):
        fetch_w_modul = mod_weight[layer]
        weights = (
            fetch_w_modul,
            lax.all_gather(mod_bias[layer], "dp", axis=2, tiled=True)
            .reshape(6, local_cols)
            .astype(jnp.float32),
            lax.all_gather(qkv_weight[layer], "dp", axis=0, tiled=True),
            lax.all_gather(qv_bias[layer], "dp", axis=2, tiled=True)
            .reshape(2, local_cols)
            .astype(jnp.float32),
            lax.all_gather(out_weight[layer], "dp", axis=1, tiled=True),
            lax.all_gather(out_bias[layer], "dp", axis=1, tiled=True)
            .reshape(local_cols)
            .astype(jnp.float32),
            lax.all_gather(up_weight[layer], "dp", axis=0, tiled=True),
            lax.all_gather(up_bias[layer], "dp", axis=1, tiled=True)
            .reshape(local_units)
            .astype(jnp.float32),
            lax.all_gather(down_weight[layer], "dp", axis=1, tiled=True),
            lax.all_gather(down_bias[layer], "dp", axis=1, tiled=True)
            .reshape(local_cols)
            .astype(jnp.float32),
        )
        (
            w_modul,
            b_modul,
            mixed_weight,
            b_mixed,
            output_weight,
            b_output,
            upward_weight,
            b_upward,
            downward_weight,
            b_downward,
        ) = weights
        partial_mod = jnp.einsum(
            "ld,dkc->lkc", cond_slice, w_modul, preferred_element_type=jnp.float32
        )
        mod_local = lax.psum_scatter(partial_mod, "dp", scatter_dimension=0, tiled=True) + b_modul
        modulation = lax.all_gather(mod_local, "tensor", axis=2, tiled=True)
        normed_one, inverse_one = normalize(residual)
        attn_in = (normed_one * (1.0 + modulation[:, 1]) + modulation[:, 0]).astype(jnp.bfloat16)
        attention_rows = all_rows(attn_in)
        mixed_heads = jnp.einsum(
            "rwj,jvo->rwvo", attention_rows, mixed_weight, preferred_element_type=jnp.float32
        )
        query = split_heads((mixed_heads[:, :, 0] + b_mixed[0]).astype(jnp.bfloat16))
        keys = split_heads(mixed_heads[:, :, 1].astype(jnp.bfloat16))
        values = split_heads((mixed_heads[:, :, 2] + b_mixed[1]).astype(jnp.bfloat16))
        scores = (
            jnp.einsum("qlhe,klhe->lhqk", query, keys, preferred_element_type=jnp.float32) * scaling
        )
        highest = jnp.max(scores, axis=-1, keepdims=True)
        expo = jnp.exp(scores - highest)
        totals = jnp.sum(expo, axis=-1, keepdims=True)
        log_total = highest + jnp.log(totals)
        probs_low = (expo / totals).astype(jnp.bfloat16)
        attention_result = jnp.einsum(
            "lhqk,klhe->qlhe", probs_low, values, preferred_element_type=jnp.float32
        )
        attention_result = attention_result.reshape(
            attention_result.shape[0], latent_count, local_cols
        ).astype(jnp.bfloat16)

        def output_rows(
            start,
            count,
            attention_result=attention_result,
            output_weight=output_weight,
            b_output=b_output,
        ):
            return jnp.einsum(
                "xrz,za->xra", attention_result, output_weight, preferred_element_type=jnp.float32
            ) + place(b_output)

        branch = sum_rows(output_rows)
        middle = residual + modulation[:, 2] * branch
        normed_two, inverse_two = normalize(middle)
        mlp_in = (normed_two * (1.0 + modulation[:, 4]) + modulation[:, 3]).astype(jnp.bfloat16)
        feedforward_rows = all_rows(mlp_in)
        hidden = (
            jnp.einsum(
                "pvg,go->pvo", feedforward_rows, upward_weight, preferred_element_type=jnp.float32
            )
            + b_upward
        )
        activated_hidden = jax.nn.gelu(hidden, approximate=False).astype(jnp.bfloat16)

        def down_rows(
            start,
            count,
            activated_hidden=activated_hidden,
            downward_weight=downward_weight,
            b_downward=b_downward,
        ):
            return jnp.einsum(
                "gkr,rz->gkz", activated_hidden, downward_weight, preferred_element_type=jnp.float32
            ) + place(b_downward)

        mlp_out = sum_rows(down_rows)
        saved.append(
            (
                weights,
                modulation,
                normed_one,
                inverse_one,
                attention_rows,
                query,
                keys,
                values,
                log_total,
                attention_result,
                branch,
                normed_two,
                inverse_two,
                feedforward_rows,
                hidden,
                activated_hidden,
                mlp_out,
            )
        )
        residual = middle + modulation[:, 5] * mlp_out
    output = jnp.transpose(residual, (1, 0, 2)).astype(jnp.bfloat16)
    layer_grads = [None] * layers
    modul_grads = [None] * layers
    for layer in reversed(range(layers)):
        (
            weights,
            modulation,
            normed_one,
            inverse_one,
            attention_rows,
            query,
            keys,
            values,
            log_total,
            attention_result,
            branch,
            normed_two,
            inverse_two,
            feedforward_rows,
            hidden,
            activated_hidden,
            mlp_out,
        ) = saved[layer]
        (
            w_modul,
            b_modul,
            mixed_weight,
            b_mixed,
            output_weight,
            b_output,
            upward_weight,
            b_upward,
            downward_weight,
            b_downward,
        ) = weights
        d_mlp = (grad_flow * modulation[:, 5]).astype(jnp.bfloat16)
        d_gate_two = jnp.sum(grad_flow * mlp_out, axis=0)
        feedforward_row_gradient = all_rows(d_mlp)
        grad_down_b = own_columns(
            jnp.sum(feedforward_row_gradient.astype(jnp.float32), axis=(0, 1))
        )
        grad_down_w = jnp.einsum(
            "qnz,qnp->zp",
            activated_hidden,
            feedforward_row_gradient,
            preferred_element_type=jnp.float32,
        )
        d_active = jnp.einsum(
            "iam,ym->iay",
            feedforward_row_gradient,
            downward_weight,
            preferred_element_type=jnp.float32,
        )
        cumulative = 0.5 * (1.0 + lax.erf(hidden * 0.7071067811865476))
        density = jnp.exp(-0.5 * hidden * hidden) * 0.3989422804014327
        hidden_gradient = (d_active * (cumulative + hidden * density)).astype(jnp.bfloat16)
        grad_up_w = jnp.einsum(
            "xtj,xtq->jq", feedforward_rows, hidden_gradient, preferred_element_type=jnp.float32
        )
        grad_up_b = jnp.sum(hidden_gradient.astype(jnp.float32), axis=(0, 1)).reshape(
            up_bias.shape[1], D
        )

        def up_back(start, count, hidden_gradient=hidden_gradient, upward_weight=upward_weight):
            return jnp.einsum(
                "wvp,yp->wvy", hidden_gradient, upward_weight, preferred_element_type=jnp.float32
            )

        d_mlp_in = sum_rows(up_back)
        d_shift_two = jnp.sum(d_mlp_in, axis=0)
        d_scale_two = jnp.sum(d_mlp_in * normed_two, axis=0)
        d_middle = grad_flow + norm_back(
            d_mlp_in * (1.0 + modulation[:, 4]), normed_two, inverse_two
        )
        d_branch = (d_middle * modulation[:, 2]).astype(jnp.bfloat16)
        d_gate_one = jnp.sum(d_middle * branch, axis=0)
        branch_row_gradient = all_rows(d_branch)
        grad_output_b = own_columns(jnp.sum(branch_row_gradient.astype(jnp.float32), axis=(0, 1)))
        grad_output_w = jnp.einsum(
            "mvr,mvb->rb", attention_result, branch_row_gradient, preferred_element_type=jnp.float32
        )
        d_attended = jnp.einsum(
            "gpw,bw->gpb", branch_row_gradient, output_weight, preferred_element_type=jnp.float32
        )
        d_attended = split_heads(d_attended.astype(jnp.bfloat16))
        scores = (
            jnp.einsum("qlhe,klhe->lhqk", query, keys, preferred_element_type=jnp.float32) * scaling
        )
        probs = jnp.exp(scores - log_total)
        probs_low = probs.astype(jnp.bfloat16)
        d_values = jnp.einsum(
            "lhqk,qlhe->klhe", probs_low, d_attended, preferred_element_type=jnp.float32
        ).astype(jnp.bfloat16)
        d_probs = jnp.einsum(
            "qlhe,klhe->lhqk", d_attended, values, preferred_element_type=jnp.float32
        )
        d_scores = (probs * (d_probs - jnp.sum(probs * d_probs, axis=-1, keepdims=True))).astype(
            jnp.bfloat16
        )
        d_query = (
            jnp.einsum("lhqk,klhe->qlhe", d_scores, keys, preferred_element_type=jnp.float32)
            * scaling
        ).astype(jnp.bfloat16)
        d_keys = (
            jnp.einsum("lhqk,qlhe->klhe", d_scores, query, preferred_element_type=jnp.float32)
            * scaling
        ).astype(jnp.bfloat16)
        row_count = d_query.shape[0]
        mixed_gradient = jnp.stack(
            [
                d_query.reshape(row_count, latent_count, local_cols),
                d_keys.reshape(row_count, latent_count, local_cols),
                d_values.reshape(row_count, latent_count, local_cols),
            ],
            axis=2,
        )
        grad_mixed_b = jnp.stack(
            [
                jnp.sum(mixed_gradient[:, :, 0].astype(jnp.float32), axis=(0, 1)),
                jnp.sum(mixed_gradient[:, :, 2].astype(jnp.float32), axis=(0, 1)),
            ]
        ).reshape(2, local_heads, HD)
        grad_mixed_w = jnp.einsum(
            "yia,yibz->abz", attention_rows, mixed_gradient, preferred_element_type=jnp.float32
        )

        def mixed_back(start, count, mixed_gradient=mixed_gradient, mixed_weight=mixed_weight):
            return jnp.einsum(
                "gyqo,jqo->gyj", mixed_gradient, mixed_weight, preferred_element_type=jnp.float32
            )

        d_attn_in = sum_rows(mixed_back)
        d_shift_one = jnp.sum(d_attn_in, axis=0)
        d_scale_one = jnp.sum(d_attn_in * normed_one, axis=0)
        grad_flow = d_middle + norm_back(
            d_attn_in * (1.0 + modulation[:, 1]), normed_one, inverse_one
        )
        d_mod_part = jnp.stack(
            [d_shift_one, d_scale_one, d_gate_one, d_shift_two, d_scale_two, d_gate_two], axis=1
        )
        d_modulation = lax.psum_scatter(
            d_mod_part, "tensor", scatter_dimension=2, tiled=True
        ).astype(jnp.bfloat16)
        grad_modul_b = jnp.sum(d_modulation.astype(jnp.float32), axis=0).reshape(6, local_heads, HD)
        d_mod_every = lax.all_gather(d_modulation, "dp", axis=0, tiled=True)
        modul_grads[layer] = jnp.einsum(
            "ld,lkc->dkc", cond_slice, d_mod_every, preferred_element_type=jnp.float32
        )
        cond_pieces = cond_pieces + jnp.einsum(
            "lkc,dkc->ld", d_mod_every, w_modul, preferred_element_type=jnp.float32
        )
        grad_output_b = grad_output_b.reshape(local_heads, HD)
        grad_down_b = grad_down_b.reshape(local_heads, HD)
        layer_grads[layer] = (
            lax.psum_scatter(grad_modul_b, "dp", scatter_dimension=2, tiled=True),
            lax.psum_scatter(grad_mixed_w, "dp", scatter_dimension=0, tiled=True),
            lax.psum_scatter(grad_mixed_b, "dp", scatter_dimension=2, tiled=True),
            lax.psum_scatter(grad_output_w, "dp", scatter_dimension=1, tiled=True),
            lax.psum_scatter(grad_output_b, "dp", scatter_dimension=1, tiled=True),
            lax.psum_scatter(grad_up_w, "dp", scatter_dimension=0, tiled=True),
            lax.psum_scatter(grad_up_b, "dp", scatter_dimension=1, tiled=True),
            lax.psum_scatter(grad_down_w, "dp", scatter_dimension=1, tiled=True),
            lax.psum_scatter(grad_down_b, "dp", scatter_dimension=1, tiled=True),
        )
    stacked = [
        jnp.stack([layer_grads[layer][member] for layer in range(layers)]) for member in range(9)
    ]
    modul_stack = jnp.stack(modul_grads)
    cond_grad = lax.all_to_all(cond_pieces, "dp", split_axis=0, concat_axis=1, tiled=True)
    grad_tokens = jnp.transpose(grad_flow, (1, 0, 2))
    cond_total = lax.psum(cond_grad, "tensor")
    sigmoid_cond = jax.nn.sigmoid(cond_full)
    grad_condition = cond_total * sigmoid_cond * (1.0 + cond_full * (1.0 - sigmoid_cond))
    return (
        output,
        grad_tokens,
        grad_condition,
        modul_stack,
        stacked[0],
        stacked[1],
        stacked[2],
        stacked[3],
        stacked[4],
        stacked[5],
        stacked[6],
        stacked[7],
        stacked[8],
    )


def solution(mesh):
    in_specs = (
        P("dp", "tensor", None),
        P("dp", None),
        P("dp", "tensor", None),
        P(None, "dp", None, "tensor"),
        P(None, None, "tensor", "dp"),
        P(None, "dp", None, "tensor"),
        P(None, None, "tensor", "dp"),
        P(None, "tensor", "dp"),
        P(None, "tensor", "dp"),
        P(None, "dp", "tensor"),
        P(None, "tensor", "dp"),
        P(None, "tensor", "dp"),
        P(None, "tensor", "dp"),
    )
    out_specs = (
        P("dp", "tensor", None),
        P("dp", "tensor", None),
        P("dp", None),
        P(None, "dp", None, "tensor"),
        P(None, None, "tensor", "dp"),
        P(None, "dp", None, "tensor"),
        P(None, None, "tensor", "dp"),
        P(None, "tensor", "dp"),
        P(None, "tensor", "dp"),
        P(None, "dp", "tensor"),
        P(None, "tensor", "dp"),
        P(None, "tensor", "dp"),
        P(None, "tensor", "dp"),
    )
    return jax.shard_map(body, mesh=mesh, in_specs=in_specs, out_specs=out_specs, check_vma=False)
```

profile of v0, /device:TPU:0, one launch (start us, length us, event | category | flops | bytes accessed | tf_op | source)
XLA Modules:
  0.0 1014.5 jit_solution(9846101790171975690)
XLA Ops:
  34.2 12.5 %all-gather.1 = bf16[1,768,3,192]{3,2,0,1:T(4,128)(2,1)S(1)} all-gather(bf16[1,96,3,192]{3,2,0,1:T(4,128)(2,1)S(1)} %copy.253), channel_id=3, replica_groups=mesh['dp'=8,'tensor'=4] {'dp'}, dimensions={1}, use_global_device_ids=true | all-gather | bytes 995328 | tf_op jit(solution)/shard_map/all_gather | solution.py:85
  80.7 15.0 %all_gather.95 = f32[1,6,768]{1,0,2:T(1,128)S(1)} all-gather(f32[1,6,192]{1,0,2:T(1,128)S(1)} %copy.159), channel_id=1, replica_groups=mesh['dp'=8,'tensor'=4] {'tensor'}, dimensions={2}, use_global_device_ids=true | all-gather | bytes 23040 | tf_op jit(solution)/shard_map/all_gather | solution.py:118
  95.7 13.7 %slice_reduce_fusion.5 = (f32[768]{0:T(1024)}, f32[768]{0:T(1024)}, f32[768]{0:T(1024)S(1)}, f32[768]{0:T(1024)S(1)}, f32[768]{0:T(1024)S(1)}, /*index=5*/f32[768]{0:T(1024)S(1)}) fusion(f32[1,6,768]{1,0,2:T(1,128)S(1)} %all_gather.95), kind=kLoop, calls=%fused_computation.145 | loop fusion | flops 1536 | bytes 36864 | tf_op jit(solution)/shard_map/slice | solution.py:200
  109.5 15.6 %all_gather.96 = bf16[256,1,768]{2,0,1:T(8,128)(2,1)S(1)} all-gather(bf16[64,1,768]{2,0,1:T(8,128)(2,1)S(1)} %fusion.128), channel_id=1, replica_groups=mesh['dp'=8,'tensor'=4] {'tensor'}, dimensions={0}, use_global_device_ids=true | all-gather | bytes 491520 | tf_op jit(solution)/shard_map/all_gather | solution.py:65
  130.9 12.8 %all-reduce.14 = (bf16[768]{0:T(1024)(128)(2,1)S(1)}, bf16[768]{0:T(1024)(128)(2,1)}) all-reduce(bf16[768]{0:T(1024)(128)(2,1)S(1)} %dynamic-update-slice, bf16[768]{0:T(1024)(128)(2,1)S(1)} %dynamic-update-slice.1), channel_id=8, replica_groups=mesh['dp'=8,'tensor'=4] {'dp'}, use_global_device_ids=true, to_apply=%add | all-reduce | flops 1536 | bytes 6144
  163.5 14.7 %all-gather.10 = bf16[1,768,3,192]{3,2,0,1:T(4,128)(2,1)S(1)} all-gather(bf16[1,96,3,192]{3,2,0,1:T(4,128)(2,1)S(1)} %copy.259), channel_id=12, replica_groups=mesh['dp'=8,'tensor'=4] {'dp'}, dimensions={1}, use_global_device_ids=true | all-gather | bytes 995328 | tf_op jit(solution)/shard_map/all_gather | solution.py:85
  204.2 14.7 %all_gather.101 = bf16[256,1,768]{2,0,1:T(8,128)(2,1)S(1)} all-gather(bf16[64,1,768]{2,0,1:T(8,128)(2,1)S(1)} %add_convert_fusion.4), channel_id=1, replica_groups=mesh['dp'=8,'tensor'=4] {'tensor'}, dimensions={0}, use_global_device_ids=true | all-gather | bytes 491520 | tf_op jit(solution)/shard_map/all_gather | solution.py:65
  239.8 15.7 %all_gather.107 = f32[1,6,768]{1,0,2:T(1,128)S(1)} all-gather(f32[1,6,192]{1,0,2:T(1,128)S(1)} %copy.174), channel_id=1, replica_groups=mesh['dp'=8,'tensor'=4] {'tensor'}, dimensions={2}, use_global_device_ids=true | all-gather | bytes 23040 | tf_op jit(solution)/shard_map/all_gather | solution.py:118
  255.4 13.7 %slice_reduce_fusion.1 = (f32[768]{0:T(1024)}, f32[768]{0:T(1024)}, f32[768]{0:T(1024)S(1)}, f32[768]{0:T(1024)S(1)}, f32[768]{0:T(1024)S(1)}, /*index=5*/f32[768]{0:T(1024)}) fusion(f32[1,6,768]{1,0,2:T(1,128)S(1)} %all_gather.107), kind=kLoop, calls=%fused_computation.139 | loop fusion | flops 1536 | bytes 36864 | tf_op jit(solution)/shard_map/slice | solution.py:200
  271.2 15.3 %all_gather.108 = bf16[256,1,768]{2,0,1:T(8,128)(2,1)S(1)} all-gather(bf16[64,1,768]{2,0,1:T(8,128)(2,1)S(1)} %add_convert_fusion.3), channel_id=1, replica_groups=mesh['dp'=8,'tensor'=4] {'tensor'}, dimensions={0}, use_global_device_ids=true | all-gather | bytes 491520 | tf_op jit(solution)/shard_map/all_gather | solution.py:65
  292.7 15.3 %all_gather.118 = bf16[256,1,768]{2,0,1:T(8,128)(2,1)S(1)} all-gather(bf16[64,1,768]{2,0,1:T(8,128)(2,1)S(1)} %fusion.157), channel_id=1, replica_groups=mesh['dp'=8,'tensor'=4] {'tensor'}, dimensions={0}, use_global_device_ids=true | all-gather | bytes 491520 | tf_op jit(solution)/shard_map/all_gather | solution.py:65
  313.3 15.5 %all_gather.113 = bf16[256,1,768]{2,0,1:T(8,128)(2,1)} all-gather(bf16[64,1,768]{2,0,1:T(8,128)(2,1)S(1)} %add_convert_fusion), channel_id=1, replica_groups=mesh['dp'=8,'tensor'=4] {'tensor'}, dimensions={0}, use_global_device_ids=true | all-gather | bytes 491520 | tf_op jit(solution)/shard_map/all_gather | solution.py:65
  342.2 22.2 %all-gather.30.cloned.1.call-done = bf16[1,768,768]{1,2,0:T(8,128)(2,1)} async-done(((bf16[1,768,96]{1,2,0:T(8,128)(2,1)}), bf16[1,768,768]{1,2,0:T(8,128)(2,1)}) %all-gather.30.cloned.1.call-update) | async-done | bytes 1179664 | tf_op jit(solution)/shard_map/all_gather | solution.py:97
  392.3 19.4 %reduce-scatter.49.cloned.1.call-done = bf16[64,1,768]{2,0,1:T(8,128)(2,1)} async-done(((bf16[256,1,768]{2,0,1:T(8,128)(2,1)}), bf16[64,1,768]{2,0,1:T(8,128)(2,1)}) %reduce-scatter.49.cloned.1.call-update) | async-done | bytes 98320 | tf_op jit(solution)/shard_map/reduce_scatter | solution.py:60
  414.8 14.8 %all_gather.119 = bf16[256,1,768]{2,0,1:T(8,128)(2,1)S(1)} all-gather(bf16[64,1,768]{2,0,1:T(8,128)(2,1)S(1)} %multiply_convert_fusion.4), channel_id=1, replica_groups=mesh['dp'=8,'tensor'=4] {'tensor'}, dimensions={0}, use_global_device_ids=true | all-gather | bytes 491520 | tf_op jit(solution)/shard_map/all_gather | solution.py:65
  435.5 18.8 %reduce-scatter.53.cloned.1.call-done = bf16[64,1,768]{2,0,1:T(8,128)(2,1)} async-done(((bf16[256,1,768]{2,0,1:T(8,128)(2,1)}), bf16[64,1,768]{2,0,1:T(8,128)(2,1)}) %reduce-scatter.53.cloned.1.call-update) | async-done | bytes 98320 | tf_op jit(solution)/shard_map/reduce_scatter | solution.py:60
  457.1 14.6 %all_gather.120 = bf16[256,1,768]{2,0,1:T(8,128)(2,1)S(1)} all-gather(bf16[64,1,768]{2,0,1:T(8,128)(2,1)S(1)} %multiply_convert_fusion.3), channel_id=1, replica_groups=mesh['dp'=8,'tensor'=4] {'tensor'}, dimensions={0}, use_global_device_ids=true | all-gather | bytes 491520 | tf_op jit(solution)/shard_map/all_gather | solution.py:65
  475.6 18.9 %reduce-scatter.55.cloned.1.call-done = bf16[64,1,768]{2,0,1:T(8,128)(2,1)} async-done(((bf16[256,1,768]{2,0,1:T(8,128)(2,1)}), bf16[64,1,768]{2,0,1:T(8,128)(2,1)}) %reduce-scatter.55.cloned.1.call-update) | async-done | bytes 98320 | tf_op jit(solution)/shard_map/reduce_scatter | solution.py:60
  497.8 14.8 %all_gather.121 = bf16[256,1,768]{2,0,1:T(8,128)(2,1)S(1)} all-gather(bf16[64,1,768]{2,0,1:T(8,128)(2,1)S(1)} %multiply_convert_fusion.2), channel_id=1, replica_groups=mesh['dp'=8,'tensor'=4] {'tensor'}, dimensions={0}, use_global_device_ids=true | all-gather | bytes 491520 | tf_op jit(solution)/shard_map/all_gather | solution.py:65
  525.2 11.6 %reduce-scatter.57.cloned.1.call-done = bf16[64,1,768]{2,0,1:T(8,128)(2,1)} async-done(((bf16[256,1,768]{2,0,1:T(8,128)(2,1)}), bf16[64,1,768]{2,0,1:T(8,128)(2,1)}) %reduce-scatter.57.cloned.1.call-update) | async-done | bytes 98320 | tf_op jit(solution)/shard_map/reduce_scatter | solution.py:60
  559.0 13.1 %reduce-scatter.81.cloned.1.call-done = f32[96,1]{1,0:T(8,128)} async-done(((f32[768,1]{1,0:T(8,128)}), f32[96,1]{1,0:T(8,128)}) %reduce-scatter.81.cloned.1.call-update) | async-done | bytes 400
  575.6 33.6 %reduce-scatter.79.cloned.1.call-done = f32[96,1]{1,0:T(8,128)} async-done(((f32[768,1]{1,0:T(8,128)}), f32[96,1]{1,0:T(8,128)}) %reduce-scatter.79.cloned.1.call-update) | async-done | bytes 400
  610.6 21.9 %reduce-scatter.71.cloned.1.call-done = f32[192,6]{1,0:T(8,128)} async-done(((f32[768,6]{1,0:T(8,128)}), f32[192,6]{1,0:T(8,128)}) %reduce-scatter.71.cloned.1.call-update) | async-done | bytes 4624
  643.6 25.9 %reduce-scatter.77.cloned.1.call-done = f32[96,192]{1,0:T(8,128)} async-done(((f32[768,192]{1,0:T(8,128)}), f32[96,192]{1,0:T(8,128)}) %reduce-scatter.77.cloned.1.call-update) | async-done | bytes 73744
  671.6 21.1 %reduce-scatter.73.cloned.1.call-done = f32[192,6]{1,0:T(8,128)} async-done(((f32[768,6]{1,0:T(8,128)}), f32[192,6]{1,0:T(8,128)}) %reduce-scatter.73.cloned.1.call-update) | async-done | bytes 4624
  707.4 25.2 %all-reduce.12 = (f32[6,3,64]{2,0,1:T(8,128)S(1)}, f32[6,3,64]{2,0,1:T(8,128)S(1)}, f32[2,3,64]{2,0,1:T(2,128)S(1)}, f32[2,3,64]{2,0,1:T(2,128)S(1)}, f32[3,64]{...) all-reduce(f32[6,3,64]{2,0,1:T(8,128)S(1)} %copy.201, ...), channel_id=33, replica_groups=mesh['dp'=8,'tensor'=4] {'dp'}, use_global_device_ids=true, to_apply=%region_48.49.clone | all-reduce | flops 3840 | bytes 30720
  749.5 26.2 %reduce-scatter.61.cloned.1.call-done = f32[96,3,192]{2,0,1:T(8,128)} async-done(((f32[768,3,192]{2,0,1:T(8,128)}), f32[96,3,192]{2,0,1:T(8,128)}) %reduce-scatter.61.cloned.1.call-update) | async-done | bytes 221200 | tf_op jit(solution)/shard_map/reduce_scatter | solution.py:356
  775.7 45.8 %reduce-scatter.59.cloned.1.call-done = f32[96,3,192]{2,0,1:T(8,128)} async-done(((f32[768,3,192]{2,0,1:T(8,128)}), f32[96,3,192]{2,0,1:T(8,128)}) %reduce-scatter.59.cloned.1.call-update) | async-done | bytes 221200 | tf_op jit(solution)/shard_map/reduce_scatter | solution.py:356
  823.5 44.3 %reduce-scatter.69.cloned.1.call-done = f32[768,96]{0,1:T(8,128)} async-done(((f32[768,768]{0,1:T(8,128)}), f32[768,96]{0,1:T(8,128)}) %reduce-scatter.69.cloned.1.call-update) | async-done | bytes 294928 | tf_op jit(solution)/shard_map/reduce_scatter | solution.py:362
  867.8 45.9 %reduce-scatter.67.cloned.1.call-done = f32[768,96]{0,1:T(8,128)} async-done(((f32[768,768]{0,1:T(8,128)}), f32[768,96]{0,1:T(8,128)}) %reduce-scatter.67.cloned.1.call-update) | async-done | bytes 294928 | tf_op jit(solution)/shard_map/reduce_scatter | solution.py:362
  915.6 44.2 %reduce-scatter.65.cloned.1.call-done = f32[96,768]{1,0:T(8,128)} async-done(((f32[768,768]{1,0:T(8,128)}), f32[96,768]{1,0:T(8,128)}) %reduce-scatter.65.cloned.1.call-update) | async-done | bytes 294928 | tf_op jit(solution)/shard_map/reduce_scatter | solution.py:360
  959.7 45.8 %reduce-scatter.63.cloned.1.call-done = f32[96,768]{1,0:T(8,128)} async-done(((f32[768,768]{1,0:T(8,128)}), f32[96,768]{1,0:T(8,128)}) %reduce-scatter.63.cloned.1.call-update) | async-done | bytes 294928 | tf_op jit(solution)/shard_map/reduce_scatter | solution.py:360
  (587 shorter events, 294.6 us)
Async XLA Ops:
  7.2 72.0 %all-reduce.17.cloned.1.call-start = ((), (), s32[]{:S(2)}) async-start(), calls=%async_computation.45 | async-start | bytes 196608
  22.7 177.8 %reduce-scatter.43.cloned.1.call-start = ((), (), s32[]{:S(2)}) async-start(), calls=%async_computation.21 | async-start | bytes 491520 | tf_op jit(solution)/shard_map/reduce_scatter | solution.py:60
  33.8 75.6 %copy-start.101 = (f32[64]{0:T(128)}, f32[64]{0:T(128)S(1)}, u32[]{:S(2)}) copy-start(f32[64]{0:T(128)S(1)} %broadcast_multiply_fusion.11) | copy-start | bytes 772
  34.0 75.4 %copy-start.120 = (f32[64]{0:T(128)}, f32[64]{0:T(128)S(1)}, u32[]{:S(2)}) copy-start(f32[64]{0:T(128)S(1)} %add_rsqrt_fusion.3) | copy-start | bytes 772
  57.5 68.3 %copy-start.80 = (f32[1,1,3,64]{3,2,1,0:T(4,128)}, f32[1,1,3,64]{3,2,1,0:T(4,128)S(1)}, u32[]{:S(2)}) copy-start(f32[1,1,3,64]{3,2,1,0:T(4,128)S(1)} %copy.164) | copy-start | bytes 2308
  57.6 68.8 %copy-start.112 = (f32[1,1,3,64]{3,2,1,0:T(4,128)}, f32[1,1,3,64]{3,2,1,0:T(4,128)S(1)}, u32[]{:S(2)}) copy-start(f32[1,1,3,64]{3,2,1,0:T(4,128)S(1)} %copy.163) | copy-start | bytes 2308
  128.1 90.8 %all-gather.24.cloned.1.call-start = ((), (), s32[]{:S(2)}) async-start(), calls=%async_computation.35 | async-start | bytes 1327104 | tf_op jit(solution)/shard_map/all_gather | solution.py:93
  128.9 94.2 %all-gather.26.cloned.1.call-start = ((), (), s32[]{:S(2)}) async-start(), calls=%async_computation.36 | async-start | bytes 1327104 | tf_op jit(solution)/shard_map/all_gather | solution.py:97
  129.7 139.4 %reduce-scatter.45.cloned.1.call-start = ((), (), s32[]{:S(2)}) async-start(), calls=%async_computation.22 | async-start | bytes 491520 | tf_op jit(solution)/shard_map/reduce_scatter | solution.py:60
  225.9 85.1 %reduce-scatter.47.cloned.1.call-start = ((), (), s32[]{:S(2)}) async-start(), calls=%async_computation.23 | async-start | bytes 491520 | tf_op jit(solution)/shard_map/reduce_scatter | solution.py:60
  290.5 47.4 %all-gather.28.cloned.1.call-start = ((), (), s32[]{:S(2)}) async-start(), calls=%async_computation.37 | async-start | bytes 1327104 | tf_op jit(solution)/shard_map/all_gather | solution.py:93
  291.2 73.2 %all-gather.30.cloned.1.call-start = ((), (), s32[]{:S(2)}) async-start(), calls=%async_computation.38 | async-start | bytes 1327104 | tf_op jit(solution)/shard_map/all_gather | solution.py:97
  292.0 98.7 %reduce-scatter.51.cloned.1.call-start = ((), (), s32[]{:S(2)}) async-start(), calls=%async_computation.25 | async-start | bytes 491520 | tf_op jit(solution)/shard_map/reduce_scatter | solution.py:60
  369.3 42.5 %reduce-scatter.49.cloned.1.call-start = ((), (), s32[]{:S(2)}) async-start(), calls=%async_computation.24 | async-start | bytes 491520 | tf_op jit(solution)/shard_map/reduce_scatter | solution.py:60
  389.2 65.1 %reduce-scatter.53.cloned.1.call-start = ((), (), s32[]{:S(2)}) async-start(), calls=%async_computation.26 | async-start | bytes 491520 | tf_op jit(solution)/shard_map/reduce_scatter | solution.py:60
  435.5 59.0 %reduce-scatter.55.cloned.1.call-start = ((), (), s32[]{:S(2)}) async-start(), calls=%async_computation.27 | async-start | bytes 491520 | tf_op jit(solution)/shard_map/reduce_scatter | solution.py:60
  475.5 61.2 %reduce-scatter.57.cloned.1.call-start = ((), (), s32[]{:S(2)}) async-start(), calls=%async_computation.28 | async-start | bytes 491520 | tf_op jit(solution)/shard_map/reduce_scatter | solution.py:60
  517.7 54.4 %reduce-scatter.81.cloned.1.call-start = ((), (), s32[]{:S(2)}) async-start(), calls=%async_computation.44 | async-start | bytes 442368
  518.7 90.4 %reduce-scatter.79.cloned.1.call-start = ((), (), s32[]{:S(2)}) async-start(), calls=%async_computation.43 | async-start | bytes 442368
  521.1 111.4 %reduce-scatter.71.cloned.1.call-start = ((), (), s32[]{:S(2)}) async-start(), calls=%async_computation.39 | async-start | bytes 491520
  522.9 146.6 %reduce-scatter.77.cloned.1.call-start = ((), (), s32[]{:S(2)}) async-start(), calls=%async_computation.42 | async-start | bytes 884736
  525.1 167.6 %reduce-scatter.73.cloned.1.call-start = ((), (), s32[]{:S(2)}) async-start(), calls=%async_computation.40 | async-start | bytes 491520
  541.4 206.4 %reduce-scatter.75.cloned.1.call-start = ((), (), s32[]{:S(2)}) async-start(), calls=%async_computation.41 | async-start | bytes 884736
  543.8 232.0 %reduce-scatter.61.cloned.1.call-start = ((), (), s32[]{:S(2)}) async-start(), calls=%async_computation.30 | async-start | bytes 2654208 | tf_op jit(solution)/shard_map/reduce_scatter | solution.py:356
  545.8 275.8 %reduce-scatter.59.cloned.1.call-start = ((), (), s32[]{:S(2)}) async-start(), calls=%async_computation.29 | async-start | bytes 2654208 | tf_op jit(solution)/shard_map/reduce_scatter | solution.py:356
  548.7 319.1 %reduce-scatter.69.cloned.1.call-start = ((), (), s32[]{:S(2)}) async-start(), calls=%async_computation.34 | async-start | bytes 2654208 | tf_op jit(solution)/shard_map/reduce_scatter | solution.py:362
  551.8 361.8 %reduce-scatter.67.cloned.1.call-start = ((), (), s32[]{:S(2)}) async-start(), calls=%async_computation.33 | async-start | bytes 2654208 | tf_op jit(solution)/shard_map/reduce_scatter | solution.py:362
  554.9 404.8 %reduce-scatter.65.cloned.1.call-start = ((), (), s32[]{:S(2)}) async-start(), calls=%async_computation.32 | async-start | bytes 2654208 | tf_op jit(solution)/shard_map/reduce_scatter | solution.py:360
  558.0 447.6 %reduce-scatter.63.cloned.1.call-start = ((), (), s32[]{:S(2)}) async-start(), calls=%async_computation.31 | async-start | bytes 2654208 | tf_op jit(solution)/shard_map/reduce_scatter | solution.py:360
  575.5 67.8 %copy-start.20 = (bf16[2,96,6,192]{3,1,2,0:T(8,128)(2,1)S(1)}, bf16[2,96,6,192]{3,1,2,0:T(8,128)(2,1)}, u32[]{:S(2)}) copy-start(bf16[2,96,6,192]{3,1,2,0:T(8,128)(2,1)} %param.16) | copy-start | bytes 1327108
  575.6 94.9 %copy-start.4 = (bf16[256,1,768]{2,0,1:T(8,128)(2,1)S(1)}, bf16[256,1,768]{2,0,1:T(8,128)(2,1)}, u32[]{:S(2)}) copy-start(bf16[256,1,768]{2,0,1:T(8,128)(2,1)} %copy-done.3) | copy-start | bytes 1179652
  704.1 32.9 %all-to-all-start = ((f32[8,1,96]{2,1,0:T(1,128)}), f32[8,1,96]{2,1,0:T(1,128)S(1)}, u32[]{:S(2)}, u32[]{:S(2)}) async-start(f32[8,1,96]{2,1,0:T(1,128)} %bitcast.88), calls=%async_computation.8 | async-start | bytes 8192 | tf_op jit(solution)/shard_map/all_to_all | solution.py:369
  (131 other events, 1592.5 us)
Sparse Core Ops, SparseCore 0:
  22.8 52.1 all-reduce.16
  128.2 20.5 reduce-scatter.42
  151.3 24.2 all-gather.23
  177.9 24.5 all-gather.25
  226.0 20.8 reduce-scatter.44
  290.6 20.3 reduce-scatter.46
  313.4 24.4 all-gather.27
  340.3 24.0 all-gather.29
  369.4 20.5 reduce-scatter.50
  392.8 18.8 reduce-scatter.48
  435.6 18.6 reduce-scatter.52
  475.6 18.8 reduce-scatter.54
  517.8 18.9 reduce-scatter.56
  539.9 32.0 reduce-scatter.80
  575.3 33.8 reduce-scatter.78
  611.9 20.5 reduce-scatter.70
  636.1 33.2 reduce-scatter.76
  672.1 20.5 reduce-scatter.72
  696.2 33.4 reduce-scatter.74
  733.3 42.4 reduce-scatter.60
  779.1 42.4 reduce-scatter.58
  825.3 42.4 reduce-scatter.68
  871.2 42.4 reduce-scatter.66
  917.2 42.4 reduce-scatter.64
  963.1 42.4 reduce-scatter.62
where the time goes:
time: 1020 us; the launch traced here: 1010 us
  waiting for transfers between devices  472 us (46%)
  blocking collectives  345 us (34%)
  other arithmetic  66.6 us (7%)
  matrix products  54.9 us (5%)
  local copies, waits for them, and re-layouts  53.4 us (5%)
  between operations  17.4 us (2%)
    all_gather x8, blocking collectives, all_rows(): return lax.all_gather(values, 'tensor', axis=0, tiled=True)  121 us
    unnamed x32, waiting for transfers between devices  117 us
    reduce_scatter x2, waiting for transfers between devices, body(): lax.psum_scatter(grad_down_w, 'dp', scatter_dimension=1, tiled=True)  90.1 us
    reduce_scatter x2, waiting for transfers between devices, body(): lax.psum_scatter(grad_up_w, 'dp', scatter_dimension=0, tiled=True)  90 us
    reduce_scatter x2, waiting for transfers between devices, body(): lax.psum_scatter(grad_mixed_w, 'dp', scatter_dimension=0, tiled=True)  72.1 us
    reduce_scatter x8, waiting for transfers between devices, sum_rows(): lax.psum_scatter(term_fn(0, full_rows).astype(jnp.bfloat16), 'tensor', sc...  71.5 us
    unnamed x2, blocking collectives  38 us
    unnamed x319, local copies, waits for them, and re-layouts  31.8 us
  transfers between devices with their start and end apart: 26, of which 18 were waited for; matrix products, arithmetic and copies ran while one was open for 11% of the time, Pallas kernels for 0%

commit v1 on v0

v1 whole, which is shorter than its diff:
```python
import math

import jax
import jax.numpy as jnp
from jax import lax
from jax.experimental import pallas as pl
from jax.experimental.pallas import tpu as pltpu
from jax.sharding import PartitionSpec as P

D = 768
HD = 64
EPS = 1e-06
AXES = ("dp", "tensor")
F32 = jnp.float32
BF16 = jnp.bfloat16

PARITY = 1
HALF = 2
CORE = 4
CHIP = 8


def call(kernel, out_shape, *args, flops=0, name=None):
    size = sum(a.size * a.dtype.itemsize for a in args) + sum(math.prod(o.shape) * o.dtype.itemsize for o in out_shape)
    return pl.pallas_call(
        kernel,
        out_shape=out_shape,
        in_specs=[pl.BlockSpec(memory_space=pltpu.VMEM)] * len(args),
        out_specs=[pl.BlockSpec(memory_space=pltpu.VMEM)] * len(out_shape),
        compiler_params=pltpu.CompilerParams(vmem_limit_bytes=48 * 1024 * 1024),
        cost_estimate=pl.CostEstimate(flops=flops, bytes_accessed=size, transcendentals=0),
        name=name,
    )(*args)


def sds(shape, dtype):
    return jax.ShapeDtypeStruct(shape, dtype)


def dot(a, b, ca=1, cb=0):
    return lax.dot_general(a, b, (((ca,), (cb,)), ((), ())), preferred_element_type=F32)


def normalize(values):
    centered = values - jnp.mean(values, axis=-1, keepdims=True)
    inverse = lax.rsqrt(jnp.mean(centered * centered, axis=-1, keepdims=True) + EPS)
    return centered * inverse, inverse


def norm_back(incoming, normed, inverse):
    average = jnp.mean(incoming, axis=-1, keepdims=True)
    along = jnp.mean(incoming * normed, axis=-1, keepdims=True)
    return inverse * (incoming - average - normed * along)


def col_sum(values):
    return jnp.sum(values, axis=0, keepdims=True)


def modulate(values, mod, shift, scale):
    normed, _ = normalize(values)
    return (normed * (1.0 + mod[scale : scale + 1]) + mod[shift : shift + 1]).astype(BF16)


def rows_of(refs):
    return jnp.concatenate([ref[...] for ref in refs], axis=0)


def split_out(total, keep_ref, send_ref):
    half = total.shape[0] // 2
    keep_ref[...] = total[:half]
    send_ref[...] = total[half:].astype(BF16)


def enter_kernel(res_ref, mod_ref, in_ref):
    in_ref[...] = modulate(res_ref[...], mod_ref[...], 0, 1)


def attention_kernel(x0, x1, x2, x3, w_ref, bias_ref, bo_ref, qkv_ref, att_ref, keep_ref, send_ref):
    x = rows_of((x0, x1, x2, x3))
    cols = w_ref.shape[1] // 4
    w = w_ref[...]
    qkv = (dot(x, w[:, : 3 * cols]) + bias_ref[...]).astype(BF16)
    qkv_ref[...] = qkv
    parts = []
    for head in range(cols // HD):
        at = head * HD
        q = qkv[:, at : at + HD]
        k = qkv[:, cols + at : cols + at + HD]
        v = qkv[:, 2 * cols + at : 2 * cols + at + HD]
        scores = dot(q, k, 1, 1) * (1.0 / math.sqrt(HD))
        expo = jnp.exp(scores - jnp.max(scores, axis=-1, keepdims=True))
        probs = expo / jnp.sum(expo, axis=-1, keepdims=True)
        parts.append(dot(probs.astype(BF16), v))
    att = jnp.concatenate(parts, axis=1).astype(BF16)
    att_ref[...] = att
    split_out(dot(att, w[:, 3 * cols :], 1, 1) + bo_ref[...], keep_ref, send_ref)


def middle_kernel(res_ref, mod_ref, part_ref, recv_ref, branch_ref, mid_ref, in_ref):
    mod = mod_ref[...]
    branch = part_ref[...] + recv_ref[...].astype(F32)
    branch_ref[...] = branch
    middle = res_ref[...] + mod[2:3] * branch
    mid_ref[...] = middle
    in_ref[...] = modulate(middle, mod, 3, 4)


def mlp_kernel(x0, x1, x2, x3, w_ref, bu_ref, bd_ref, hid_ref, act_ref, keep_ref, send_ref):
    x = rows_of((x0, x1, x2, x3))
    units = w_ref.shape[1] // 2
    hidden = dot(x, w_ref[:, :units]) + bu_ref[...]
    hid_ref[...] = hidden
    act = (0.5 * hidden * (1.0 + lax.erf(hidden * 0.7071067811865476))).astype(BF16)
    act_ref[...] = act
    split_out(dot(act, w_ref[:, units:], 1, 1) + bd_ref[...], keep_ref, send_ref)


def next_kernel(mid_ref, mod_ref, part_ref, recv_ref, mod_next_ref, out_ref, res_ref, in_ref):
    mlp_out = part_ref[...] + recv_ref[...].astype(F32)
    out_ref[...] = mlp_out
    residual = mid_ref[...] + mod_ref[5:6] * mlp_out
    res_ref[...] = residual
    in_ref[...] = modulate(residual, mod_next_ref[...], 0, 1)


def last_kernel(mid_ref, mod_ref, part_ref, recv_ref, g_ref, out_ref, dmlp_ref, dgate_ref):
    mlp_out = part_ref[...] + recv_ref[...].astype(F32)
    out_ref[...] = (mid_ref[...] + mod_ref[5:6] * mlp_out).astype(BF16)
    g = g_ref[...].astype(F32)
    dmlp_ref[...] = (g * mod_ref[5:6]).astype(BF16)
    dgate_ref[...] = col_sum(g * mlp_out)


def mlp_back_kernel(x0, x1, x2, x3, w_ref, hid_ref, dhid_ref, keep_ref, send_ref):
    x = rows_of((x0, x1, x2, x3))
    units = w_ref.shape[1] // 2
    hidden = hid_ref[...]
    d_active = dot(x, w_ref[:, units:])
    cumulative = 0.5 * (1.0 + lax.erf(hidden * 0.7071067811865476))
    density = jnp.exp(-0.5 * hidden * hidden) * 0.3989422804014327
    d_hidden = (d_active * (cumulative + hidden * density)).astype(BF16)
    dhid_ref[...] = d_hidden
    split_out(dot(d_hidden, w_ref[:, :units], 1, 1), keep_ref, send_ref)


def mlp_grad_kernel(y0, y1, y2, y3, x0, x1, x2, x3, dhid_ref, act_ref, grad_ref, bu_ref, bd_ref):
    y = rows_of((y0, y1, y2, y3))
    x = rows_of((x0, x1, x2, x3))
    units = act_ref.shape[1]
    d_hidden = dhid_ref[...]
    grad_ref[:, :units] = dot(x, d_hidden, 0, 0).astype(BF16)
    grad_ref[:, units:] = dot(y, act_ref[...], 0, 0).astype(BF16)
    bu_ref[...] = col_sum(d_hidden.astype(F32))
    bd_ref[...] = col_sum(y.astype(F32))


def middle_back_kernel(g_ref, mod_ref, part_ref, recv_ref, mid_ref, branch_ref, dmid_ref, dbranch_ref, sums_ref):
    mod = mod_ref[...]
    incoming = part_ref[...] + recv_ref[...].astype(F32)
    normed, inverse = normalize(mid_ref[...])
    d_middle = g_ref[...].astype(F32) + norm_back(incoming * (1.0 + mod[4:5]), normed, inverse)
    dmid_ref[...] = d_middle
    dbranch_ref[...] = (d_middle * mod[2:3]).astype(BF16)
    sums_ref[...] = jnp.concatenate(
        [col_sum(d_middle * branch_ref[...]), col_sum(incoming), col_sum(incoming * normed)], axis=0
    )


def attention_back_kernel(x0, x1, x2, x3, w_ref, qkv_ref, dqkv_ref, keep_ref, send_ref):
    x = rows_of((x0, x1, x2, x3))
    cols = w_ref.shape[1] // 4
    w = w_ref[...]
    qkv = qkv_ref[...]
    scaling = 1.0 / math.sqrt(HD)
    d_att = dot(x, w[:, 3 * cols :]).astype(BF16)
    grads = ([], [], [])
    for head in range(cols // HD):
        at = head * HD
        q = qkv[:, at : at + HD]
        k = qkv[:, cols + at : cols + at + HD]
        v = qkv[:, 2 * cols + at : 2 * cols + at + HD]
        d_out = d_att[:, at : at + HD]
        scores = dot(q, k, 1, 1) * scaling
        expo = jnp.exp(scores - jnp.max(scores, axis=-1, keepdims=True))
        probs = expo / jnp.sum(expo, axis=-1, keepdims=True)
        d_probs = dot(d_out, v, 1, 1)
        d_scores = (probs * (d_probs - jnp.sum(probs * d_probs, axis=-1, keepdims=True))).astype(BF16)
        grads[0].append(dot(d_scores, k) * scaling)
        grads[1].append(dot(d_scores, q, 0, 0) * scaling)
        grads[2].append(dot(probs.astype(BF16), d_out, 0, 0))
    d_qkv = jnp.concatenate(grads[0] + grads[1] + grads[2], axis=1).astype(BF16)
    dqkv_ref[...] = d_qkv
    split_out(dot(d_qkv, w[:, : 3 * cols], 1, 1), keep_ref, send_ref)


def attention_grad_kernel(y0, y1, y2, y3, x0, x1, x2, x3, dqkv_ref, att_ref, grad_ref, bqkv_ref, bo_ref):
    y = rows_of((y0, y1, y2, y3))
    x = rows_of((x0, x1, x2, x3))
    cols = att_ref.shape[1]
    d_qkv = dqkv_ref[...]
    grad_ref[...] = jnp.concatenate([dot(x, d_qkv, 0, 0), dot(y, att_ref[...], 0, 0)], axis=1).astype(BF16)
    bqkv_ref[...] = col_sum(d_qkv.astype(F32))
    bo_ref[...] = col_sum(y.astype(F32))


def enter_back(dmid_ref, mod_ref, part_ref, recv_ref, res_ref):
    incoming = part_ref[...] + recv_ref[...].astype(F32)
    normed, inverse = normalize(res_ref[...])
    g = dmid_ref[...] + norm_back(incoming * (1.0 + mod_ref[1:2]), normed, inverse)
    return g, col_sum(incoming), col_sum(incoming * normed)


def enter_back_kernel(dmid_ref, mod_ref, part_ref, recv_ref, res_ref, g_ref, sums_ref):
    g, shift, scale = enter_back(dmid_ref, mod_ref, part_ref, recv_ref, res_ref)
    g_ref[...] = g
    sums_ref[...] = jnp.concatenate([shift, scale], axis=0)


def previous_kernel(
    dmid_ref, mod_ref, part_ref, recv_ref, res_ref, mod_prev_ref, out_prev_ref, g_ref, sums_ref, dmlp_ref, dgate_ref
):
    g, shift, scale = enter_back(dmid_ref, mod_ref, part_ref, recv_ref, res_ref)
    g_ref[...] = g
    sums_ref[...] = jnp.concatenate([shift, scale], axis=0)
    dmlp_ref[...] = (g * mod_prev_ref[5:6]).astype(BF16)
    dgate_ref[...] = col_sum(g * out_prev_ref[...])


def body(
    tokens,
    condition,
    cotangent,
    mod_weight,
    mod_bias,
    qkv_weight,
    qv_bias,
    out_weight,
    out_bias,
    up_weight,
    up_bias,
    down_weight,
    down_bias,
):
    layers = mod_weight.shape[0]
    n_dp = lax.axis_size("dp")
    n_chips = n_dp // 2
    n_all = n_dp * 4
    dp = lax.axis_index("dp")
    z = lax.axis_index("tensor")
    chip = dp // 2
    core = dp % 2
    half = z // 2
    quarter = 2 * (half ^ core) + z % 2
    cols = mod_weight.shape[3]
    rows = tokens.shape[1]
    shard = qkv_weight.shape[1]
    units = up_weight.shape[2]
    piece = qv_bias.shape[3]

    def move(values, target):
        return lax.ppermute(values, AXES, [(i, target(i)) for i in range(n_all)])

    def xor(values, mask):
        return move(values, lambda i: i ^ mask)

    def swap_core_half(i):
        return i & ~6 | (i & HALF) << 1 | (i & CORE) >> 1

    def to_other(i):
        return i ^ CORE if i & CORE else i ^ CORE ^ HALF

    def from_other(i):
        return i ^ CORE ^ HALF if i & CORE else i ^ CORE

    def to_same(i):
        return i ^ HALF if i & CORE else i

    def pick(values, index):
        return lax.dynamic_index_in_dim(values, index, 0, keepdims=False)

    def chip_gather(values):
        if n_chips > 8:
            groups = [[2 * i + c for i in range(n_chips)] for c in range(2)]
            return lax.all_gather(values, "dp", axis_index_groups=groups)
        out = jnp.zeros((n_chips,) + values.shape, values.dtype)
        for j in range(n_chips):
            got = xor(values, CHIP * j) if j else values
            out = lax.dynamic_update_index_in_dim(out, got, chip ^ j, 0)
        return out

    def chip_swap(values):
        if n_chips > 8:
            groups = [[2 * i + c for i in range(n_chips)] for c in range(2)]
            got = lax.all_to_all(values, "dp", 0, 0, axis_index_groups=groups, tiled=True)
            return [got[i] for i in range(n_chips)]
        return [xor(pick(values, chip ^ j), CHIP * j) if j else pick(values, chip) for j in range(n_chips)]

    def chip_sum(values):
        return sum(part.astype(F32) for part in chip_swap(values))

    def fetch(own):
        same = move(own, to_same)
        other = move(own, to_other)
        pair = jnp.where(core == 0, jnp.stack([same, other]), jnp.stack([other, same]))
        return chip_gather(pair)

    def give(total):
        low = chip_sum(total).astype(BF16)
        same = move(pick(low, core), to_same)
        other = move(pick(low, core ^ 1), from_other)
        return same.astype(F32) + other.astype(F32)

    def all_rows(values):
        other = xor(values, PARITY)
        return (values, other, xor(values, CORE), xor(other, CORE))

    def sum_rows(keep, send):
        total = keep + xor(send, CORE).astype(F32)
        return total[:rows], xor(total[rows:].astype(BF16), PARITY)

    cond_full = condition.astype(F32)
    cond_act = jax.nn.silu(cond_full).astype(BF16)
    cond_other = xor(cond_act, CORE)
    cond_pair = jnp.where(core == 0, jnp.stack([cond_act, cond_other]), jnp.stack([cond_other, cond_act]))
    cond_every = chip_gather(cond_pair).reshape(n_dp, D)
    cond_slice = lax.dynamic_slice_in_dim(cond_every, dp * shard, shard, 1)
    bias_at = lax.dynamic_update_slice(
        jnp.zeros((layers, 6, cols // HD, HD), F32), mod_bias.astype(F32), (0, 0, 0, dp * piece)
    ).reshape(layers, 6, cols)
    partial_mod = jnp.einsum("ld,ydkc->lykc", cond_slice, mod_weight, preferred_element_type=F32) + bias_at
    mod_sum = chip_sum(partial_mod.reshape((n_chips, 2) + partial_mod.shape[1:]))
    mod_sum = mod_sum + xor(mod_sum, CORE)
    mod_own = pick(mod_sum, half)
    mod_far = pick(mod_sum, half ^ 1)
    modulation = jnp.zeros((4,) + mod_own.shape, F32)
    for mask in range(4):
        got = xor(mod_far if mask & HALF else mod_own, mask) if mask else mod_own
        modulation = lax.dynamic_update_index_in_dim(modulation, got, z ^ mask, 0)
    modulation = jnp.transpose(modulation, (1, 2, 0, 3)).reshape(layers, 6, D)

    moved = move(jnp.concatenate([tokens[0], cotangent[0]]), swap_core_half)
    residual = moved[:rows].astype(F32)
    cotan = moved[rows:]

    bias_len = 12 * piece + up_bias.shape[2]
    bias_vec = jnp.concatenate(
        [
            qv_bias.reshape(layers, 6 * piece),
            out_bias.reshape(layers, 3 * piece),
            down_bias.reshape(layers, 3 * piece),
            up_bias.reshape(layers, -1),
        ],
        axis=1,
    )
    bias_block = lax.dynamic_update_slice(jnp.zeros((16, D), BF16), bias_vec, (0, 0))
    attention_weights = []
    mlp_weights = []
    for layer in range(layers):
        own = jnp.concatenate([qkv_weight[layer].reshape(shard, 3 * cols), out_weight[layer].T], axis=1)
        if layer == 0:
            got = fetch(jnp.concatenate([own, bias_block])).reshape(n_dp, shard + 16, 4 * cols)
            bias_every = got[:, shard : shard + layers, :bias_len].astype(F32)
            attention_weights.append(got[:, :shard].reshape(D, 4 * cols))
        else:
            attention_weights.append(fetch(own).reshape(D, 4 * cols))
        own = jnp.concatenate([up_weight[layer], down_weight[layer].T], axis=1)
        mlp_weights.append(fetch(own).reshape(D, 2 * units))

    def heads_of(values, count):
        return jnp.transpose(values.reshape(n_dp, layers, count, 3, piece), (1, 2, 3, 0, 4)).reshape(layers, count, cols)

    head_bias = heads_of(bias_every[:, :, : 12 * piece], 4)
    qkv_bias_all = jnp.concatenate([head_bias[:, :1], jnp.zeros_like(head_bias[:, :1]), head_bias[:, 1:2]], axis=1)
    qkv_bias_all = qkv_bias_all.reshape(layers, 1, 3 * cols)
    wide_bias = lax.dynamic_update_slice(jnp.zeros((layers, 2, D), F32), head_bias[:, 2:4], (0, 0, quarter * cols))
    up_bias_all = jnp.transpose(bias_every[:, :, 12 * piece :], (1, 0, 2)).reshape(layers, 1, units)

    full = 4 * rows
    keep_send = [sds((full // 2, D), F32), sds((full // 2, D), BF16)]
    row_f32 = sds((rows, D), F32)
    row_bf16 = sds((rows, D), BF16)
    line = sds((1, D), F32)
    attention_flops = 2 * full * D * 4 * cols + 4 * full * full * cols
    mlp_flops = 4 * full * D * units

    saved = []
    (attn_in,) = call(enter_kernel, [row_bf16], residual, modulation[0], name="enter")
    for layer in range(layers):
        mod = modulation[layer]
        attn_rows = all_rows(attn_in)
        qkv, att, keep, send = call(
            attention_kernel,
            [sds((full, 3 * cols), BF16), sds((full, cols), BF16)] + keep_send,
            *attn_rows,
            attention_weights[layer],
            qkv_bias_all[layer],
            wide_bias[layer, :1],
            flops=attention_flops,
            name="attention",
        )
        branch, middle, mlp_in = call(
            middle_kernel, [row_f32, row_f32, row_bf16], residual, mod, *sum_rows(keep, send), name="middle"
        )
        mlp_rows = all_rows(mlp_in)
        hidden, act, keep, send = call(
            mlp_kernel,
            [sds((full, units), F32), sds((full, units), BF16)] + keep_send,
            *mlp_rows,
            mlp_weights[layer],
            up_bias_all[layer],
            wide_bias[layer, 1:],
            flops=mlp_flops,
            name="mlp",
        )
        part, recv = sum_rows(keep, send)
        saved.append((residual, attn_rows, qkv, att, branch, middle, mlp_rows, hidden, act))
        if layer + 1 < layers:
            mlp_out, residual, attn_in = call(
                next_kernel,
                [row_f32, row_f32, row_bf16],
                middle,
                mod,
                part,
                recv,
                modulation[layer + 1],
                name="next",
            )
            saved[-1] += (mlp_out,)
        else:
            output, d_mlp, d_gate_two = call(
                last_kernel, [row_bf16, row_bf16, line], middle, mod, part, recv, cotan, name="last"
            )

    output = move(output, swap_core_half)[None]
    flow = cotan
    mod_lines = [None] * layers
    packs = [None] * layers
    for layer in reversed(range(layers)):
        residual, attn_rows, qkv, att, branch, middle, mlp_rows, hidden, act = saved[layer][:9]
        mod = modulation[layer]
        d_mlp_rows = all_rows(d_mlp)
        d_hidden, keep, send = call(
            mlp_back_kernel,
            [sds((full, units), BF16)] + keep_send,
            *d_mlp_rows,
            mlp_weights[layer],
            hidden,
            flops=mlp_flops,
            name="mlp_back",
        )
        part, recv = sum_rows(keep, send)
        grad_mlp, grad_up_b, grad_down_b = call(
            mlp_grad_kernel,
            [sds((D, 2 * units), BF16), sds((1, units), F32), line],
            *d_mlp_rows,
            *mlp_rows,
            d_hidden,
            act,
            flops=mlp_flops,
            name="mlp_grad",
        )
        d_middle, d_branch, sums_mid = call(
            middle_back_kernel,
            [row_f32, row_bf16, sds((3, D), F32)],
            flow,
            mod,
            part,
            recv,
            middle,
            branch,
            name="middle_back",
        )
        d_branch_rows = all_rows(d_branch)
        d_qkv, keep, send = call(
            attention_back_kernel,
            [sds((full, 3 * cols), BF16)] + keep_send,
            *d_branch_rows,
            attention_weights[layer],
            qkv,
            flops=attention_flops * 2,
            name="attention_back",
        )
        part, recv = sum_rows(keep, send)
        grad_att, grad_qkv_b, grad_out_b = call(
            attention_grad_kernel,
            [sds((D, 4 * cols), BF16), sds((1, 3 * cols), F32), line],
            *d_branch_rows,
            *attn_rows,
            d_qkv,
            att,
            flops=attention_flops,
            name="attention_grad",
        )
        if layer:
            flow, sums_in, d_mlp, gate_next = call(
                previous_kernel,
                [row_f32, sds((2, D), F32), row_bf16, line],
                d_middle,
                mod,
                part,
                recv,
                residual,
                modulation[layer - 1],
                saved[layer - 1][9],
                name="previous",
            )
        else:
            flow, sums_in = call(
                enter_back_kernel,
                [row_f32, sds((2, D), F32)],
                d_middle,
                mod,
                part,
                recv,
                residual,
                name="enter_back",
            )
            gate_next = None
        mod_lines[layer] = jnp.concatenate([sums_in, sums_mid, d_gate_two], axis=0)
        d_gate_two = gate_next

        wide = lax.dynamic_slice(jnp.concatenate([grad_out_b, grad_down_b]), (0, quarter * cols), (2, cols))
        grad_heads = jnp.concatenate([grad_qkv_b[:, :cols], grad_qkv_b[:, 2 * cols :], wide])
        grad_heads = jnp.transpose(grad_heads.reshape(4, 3, n_dp, piece), (2, 0, 1, 3)).reshape(n_dp, 12 * piece)
        grad_vec = jnp.concatenate([grad_heads, grad_up_b.reshape(n_dp, -1)], axis=1).astype(BF16)
        grad_vec = jnp.pad(grad_vec[:, None], ((0, 0), (0, 15), (0, D - bias_len)))
        pack = jnp.concatenate([grad_att.reshape(n_dp, shard, 4 * cols), grad_vec], axis=1)
        packs[layer] = (
            give(pack.reshape(n_chips, 2, shard + 16, 4 * cols)),
            give(grad_mlp.reshape(n_chips, 2, shard, 2 * units)),
        )

    d_mod = jnp.stack(mod_lines)
    d_mod = d_mod + xor(d_mod, CORE)
    d_mod = (d_mod + xor(d_mod, PARITY)).astype(BF16).reshape(layers * 6, 4, cols)
    d_mod = jnp.transpose(d_mod, (1, 0, 2))
    mine = pick(d_mod, z)
    far = xor(pick(d_mod, z ^ HALF), HALF)
    d_mod_pair = jnp.where(half == 0, jnp.stack([mine, far]), jnp.stack([far, mine]))
    d_mod_every = chip_gather(d_mod_pair).reshape(n_dp, layers, 6, cols)
    grad_mod_w = jnp.einsum("ld,lykc->ydkc", cond_slice, d_mod_every, preferred_element_type=F32)
    grad_mod_b = jnp.sum(d_mod_every.astype(F32), axis=0).reshape(layers, 6, cols // HD, HD)
    grad_mod_b = lax.dynamic_slice_in_dim(grad_mod_b, dp * piece, piece, 3)
    cond_pieces = jnp.einsum("lykc,ydkc->ld", d_mod_every, mod_weight, preferred_element_type=F32)
    cond_pieces = jnp.stack(chip_swap(cond_pieces.reshape(n_chips, 2, shard)), axis=1)
    if n_chips <= 8:
        source = chip ^ jnp.arange(n_chips)
        cond_pieces = jnp.take(cond_pieces, source, axis=1)
    cond_mine = pick(cond_pieces, core)
    cond_sent = xor(pick(cond_pieces, core ^ 1), CORE)
    cond_total = jnp.where(
        core == 0, jnp.stack([cond_mine, cond_sent], axis=1), jnp.stack([cond_sent, cond_mine], axis=1)
    ).reshape(1, D)
    cond_total = cond_total + xor(cond_total, PARITY)
    cond_total = cond_total + xor(cond_total, HALF)
    sigmoid_cond = jax.nn.sigmoid(cond_full)
    grad_condition = cond_total * sigmoid_cond * (1.0 + cond_full * (1.0 - sigmoid_cond))

    grad_tokens = move(flow, swap_core_half)[None]
    att_pack = jnp.stack([packs[layer][0] for layer in range(layers)])
    mlp_pack = jnp.stack([packs[layer][1] for layer in range(layers)])
    vec = att_pack[:, shard, :bias_len]
    vec_heads = vec[:, : 12 * piece].reshape(layers, 4, 3, piece)
    return (
        output,
        grad_tokens,
        grad_condition,
        grad_mod_w,
        grad_mod_b,
        att_pack[:, :shard, : 3 * cols].reshape(layers, shard, 3, cols),
        vec_heads[:, :2],
        jnp.transpose(att_pack[:, :shard, 3 * cols :], (0, 2, 1)),
        vec_heads[:, 2],
        mlp_pack[:, :, :units],
        vec[:, 12 * piece :].reshape(layers, 1, -1),
        jnp.transpose(mlp_pack[:, :, units:], (0, 2, 1)),
        vec_heads[:, 3],
    )


def solution(mesh):
    in_specs = (
        P("dp", "tensor", None),
        P("dp", None),
        P("dp", "tensor", None),
        P(None, "dp", None, "tensor"),
        P(None, None, "tensor", "dp"),
        P(None, "dp", None, "tensor"),
        P(None, None, "tensor", "dp"),
        P(None, "tensor", "dp"),
        P(None, "tensor", "dp"),
        P(None, "dp", "tensor"),
        P(None, "tensor", "dp"),
        P(None, "tensor", "dp"),
        P(None, "tensor", "dp"),
    )
    out_specs = (
        P("dp", "tensor", None),
        P("dp", "tensor", None),
        P("dp", None),
        P(None, "dp", None, "tensor"),
        P(None, None, "tensor", "dp"),
        P(None, "dp", None, "tensor"),
        P(None, None, "tensor", "dp"),
        P(None, "tensor", "dp"),
        P(None, "tensor", "dp"),
        P(None, "dp", "tensor"),
        P(None, "tensor", "dp"),
        P(None, "tensor", "dp"),
        P(None, "tensor", "dp"),
    )
    return jax.shard_map(body, mesh=mesh, in_specs=in_specs, out_specs=out_specs, check_vma=False)
```

time: 1020 us -> 438 us (0.43)
  blocking collectives: 345 us -> 0 us
  waiting for transfers between devices: 472 us -> 146 us
  starting transfers between devices: 4.81 us -> 137 us
  matrix products: 54.9 us -> 1.62 us
  other arithmetic: 66.6 us -> 24.2 us
  local copies, waits for them, and re-layouts: 53.4 us -> 87.3 us
  Pallas kernels: 0 us -> 30.6 us
  between operations: 17.4 us -> 3.06 us
    reduce_scatter x14 -> x0, waiting for transfers between devices: 324 us -> none  [the longest x2 90.1 us: body(): lax.psum_scatter(grad_down_w, 'dp', scatter_dimension=1, tiled=True)]
    all_gather x25 -> x0, blocking collectives: 298 us -> none  [the longest x8 121 us: all_rows(): return lax.all_gather(values, 'tensor', axis=0, tiled=True)]
    ppermute x0 -> x106, waiting for transfers between devices: none -> 146 us  [move(): return lax.ppermute(values, AXES, [(i, target(i)) for i in range(n_all)])]
    ppermute x0 -> x106, starting transfers between devices: none -> 137 us  [move(): return lax.ppermute(values, AXES, [(i, target(i)) for i in range(n_all)])]
    unnamed x32 -> x0, waiting for transfers between devices: 117 us -> none
    dot_general x38 -> x3, matrix products: 49.6 us -> 1.62 us  [the longest x1 1.08 us: body(): jnp.einsum('ld,lykc->ydkc', cond_slice, d_mod_every, preferred_element_ty...]
    unnamed x2 -> x0, blocking collectives: 38 us -> none
    all_gather x4 -> x0, waiting for transfers between devices: 31.3 us -> none  [the longest x2 22.2 us: body(): lax.all_gather(down_weight[layer], 'dp', axis=1, tiled=True)]
  transfers between devices with their start and end apart: 26 -> 106, of which waited for: 18 -> 44; matrix products, arithmetic and copies ran while one was open for 11% -> 17% of each run, Pallas kernels for 0% -> 4%
where the time goes in v1:
time: 438 us; the launch traced here: 429 us
  waiting for transfers between devices  146 us (33%)
  starting transfers between devices  137 us (31%)
  local copies, waits for them, and re-layouts  87.3 us (20%)
  Pallas kernels  30.6 us (7%)
  other arithmetic  24.2 us (6%)
    ppermute x106, waiting for transfers between devices, move(): return lax.ppermute(values, AXES, [(i, target(i)) for i in range(n_all)])  146 us
    ppermute x106, starting transfers between devices, move(): return lax.ppermute(values, AXES, [(i, target(i)) for i in range(n_all)])  137 us
    unnamed x243, local copies, waits for them, and re-layouts  35.1 us
    pallas_call x21, Pallas kernels, call(): pl.pallas_call(kernel, out_shape=out_shape, in_specs=[pl.BlockSpec(memory...  30.6 us
    dynamic_update_slice x21, local copies, waits for them, and re-layouts, chip_gather(): out = lax.dynamic_update_index_in_dim(out, got, chip ^ j, 0)  18.6 us
  transfers between devices with their start and end apart: 106, of which 44 were waited for; matrix products, arithmetic and copies ran while one was open for 17% of the time, Pallas kernels for 4%

profile of v1, /device:TPU:0, one launch (start us, length us, event | category | flops | bytes accessed | tf_op | source)
XLA Modules:
  0.0 429.4 jit_solution(4359382393297973723)
XLA Ops:
  5.2 3.8 collective-permute-start.26
  11.2 3.2 collective-permute-start.2
  21.8 3.0 collective-permute-start.7
  32.4 3.2 collective-permute-done.9
  39.5 9.6 %collective-permute-start.16 = (bf16[112,768]{0,1:T(8,128)(2,1)S(1)}, bf16[112,768]{0,1:T(8,128)(2,1)S(1)}, u32[]{:S(2)}, u32[]{:S(2)}) collective-permute-start(bf16[112,768]{0,1:T(8,128)(2,1)S(1)} %fusion.36), channel_id=1, source_target_pairs={{0,6},{1,7},{2,4},{3,5},{4,0},{5,1},{6,2},{7,3},{8,14},{9,15},{10,... | collective-permute-start | bytes 516104 | tf_op jit(solution)/shard_map/ppermute | solution.py:262
  49.1 3.7 collective-permute-start.45
  65.0 3.0 collective-permute-done.17
  68.0 8.7 %collective-permute-start.12 = (bf16[64,768]{1,0:T(8,128)(2,1)S(1)}, bf16[64,768]{1,0:T(8,128)(2,1)S(1)}, u32[]{:S(2)}, u32[]{:S(2)}) collective-permute-start(bf16[64,768]{1,0:T(8,128)(2,1)S(1)} %enter.1.x0), channel_id=1, source_target_pairs={{0,1},{1,0},{2,3},{3,2},{4,5},{5,4},{6,7},{7,6},{8,9},{9,8},{10,11... | collective-permute-start | bytes 294920 | tf_op jit(solution)/shard_map/ppermute | solution.py:262
  77.5 10.9 %collective-permute-start.13 = (bf16[64,768]{1,0:T(8,128)(2,1)S(1)}, bf16[64,768]{1,0:T(8,128)(2,1)S(1)}, u32[]{:S(2)}, u32[]{:S(2)}) collective-permute-start(bf16[64,768]{1,0:T(8,128)(2,1)S(1)} %enter.1.x0), channel_id=1, source_target_pairs={{0,4},{1,5},{2,6},{3,7},{4,0},{5,1},{6,2},{7,3},{8,12},{9,13},{10,... | collective-permute-start | bytes 294920 | tf_op jit(solution)/shard_map/ppermute | solution.py:262
  89.2 4.9 %copy.166 = bf16[4,2,112,768]{3,1,0,2:T(2,128)(2,1)} copy(bf16[4,2,112,768]{2,3,1,0:T(8,128)(2,1)} %bitcast_dynamic-update-slice_fusion.6) | data formatting | bytes 2752512 | tf_op jit(solution)/shard_map/jit(dynamic_update_index_in_dim)/dynamic_update_slice | solution.py:289
  95.7 4.2 reshape.679
  121.3 16.5 %collective-permute-done.29 = bf16[2,96,1536]{2,1,0:T(8,128)(2,1)S(1)} collective-permute-done((bf16[2,96,1536]{2,1,0:T(8,128)(2,1)}, bf16[2,96,1536]{2,1,0:T(8,128)(2,1)S(1)}, u32[]{:S(2)}, u32[]{:S(2)}) %collective-permute-start.29) | collective-permute-done | bytes 589856 | tf_op jit(solution)/shard_map/ppermute | solution.py:262
  152.2 7.6 %collective-permute-done.38 = bf16[2,96,768]{1,2,0:T(8,128)(2,1)} collective-permute-done((bf16[2,96,768]{1,2,0:T(8,128)(2,1)}, bf16[2,96,768]{1,2,0:T(8,128)(2,1)}, u32[]{:S(2)}, u32[]{:S(2)}) %collective-permute-start.38) | collective-permute-done | bytes 294944 | tf_op jit(solution)/shard_map/ppermute | solution.py:262
  180.4 3.4 attention.3
  207.2 3.5 collective-permute-done.51.recv_ref
  212.9 3.0 collective-permute-done.53.x1.y1
  223.2 3.3 collective-permute-done.57.recv_ref
  245.5 5.3 %attention_back.2 = (bf16[256,576]{1,0:T(8,128)(2,1)S(1)}, f32[128,768]{1,0:T(8,128)S(1)}, bf16[128,768]{1,0:T(8,128)(2,1)}) custom-call(bf16[64,768]{1,0:T(8,128)(2,1)} %get-tuple-element.98.x0.y0, bf16[64,768]{1,0:T(8,128)(2,1)S(1)} %collective-permute-done.58.x1.y1, bf16[64,768]{1,0:T(8,128)(2,1)} %collective-permute-done.59.x2.y2, ...), custom_call_target="tpu_custom_call" | custom-call | flops 704643072 | bytes 2752512 | tf_op jit(solution)/shard_map/attention_back/pallas_call | solution.py:25
  250.7 2.8 collective-permute-start.61
  265.0 4.6 %collective-permute-done.62.recv_ref = bf16[64,768]{1,0:T(8,128)(2,1)S(1)} collective-permute-done((bf16[64,768]{1,0:T(8,128)(2,1)S(1)}, bf16[64,768]{1,0:T(8,128)(2,1)S(1)}, u32[]{:S(2)}, u32[]{:S(2)}) %collective-permute-start.62) | collective-permute-done | bytes 98336 | tf_op jit(solution)/shard_map/ppermute | solution.py:262
  270.7 4.6 %collective-permute-done.63.x1.y1 = bf16[64,768]{1,0:T(8,128)(2,1)} collective-permute-done((bf16[64,768]{1,0:T(8,128)(2,1)S(1)}, bf16[64,768]{1,0:T(8,128)(2,1)}, u32[]{:S(2)}, u32[]{:S(2)}) %collective-permute-start.63) | collective-permute-done | bytes 98336 | tf_op jit(solution)/shard_map/ppermute | solution.py:262
  283.9 2.8 collective-permute-done.67.recv_ref
  288.8 2.9 collective-permute-done.68.x1.y1
  309.9 28.2 %collective-permute-done.97 = bf16[2,96,1536]{2,1,0:T(8,128)(2,1)} collective-permute-done((bf16[2,96,1536]{2,1,0:T(8,128)(2,1)}, bf16[2,96,1536]{2,1,0:T(8,128)(2,1)}, u32[]{:S(2)}, u32[]{:S(2)}) %collective-permute-start.97) | collective-permute-done | bytes 589856 | tf_op jit(solution)/shard_map/ppermute | solution.py:262
  339.9 3.1 fusion.2
  348.5 3.7 collective-permute-start.99
  352.8 10.5 %collective-permute-done.87 = bf16[2,112,768]{2,1,0:T(8,128)(2,1)S(1)} collective-permute-done((bf16[2,112,768]{2,1,0:T(8,128)(2,1)S(1)}, bf16[2,112,768]{2,1,0:T(8,128)(2,1)S(1)}, u32[]{:S(2)}, u32[]{:S(2)}) %collective-permute-start.87) | collective-permute-done | bytes 344096 | tf_op jit(solution)/shard_map/ppermute | solution.py:262
  365.8 2.7 collective-permute-done.76
  397.5 2.7 collective-permute-start.95
  403.0 2.8 collective-permute-start.90
  407.0 11.0 %collective-permute-done.95 = bf16[112,768]{0,1:T(8,128)(2,1)S(1)} collective-permute-done((bf16[112,768]{0,1:T(8,128)(2,1)}, bf16[112,768]{0,1:T(8,128)(2,1)S(1)}, u32[]{:S(2)}, u32[]{:S(2)}) %collective-permute-start.95) | collective-permute-done | bytes 172064 | tf_op jit(solution)/shard_map/ppermute | solution.py:262
  418.0 4.2 collective-permute-done.90
  (655 shorter events, 238.8 us)
Async XLA Ops:
  3.6 58.9 %collective-permute-start.25 = (bf16[96,1536]{1,0:T(8,128)(2,1)}, bf16[96,1536]{1,0:T(8,128)(2,1)S(1)}, u32[]{:S(2)}, u32[]{:S(2)}) collective-permute-start(bf16[96,1536]{1,0:T(8,128)(2,1)} %pad_maximum_fusion.1), channel_id=1, source_target_pairs={{0,0},{1,1},{2,2},{3,3},{4,6},{5,7},{6,4},{7,5},{8,8},{9,9},{10,10... | collective-permute-start | bytes 884744 | tf_op jit(solution)/shard_map/ppermute | solution.py:262
  5.2 58.9 %collective-permute-start.26 = (bf16[96,1536]{1,0:T(8,128)(2,1)}, bf16[96,1536]{1,0:T(8,128)(2,1)S(1)}, u32[]{:S(2)}, u32[]{:S(2)}) collective-permute-start(bf16[96,1536]{1,0:T(8,128)(2,1)} %pad_maximum_fusion.1), channel_id=1, source_target_pairs={{0,6},{1,7},{2,4},{3,5},{4,0},{5,1},{6,2},{7,3},{8,14},{9,15},{10,... | collective-permute-start | bytes 884744 | tf_op jit(solution)/shard_map/ppermute | solution.py:262
  49.1 96.7 %collective-permute-start.45 = (bf16[96,1536]{1,0:T(8,128)(2,1)}, bf16[96,1536]{1,0:T(8,128)(2,1)}, u32[]{:S(2)}, u32[]{:S(2)}) collective-permute-start(bf16[96,1536]{1,0:T(8,128)(2,1)} %pad_maximum_fusion.2), channel_id=1, source_target_pairs={{0,0},{1,1},{2,2},{3,3},{4,6},{5,7},{6,4},{7,5},{8,8},{9,9},{10,10... | collective-permute-start | bytes 884744 | tf_op jit(solution)/shard_map/ppermute | solution.py:262
  55.9 90.0 %collective-permute-start.46 = (bf16[96,1536]{1,0:T(8,128)(2,1)}, bf16[96,1536]{1,0:T(8,128)(2,1)}, u32[]{:S(2)}, u32[]{:S(2)}) collective-permute-start(bf16[96,1536]{1,0:T(8,128)(2,1)} %pad_maximum_fusion.2), channel_id=1, source_target_pairs={{0,6},{1,7},{2,4},{3,5},{4,0},{5,1},{6,2},{7,3},{8,14},{9,15},{10,... | collective-permute-start | bytes 884744 | tf_op jit(solution)/shard_map/ppermute | solution.py:262
  64.0 30.3 %collective-permute-start.19 = (bf16[2,112,768]{1,2,0:T(8,128)(2,1)S(1)}, bf16[2,112,768]{1,2,0:T(8,128)(2,1)S(1)}, u32[]{:S(2)}, u32[]{:S(2)}) collective-permute-start(bf16[2,112,768]{1,2,0:T(8,128)(2,1)S(1)} %maximum_select_fusion.5), channel_id=1, source_target_pairs={{0,24},{1,25},{2,26},{3,27},{4,28},{5,29},{6,30},{7,31},{8,16},{9,... | collective-permute-start | bytes 1032200 | tf_op jit(solution)/shard_map/ppermute | solution.py:262
  68.0 26.1 %collective-permute-start.12 = (bf16[64,768]{1,0:T(8,128)(2,1)S(1)}, bf16[64,768]{1,0:T(8,128)(2,1)S(1)}, u32[]{:S(2)}, u32[]{:S(2)}) collective-permute-start(bf16[64,768]{1,0:T(8,128)(2,1)S(1)} %enter.1.x0), channel_id=1, source_target_pairs={{0,1},{1,0},{2,3},{3,2},{4,5},{5,4},{6,7},{7,6},{8,9},{9,8},{10,11... | collective-permute-start | bytes 294920 | tf_op jit(solution)/shard_map/ppermute | solution.py:262
  77.5 24.9 %collective-permute-start.13 = (bf16[64,768]{1,0:T(8,128)(2,1)S(1)}, bf16[64,768]{1,0:T(8,128)(2,1)S(1)}, u32[]{:S(2)}, u32[]{:S(2)}) collective-permute-start(bf16[64,768]{1,0:T(8,128)(2,1)S(1)} %enter.1.x0), channel_id=1, source_target_pairs={{0,4},{1,5},{2,6},{3,7},{4,0},{5,1},{6,2},{7,3},{8,12},{9,13},{10,... | collective-permute-start | bytes 294920 | tf_op jit(solution)/shard_map/ppermute | solution.py:262
  94.1 22.7 %collective-permute-start.27 = (bf16[2,96,1536]{2,1,0:T(8,128)(2,1)}, bf16[2,96,1536]{2,1,0:T(8,128)(2,1)}, u32[]{:S(2)}, u32[]{:S(2)}) collective-permute-start(bf16[2,96,1536]{2,1,0:T(8,128)(2,1)} %maximum_select_fusion.1), channel_id=1, source_target_pairs={{0,8},{1,9},{2,10},{3,11},{4,12},{5,13},{6,14},{7,15},{8,0},{9,1},... | collective-permute-start | bytes 1769480 | tf_op jit(solution)/shard_map/ppermute | solution.py:262
  114.5 34.3 %collective-permute-start.37 = (bf16[2,96,768]{1,2,0:T(8,128)(2,1)}, bf16[2,96,768]{1,2,0:T(8,128)(2,1)}, u32[]{:S(2)}, u32[]{:S(2)}) collective-permute-start(bf16[2,96,768]{1,2,0:T(8,128)(2,1)} %maximum_select_fusion.7), channel_id=1, source_target_pairs={{0,8},{1,9},{2,10},{3,11},{4,12},{5,13},{6,14},{7,15},{8,0},{9,1},... | collective-permute-start | bytes 884744 | tf_op jit(solution)/shard_map/ppermute | solution.py:262
  116.9 21.0 %collective-permute-start.29 = (bf16[2,96,1536]{2,1,0:T(8,128)(2,1)}, bf16[2,96,1536]{2,1,0:T(8,128)(2,1)S(1)}, u32[]{:S(2)}, u32[]{:S(2)}) collective-permute-start(bf16[2,96,1536]{2,1,0:T(8,128)(2,1)} %maximum_select_fusion.1), channel_id=1, source_target_pairs={{0,24},{1,25},{2,26},{3,27},{4,28},{5,29},{6,30},{7,31},{8,16},{9,... | collective-permute-start | bytes 1769480 | tf_op jit(solution)/shard_map/ppermute | solution.py:262
  119.0 18.8 %collective-permute-start.22 = (bf16[64,768]{1,0:T(8,128)(2,1)S(1)}, bf16[64,768]{1,0:T(8,128)(2,1)S(1)}, u32[]{:S(2)}, u32[]{:S(2)}) collective-permute-start(bf16[64,768]{1,0:T(8,128)(2,1)S(1)} %get-tuple-element.80.x0), channel_id=1, source_target_pairs={{0,1},{1,0},{2,3},{3,2},{4,5},{5,4},{6,7},{7,6},{8,9},{9,8},{10,11... | collective-permute-start | bytes 294920 | tf_op jit(solution)/shard_map/ppermute | solution.py:262
  139.1 20.7 %collective-permute-start.38 = (bf16[2,96,768]{1,2,0:T(8,128)(2,1)}, bf16[2,96,768]{1,2,0:T(8,128)(2,1)}, u32[]{:S(2)}, u32[]{:S(2)}) collective-permute-start(bf16[2,96,768]{1,2,0:T(8,128)(2,1)} %maximum_select_fusion.7), channel_id=1, source_target_pairs={{0,16},{1,17},{2,18},{3,19},{4,20},{5,21},{6,22},{7,23},{8,24},{9,... | collective-permute-start | bytes 884744 | tf_op jit(solution)/shard_map/ppermute | solution.py:262
  140.7 23.2 %collective-permute-start.39 = (bf16[2,96,768]{1,2,0:T(8,128)(2,1)}, bf16[2,96,768]{1,2,0:T(8,128)(2,1)}, u32[]{:S(2)}, u32[]{:S(2)}) collective-permute-start(bf16[2,96,768]{1,2,0:T(8,128)(2,1)} %maximum_select_fusion.7), channel_id=1, source_target_pairs={{0,24},{1,25},{2,26},{3,27},{4,28},{5,29},{6,30},{7,31},{8,16},{9,... | collective-permute-start | bytes 884744 | tf_op jit(solution)/shard_map/ppermute | solution.py:262
  145.9 19.9 %collective-permute-start.30 = (bf16[128,768]{1,0:T(8,128)(2,1)}, bf16[128,768]{1,0:T(8,128)(2,1)}, u32[]{:S(2)}, u32[]{:S(2)}) collective-permute-start(bf16[128,768]{1,0:T(8,128)(2,1)} %get-tuple-element.82), channel_id=1, source_target_pairs={{0,4},{1,5},{2,6},{3,7},{4,0},{5,1},{6,2},{7,3},{8,12},{9,13},{10,... | collective-permute-start | bytes 589832 | tf_op jit(solution)/shard_map/ppermute | solution.py:262
  148.0 42.7 %collective-permute-start.47 = (bf16[2,96,1536]{2,1,0:T(8,128)(2,1)}, bf16[2,96,1536]{2,1,0:T(8,128)(2,1)}, u32[]{:S(2)}, u32[]{:S(2)}) collective-permute-start(bf16[2,96,1536]{2,1,0:T(8,128)(2,1)} %maximum_select_fusion.3), channel_id=1, source_target_pairs={{0,8},{1,9},{2,10},{3,11},{4,12},{5,13},{6,14},{7,15},{8,0},{9,1},... | collective-permute-start | bytes 1769480 | tf_op jit(solution)/shard_map/ppermute | solution.py:262
  148.8 47.3 %collective-permute-start.48 = (bf16[2,96,1536]{2,1,0:T(8,128)(2,1)}, bf16[2,96,1536]{2,1,0:T(8,128)(2,1)}, u32[]{:S(2)}, u32[]{:S(2)}) collective-permute-start(bf16[2,96,1536]{2,1,0:T(8,128)(2,1)} %maximum_select_fusion.3), channel_id=1, source_target_pairs={{0,16},{1,17},{2,18},{3,19},{4,20},{5,21},{6,22},{7,23},{8,24},{9,... | collective-permute-start | bytes 1769480 | tf_op jit(solution)/shard_map/ppermute | solution.py:262
  159.8 39.3 %collective-permute-start.49 = (bf16[2,96,1536]{2,1,0:T(8,128)(2,1)}, bf16[2,96,1536]{2,1,0:T(8,128)(2,1)}, u32[]{:S(2)}, u32[]{:S(2)}) collective-permute-start(bf16[2,96,1536]{2,1,0:T(8,128)(2,1)} %maximum_select_fusion.3), channel_id=1, source_target_pairs={{0,24},{1,25},{2,26},{3,27},{4,28},{5,29},{6,30},{7,31},{8,16},{9,... | collective-permute-start | bytes 1769480 | tf_op jit(solution)/shard_map/ppermute | solution.py:262
  254.8 46.8 %collective-permute-start.101 = (bf16[2,96,1536]{2,1,0:T(8,128)(2,1)}, bf16[2,96,1536]{2,1,0:T(8,128)(2,1)}, u32[]{:S(2)}, u32[]{:S(2)}) collective-permute-start(bf16[2,96,1536]{2,1,0:T(8,128)(2,1)} %get-tuple-element.195), channel_id=1, source_target_pairs={{0,8},{1,9},{2,10},{3,11},{4,12},{5,13},{6,14},{7,15},{8,0},{9,1},... | collective-permute-start | bytes 1769480 | tf_op jit(solution)/shard_map/ppermute | solution.py:262
  255.4 49.7 %collective-permute-start.102 = (bf16[2,96,1536]{2,1,0:T(8,128)(2,1)}, bf16[2,96,1536]{2,1,0:T(8,128)(2,1)}, u32[]{:S(2)}, u32[]{:S(2)}) collective-permute-start(bf16[2,96,1536]{2,1,0:T(8,128)(2,1)} %get-tuple-element.197), channel_id=1, source_target_pairs={{0,16},{1,17},{2,18},{3,19},{4,20},{5,21},{6,22},{7,23},{8,24},{9,... | collective-permute-start | bytes 1769480 | tf_op jit(solution)/shard_map/ppermute | solution.py:262
  255.7 50.8 %collective-permute-start.103 = (bf16[2,96,1536]{2,1,0:T(8,128)(2,1)}, bf16[2,96,1536]{2,1,0:T(8,128)(2,1)}, u32[]{:S(2)}, u32[]{:S(2)}) collective-permute-start(bf16[2,96,1536]{2,1,0:T(8,128)(2,1)} %get-tuple-element.196), channel_id=1, source_target_pairs={{0,24},{1,25},{2,26},{3,27},{4,28},{5,29},{6,30},{7,31},{8,16},{9,... | collective-permute-start | bytes 1769480 | tf_op jit(solution)/shard_map/ppermute | solution.py:262
  301.6 36.6 %collective-permute-start.97 = (bf16[2,96,1536]{2,1,0:T(8,128)(2,1)}, bf16[2,96,1536]{2,1,0:T(8,128)(2,1)}, u32[]{:S(2)}, u32[]{:S(2)}) collective-permute-start(bf16[2,96,1536]{2,1,0:T(8,128)(2,1)} %get-tuple-element.200), channel_id=1, source_target_pairs={{0,16},{1,17},{2,18},{3,19},{4,20},{5,21},{6,22},{7,23},{8,24},{9,... | collective-permute-start | bytes 1769480 | tf_op jit(solution)/shard_map/ppermute | solution.py:262
  302.7 36.9 %collective-permute-start.98 = (bf16[2,96,1536]{2,1,0:T(8,128)(2,1)}, bf16[2,96,1536]{2,1,0:T(8,128)(2,1)}, u32[]{:S(2)}, u32[]{:S(2)}) collective-permute-start(bf16[2,96,1536]{2,1,0:T(8,128)(2,1)} %get-tuple-element.199), channel_id=1, source_target_pairs={{0,24},{1,25},{2,26},{3,27},{4,28},{5,29},{6,30},{7,31},{8,16},{9,... | collective-permute-start | bytes 1769480 | tf_op jit(solution)/shard_map/ppermute | solution.py:262
  305.9 39.6 %collective-permute-start.91 = (bf16[2,112,768]{2,1,0:T(8,128)(2,1)S(1)}, bf16[2,112,768]{2,1,0:T(8,128)(2,1)S(1)}, u32[]{:S(2)}, u32[]{:S(2)}) collective-permute-start(bf16[2,112,768]{2,1,0:T(8,128)(2,1)S(1)} %copy-done.95), channel_id=1, source_target_pairs={{0,8},{1,9},{2,10},{3,11},{4,12},{5,13},{6,14},{7,15},{8,0},{9,1},... | collective-permute-start | bytes 1032200 | tf_op jit(solution)/shard_map/ppermute | solution.py:262
  306.5 41.9 %collective-permute-start.92 = (bf16[2,112,768]{2,1,0:T(8,128)(2,1)S(1)}, bf16[2,112,768]{2,1,0:T(8,128)(2,1)S(1)}, u32[]{:S(2)}, u32[]{:S(2)}) collective-permute-start(bf16[2,112,768]{2,1,0:T(8,128)(2,1)S(1)} %copy-done.94), channel_id=1, source_target_pairs={{0,16},{1,17},{2,18},{3,19},{4,20},{5,21},{6,22},{7,23},{8,24},{9,... | collective-permute-start | bytes 1032200 | tf_op jit(solution)/shard_map/ppermute | solution.py:262
  309.6 38.9 %collective-permute-start.93 = (bf16[2,112,768]{2,1,0:T(8,128)(2,1)S(1)}, bf16[2,112,768]{2,1,0:T(8,128)(2,1)S(1)}, u32[]{:S(2)}, u32[]{:S(2)}) collective-permute-start(bf16[2,112,768]{2,1,0:T(8,128)(2,1)S(1)} %copy-done.93), channel_id=1, source_target_pairs={{0,24},{1,25},{2,26},{3,27},{4,28},{5,29},{6,30},{7,31},{8,16},{9,... | collective-permute-start | bytes 1032200 | tf_op jit(solution)/shard_map/ppermute | solution.py:262
  345.5 17.8 %collective-permute-start.87 = (bf16[2,112,768]{2,1,0:T(8,128)(2,1)S(1)}, bf16[2,112,768]{2,1,0:T(8,128)(2,1)S(1)}, u32[]{:S(2)}, u32[]{:S(2)}) collective-permute-start(bf16[2,112,768]{2,1,0:T(8,128)(2,1)S(1)} %get-tuple-element.205), channel_id=1, source_target_pairs={{0,16},{1,17},{2,18},{3,19},{4,20},{5,21},{6,22},{7,23},{8,24},{9,... | collective-permute-start | bytes 1032200 | tf_op jit(solution)/shard_map/ppermute | solution.py:262
  348.4 47.6 %collective-permute-start.100 = (bf16[96,1536]{1,0:T(8,128)(2,1)}, bf16[96,1536]{1,0:T(8,128)(2,1)}, u32[]{:S(2)}, u32[]{:S(2)}) collective-permute-start(bf16[96,1536]{1,0:T(8,128)(2,1)} %get-tuple-element.212), channel_id=1, source_target_pairs={{0,4},{1,5},{2,6},{3,7},{4,2},{5,3},{6,0},{7,1},{8,12},{9,13},{10,... | collective-permute-start | bytes 884744 | tf_op jit(solution)/shard_map/ppermute | solution.py:262
  348.5 49.1 %collective-permute-start.99 = (bf16[96,1536]{1,0:T(8,128)(2,1)}, bf16[96,1536]{1,0:T(8,128)(2,1)}, u32[]{:S(2)}, u32[]{:S(2)}) collective-permute-start(bf16[96,1536]{1,0:T(8,128)(2,1)} %get-tuple-element.211), channel_id=1, source_target_pairs={{0,0},{1,1},{2,2},{3,3},{4,6},{5,7},{6,4},{7,5},{8,8},{9,9},{10,10... | collective-permute-start | bytes 884744 | tf_op jit(solution)/shard_map/ppermute | solution.py:262
  381.4 20.0 %collective-permute-start.104 = (bf16[96,1536]{1,0:T(8,128)(2,1)S(1)}, bf16[96,1536]{1,0:T(8,128)(2,1)S(1)}, u32[]{:S(2)}, u32[]{:S(2)}) collective-permute-start(bf16[96,1536]{1,0:T(8,128)(2,1)S(1)} %copy-done.98), channel_id=1, source_target_pairs={{0,0},{1,1},{2,2},{3,3},{4,6},{5,7},{6,4},{7,5},{8,8},{9,9},{10,10... | collective-permute-start | bytes 884744 | tf_op jit(solution)/shard_map/ppermute | solution.py:262
  382.1 20.9 %collective-permute-start.105 = (bf16[96,1536]{1,0:T(8,128)(2,1)S(1)}, bf16[96,1536]{1,0:T(8,128)(2,1)S(1)}, u32[]{:S(2)}, u32[]{:S(2)}) collective-permute-start(bf16[96,1536]{1,0:T(8,128)(2,1)S(1)} %copy-done.97), channel_id=1, source_target_pairs={{0,4},{1,5},{2,6},{3,7},{4,2},{5,3},{6,0},{7,1},{8,12},{9,13},{10,... | collective-permute-start | bytes 884744 | tf_op jit(solution)/shard_map/ppermute | solution.py:262
  397.5 20.4 %collective-permute-start.95 = (bf16[112,768]{0,1:T(8,128)(2,1)}, bf16[112,768]{0,1:T(8,128)(2,1)S(1)}, u32[]{:S(2)}, u32[]{:S(2)}) collective-permute-start(bf16[112,768]{0,1:T(8,128)(2,1)} %bitcast.308), channel_id=1, source_target_pairs={{0,4},{1,5},{2,6},{3,7},{4,2},{5,3},{6,0},{7,1},{8,12},{9,13},{10,... | collective-permute-start | bytes 516104 | tf_op jit(solution)/shard_map/ppermute | solution.py:262
  403.0 19.1 %collective-permute-start.90 = (bf16[112,768]{0,1:T(8,128)(2,1)S(1)}, bf16[112,768]{0,1:T(8,128)(2,1)S(1)}, u32[]{:S(2)}, u32[]{:S(2)}) collective-permute-start(bf16[112,768]{0,1:T(8,128)(2,1)S(1)} %bitcast.306), channel_id=1, source_target_pairs={{0,4},{1,5},{2,6},{3,7},{4,2},{5,3},{6,0},{7,1},{8,12},{9,13},{10,... | collective-permute-start | bytes 516104 | tf_op jit(solution)/shard_map/ppermute | solution.py:262
  (190 other events, 1149.8 us)

commit v2 on v1

v2 whole, which is shorter than its diff:
```python
import functools
import math

import jax
import jax.numpy as jnp
from jax import lax
from jax.experimental import pallas as pl
from jax.experimental.pallas import tpu as pltpu
from jax.sharding import PartitionSpec as P

D = 768
HD = 64
EPS = 1e-06
AXES = ("dp", "tensor")
F32 = jnp.float32
BF16 = jnp.bfloat16
VMEM_LIMIT = 16 * 1024 * 1024

PARITY = 1
HALF = 2
CORE = 4
CHIP = 8


class Stored:
    def __init__(self, source, target, sem, local):
        self.copy = pltpu.make_async_copy(source, target, sem)
        self.local = local
        self.shape = local.shape
        self.busy = False
        self.dirty = False

    def start(self):
        self.copy.start()
        self.busy = True
        self.dirty = False

    def settle(self):
        if self.busy:
            self.copy.wait()
            self.busy = False

    def __getitem__(self, index):
        self.settle()
        return self.local[index]

    def __setitem__(self, index, value):
        self.local[index] = value
        self.dirty = True
        if index is Ellipsis:
            self.start()


def call(
    kernel, out_shape, *args, flops=0, name=None, scalars=None, after=(), scratch=(), stored=(), kept=(), window=()
):
    size = sum(a.size * a.dtype.itemsize for a in args) + sum(math.prod(o.shape) * o.dtype.itemsize for o in out_shape)
    hbm = pl.BlockSpec(memory_space=pltpu.HBM)
    vmem = pl.BlockSpec(memory_space=pltpu.VMEM)
    in_specs = [hbm if i in stored else vmem for i in range(len(args))]
    out_specs = [hbm if i in kept else vmem for i in range(len(out_shape))]
    window = dict(window)
    copies = [pltpu.VMEM((args[i].shape[0], window[i][1]) if i in window else args[i].shape, args[i].dtype) for i in stored]
    copies += [pltpu.VMEM(out_shape[i].shape, out_shape[i].dtype) for i in kept]
    lead = 0
    if after:
        args = (gate(args[0], *after),) + args[1:]
    if scalars is not None:
        args = (scalars,) + args
        in_specs = [pl.BlockSpec(memory_space=pltpu.SMEM)] + in_specs
        lead = 1

    def run(*refs):
        ins = list(refs[: len(args)])
        outs = list(refs[len(args) : len(args) + len(out_shape)])
        rest = refs[len(args) + len(out_shape) :]
        own, local = rest[: len(scratch)], rest[len(scratch) :]
        held = []
        for n, i in enumerate(stored):
            source = ins[lead + i].at[:, pl.ds(*window[i])] if i in window else ins[lead + i]
            held.append(Stored(source, local[n], local[-1].at[n], local[n]))
            held[-1].start()
            ins[lead + i] = held[-1]
        for n, i in enumerate(kept, len(stored)):
            held.append(Stored(local[n], outs[i], local[-1].at[n], local[n]))
            outs[i] = held[-1]
        kernel(*ins, *outs, *own)
        for item in held:
            if item.dirty:
                item.start()
        for item in held:
            item.settle()

    return pl.pallas_call(
        run,
        out_shape=out_shape,
        in_specs=in_specs,
        out_specs=out_specs,
        scratch_shapes=list(scratch) + copies + ([pltpu.SemaphoreType.DMA((len(copies),))] if copies else []),
        compiler_params=pltpu.CompilerParams(vmem_limit_bytes=VMEM_LIMIT),
        cost_estimate=pl.CostEstimate(flops=flops, bytes_accessed=size, transcendentals=0),
        name=name,
    )(*args)


def gate(value, *others):
    return lax.optimization_barrier((value,) + others)[0]


def place_parts(kernel, out_shape, *args, scalars, name, copies):
    count = len(args)

    def run(place_ref, *refs):
        outs = refs[count : count + len(out_shape)]
        sems = refs[-1]
        moves = [
            pltpu.make_async_copy(source, target, sems.at[n])
            for n, (source, target) in enumerate(kernel(place_ref, refs[:count], outs))
        ]
        for item in moves:
            item.start()
        for item in moves:
            item.wait()

    size = sum(a.size * a.dtype.itemsize for a in args)
    return pl.pallas_call(
        run,
        out_shape=out_shape,
        in_specs=[pl.BlockSpec(memory_space=pltpu.SMEM)]
        + [pl.BlockSpec(memory_space=pltpu.HBM)] * count,
        out_specs=[pl.BlockSpec(memory_space=pltpu.HBM)] * len(out_shape),
        scratch_shapes=[pltpu.SemaphoreType.DMA((copies,))],
        compiler_params=pltpu.CompilerParams(vmem_limit_bytes=VMEM_LIMIT),
        cost_estimate=pl.CostEstimate(flops=0, bytes_accessed=2 * size, transcendentals=0),
        name=name,
    )(scalars, *args)


def sds(shape, dtype):
    return jax.ShapeDtypeStruct(shape, dtype)


def dot(a, b, ca=1, cb=0):
    return lax.dot_general(a, b, (((ca,), (cb,)), ((), ())), preferred_element_type=F32)


def normalize(values):
    centered = values - jnp.mean(values, axis=-1, keepdims=True)
    inverse = lax.rsqrt(jnp.mean(centered * centered, axis=-1, keepdims=True) + EPS)
    return centered * inverse, inverse


def norm_back(incoming, normed, inverse):
    average = jnp.mean(incoming, axis=-1, keepdims=True)
    along = jnp.mean(incoming * normed, axis=-1, keepdims=True)
    return inverse * (incoming - average - normed * along)


def col_sum(values):
    return jnp.sum(values, axis=0, keepdims=True)


def modulate(values, mod, shift, scale):
    normed, _ = normalize(values)
    return (normed * (1.0 + mod[scale : scale + 1]) + mod[shift : shift + 1]).astype(BF16)


def rows_of(refs):
    return jnp.concatenate([ref[...] for ref in refs], axis=0)


def split_out(total, keep_ref, near_ref, send_ref):
    quarter = total.shape[0] // 4
    keep_ref[...] = total[:quarter]
    near_ref[...] = total[quarter : 2 * quarter]
    send_ref[...] = total[2 * quarter :].astype(BF16)


def summed(keep_ref, core_ref, far_ref):
    return keep_ref[...] + core_ref[: keep_ref.shape[0]].astype(F32) + far_ref[...].astype(F32)


def attention_pack(qkv_ref, out_ref):
    out = out_ref[...].astype(F32).T.astype(BF16)
    return jnp.concatenate([qkv_ref[0], qkv_ref[1], qkv_ref[2], out], axis=1)


def pack_block_kernel(qkv_ref, out_ref, up_ref, down_ref, pack_ref):
    wide = 4 * out_ref.shape[0]
    units = up_ref.shape[1]
    pack_ref[:, :wide] = attention_pack(qkv_ref, out_ref)
    pack_ref[:, wide : wide + units] = up_ref[...]
    pack_ref[:, wide + units :] = down_ref[...]


def pack_first_kernel(qkv_ref, out_ref, bias_ref, pack_ref):
    shard = out_ref.shape[1]
    pack_ref[:shard] = attention_pack(qkv_ref, out_ref)
    pack_ref[shard:] = bias_ref[...]


def pack_mlp_kernel(up_ref, down_ref, pack_ref):
    units = up_ref.shape[1]
    pack_ref[:, :units] = up_ref[...]
    pack_ref[:, units:] = down_ref[...]


def join_moves(place_ref, ins, outs):
    shard = outs[0].shape[2]
    moves = []
    for j, part in enumerate(ins):
        at = place_ref[0] ^ j
        moves.append((part.at[:, :shard], outs[0].at[at]))
        if len(outs) == 2:
            moves.append((part.at[:, shard:], outs[1].at[at]))
    return moves


def assemble_kernel(place_ref, *refs):
    parts, out_ref = refs[:-1], refs[-1]
    cols = parts[0].shape[2]
    for layer in range(out_ref.shape[0]):
        for at in range(4):
            quarter = sum(
                jnp.where(place_ref[3] ^ mask == at, part[layer], 0.0) for mask, part in enumerate(parts)
            )
            out_ref[layer, :, at * cols : (at + 1) * cols] = quarter


def spread_kernel(place_ref, *refs):
    parts, out_ref = refs[:-1], refs[-1]
    for j, part in enumerate(parts):
        out_ref[place_ref[0] ^ j] = part[...]


def couple_kernel(place_ref, own_ref, other_ref, *out_refs):
    first = place_ref[1] == 0
    at = 0
    for out_ref in out_refs:
        end = at + out_ref.shape[-1]
        own, other = own_ref[..., at:end], other_ref[..., at:end]
        out_ref[0] = jnp.where(first, own, other)
        out_ref[1] = jnp.where(first, other, own)
        at = end


def head_select(n_dp, piece, cols):
    row = lax.broadcasted_iota(jnp.int32, (3 * piece, cols), 0)
    col = lax.broadcasted_iota(jnp.int32, (3 * piece, cols), 1)
    return (row == col // HD * piece + col % piece).astype(F32)


def head_mask(n_dp, piece, cols):
    row = lax.broadcasted_iota(jnp.int32, (n_dp, cols), 0)
    col = lax.broadcasted_iota(jnp.int32, (n_dp, cols), 1)
    return (col % HD // piece == row).astype(F32)


def exact(a, b):
    return lax.dot_general(
        a, b, (((1,), (0,)), ((), ())), preferred_element_type=F32, precision=lax.Precision.HIGHEST
    )


def heads_back(line, at, n_dp, length):
    cols, piece = line.shape[1], HD // n_dp
    row = lax.broadcasted_iota(jnp.int32, (length, cols), 0) - at
    col = lax.broadcasted_iota(jnp.int32, (length, cols), 1)
    select = (row == col // HD * piece + col % piece).astype(F32)
    return lax.dot_general(
        head_mask(n_dp, piece, cols) * line,
        select,
        (((1,), (1,)), ((), ())),
        preferred_element_type=F32,
        precision=lax.Precision.HIGHEST,
    )


def units_back(line, at, n_dp, length):
    units = line.shape[1]
    width = units // n_dp
    row = lax.broadcasted_iota(jnp.int32, (length, units), 0) - at
    col = lax.broadcasted_iota(jnp.int32, (length, units), 1)
    mask = (
        lax.broadcasted_iota(jnp.int32, (n_dp, units), 1) // width
        == lax.broadcasted_iota(jnp.int32, (n_dp, units), 0)
    )
    return lax.dot_general(
        mask.astype(F32) * line,
        (col % width == row).astype(F32),
        (((1,), (1,)), ((), ())),
        preferred_element_type=F32,
        precision=lax.Precision.HIGHEST,
    )


def own_quarter(line, cols, place_ref):
    return sum(
        jnp.where(place_ref[2] == i, line[:, i * cols : (i + 1) * cols], 0.0) for i in range(line.shape[1] // cols)
    )


def bias_kernel(place_ref, vec_ref, qkv_ref, wide_ref, up_ref):
    n_dp, piece = vec_ref.shape[0] // 16, HD * 16 // vec_ref.shape[0]
    vec_row = lax.broadcasted_iota(jnp.int32, (n_dp, vec_ref.shape[0]), 0)
    vec_col = lax.broadcasted_iota(jnp.int32, (n_dp, vec_ref.shape[0]), 1)
    cols, units = qkv_ref.shape[2] // 3, up_ref.shape[2]
    select, mask = head_select(n_dp, piece, cols), head_mask(n_dp, piece, cols)
    width = units // n_dp
    row = lax.broadcasted_iota(jnp.int32, (width, units), 0)
    col = lax.broadcasted_iota(jnp.int32, (width, units), 1)
    up_select = (col % width == row).astype(F32)
    up_row = lax.broadcasted_iota(jnp.int32, (n_dp, units), 0)
    up_col = lax.broadcasted_iota(jnp.int32, (n_dp, units), 1)
    up_mask = (up_col // width == up_row).astype(F32)
    quarters = wide_ref.shape[2] // cols
    place = lax.broadcasted_iota(jnp.int32, (1, quarters * cols), 1) // cols == place_ref[2]
    for layer in range(qkv_ref.shape[0]):
        vec = dot((vec_col == 16 * vec_row + layer).astype(BF16), vec_ref[...])
        heads = [col_sum(exact(vec[:, 3 * t * piece : 3 * (t + 1) * piece], select) * mask) for t in range(4)]
        qkv_ref[layer] = jnp.concatenate([heads[0], jnp.zeros_like(heads[0]), heads[1]], axis=1)
        for t in range(2):
            wide_ref[layer, t : t + 1] = jnp.where(place, jnp.concatenate([heads[2 + t]] * quarters, axis=1), 0.0)
        up_ref[layer] = col_sum(exact(vec[:, 12 * piece : 12 * piece + width], up_select) * up_mask)


def sum_parts_kernel(count, shard, place_ref, *refs):
    parts, (same_ref, other_ref) = refs[:-2], refs[-2:]
    first = place_ref[1] == 0
    at = 0
    for start in range(0, len(parts), count):
        low = sum(part[...].astype(F32) for part in parts[start : start + count])
        end = at + low.shape[1]
        mine, far = low[:shard], low[shard : 2 * shard]
        same_ref[:shard, at:end] = jnp.where(first, mine, far).astype(BF16)
        other_ref[:shard, at:end] = jnp.where(first, far, mine).astype(BF16)
        if low.shape[0] > 2 * shard:
            mine, far = low[2 * shard : 2 * shard + 1], low[2 * shard + 1 : 2 * shard + 2]
            same_ref[shard:, at:end] = jnp.broadcast_to(jnp.where(first, mine, far), (16, end - at)).astype(BF16)
            other_ref[shard:, at:end] = jnp.broadcast_to(jnp.where(first, far, mine), (16, end - at)).astype(BF16)
            same_ref[shard:, end:] = jnp.zeros((16, same_ref.shape[1] - end), BF16)
            other_ref[shard:, end:] = jnp.zeros((16, same_ref.shape[1] - end), BF16)
        at = end


def finish_kernel(*refs):
    parts, (qkv_ref, out_ref, up_ref, down_ref, vec_ref) = refs[:-5], refs[-5:]
    shard, cols, units = up_ref.shape[1], out_ref.shape[1], up_ref.shape[2]
    for layer in range(qkv_ref.shape[0]):
        total = parts[2 * layer][...].astype(F32) + parts[2 * layer + 1][...].astype(F32)
        for i in range(3):
            qkv_ref[layer, i] = total[:shard, i * cols : (i + 1) * cols]
        out_ref[layer] = total[:shard, 3 * cols : 4 * cols].T
        up_ref[layer] = total[:shard, 4 * cols : 4 * cols + units]
        down_ref[layer] = total[:shard, 4 * cols + units :]
        if layer == 0:
            vec_ref[...] = total[shard : shard + 8, : 4 * cols]


def enter_kernel(moved_ref, mod_ref, res_ref, far_res_ref, in_ref):
    residual = moved_ref[: res_ref.shape[0]].astype(F32)
    far_res_ref[...] = residual
    res_ref[...] = residual
    in_ref[...] = modulate(residual, mod_ref[...], 0, 1)


def attention_kernel(x0, x1, x2, x3, w_ref, bias_ref, bo_ref, x_ref, qkv_ref, att_ref, keep_ref, near_ref, send_ref):
    x = rows_of((x0, x1, x2, x3))
    x_ref[...] = x
    cols = w_ref.shape[1] // 4
    qkv = (dot(x, w_ref[:, : 3 * cols]) + bias_ref[...]).astype(BF16)
    qkv_ref[...] = qkv
    parts = []
    for head in range(cols // HD):
        at = head * HD
        q = qkv[:, at : at + HD]
        k = qkv[:, cols + at : cols + at + HD]
        v = qkv[:, 2 * cols + at : 2 * cols + at + HD]
        scores = dot(q, k, 1, 1) * (1.0 / math.sqrt(HD))
        expo = jnp.exp(scores - jnp.max(scores, axis=-1, keepdims=True))
        probs = expo / jnp.sum(expo, axis=-1, keepdims=True)
        parts.append(dot(probs.astype(BF16), v))
    att = jnp.concatenate(parts, axis=1).astype(BF16)
    att_ref[...] = att
    split_out(dot(att, w_ref[:, 3 * cols :], 1, 1) + bo_ref[...], keep_ref, near_ref, send_ref)


def middle_kernel(res_ref, mod_ref, keep_ref, core_ref, far_ref, branch_ref, far_mid_ref, mid_ref, in_ref):
    mod = mod_ref[...]
    branch = summed(keep_ref, core_ref, far_ref)
    branch_ref[...] = branch
    middle = res_ref[...] + mod[2:3] * branch
    far_mid_ref[...] = middle
    mid_ref[...] = middle
    in_ref[...] = modulate(middle, mod, 3, 4)


def mlp_kernel(x0, x1, x2, x3, w_ref, bu_ref, bd_ref, x_ref, hid_ref, act_ref, keep_ref, near_ref, send_ref):
    x = rows_of((x0, x1, x2, x3))
    x_ref[...] = x
    units = w_ref.shape[1] // 2
    hidden = dot(x, w_ref[:, :units]) + bu_ref[...]
    hid_ref[...] = hidden
    act = (0.5 * hidden * (1.0 + lax.erf(hidden * 0.7071067811865476))).astype(BF16)
    act_ref[...] = act
    split_out(dot(act, w_ref[:, units:], 1, 1) + bd_ref[...], keep_ref, near_ref, send_ref)


def next_kernel(
    mid_ref, mod_ref, keep_ref, core_ref, far_ref, mod_next_ref, out_ref, far_res_ref, res_ref, in_ref
):
    mlp_out = summed(keep_ref, core_ref, far_ref)
    out_ref[...] = mlp_out
    residual = mid_ref[...] + mod_ref[5:6] * mlp_out
    far_res_ref[...] = residual
    res_ref[...] = residual
    in_ref[...] = modulate(residual, mod_next_ref[...], 0, 1)


def last_kernel(mid_ref, mod_ref, keep_ref, core_ref, far_ref, g_ref, out_ref, dgate_ref):
    mlp_out = summed(keep_ref, core_ref, far_ref)
    out_ref[...] = (mid_ref[...] + mod_ref[5:6] * mlp_out).astype(BF16)
    dgate_ref[...] = col_sum(g_ref[...] * mlp_out)


def turn_kernel(moved_ref, mod_ref, g_ref, dmlp_ref):
    g = moved_ref[dmlp_ref.shape[0] :].astype(F32)
    g_ref[...] = g
    dmlp_ref[...] = (g * mod_ref[5:6]).astype(BF16)


def mlp_back_kernel(x0, x1, x2, x3, w_ref, hid_ref, x_ref, dhid_ref, keep_ref, near_ref, send_ref):
    x = rows_of((x0, x1, x2, x3))
    x_ref[...] = x
    units = w_ref.shape[1] // 2
    hidden = hid_ref[...]
    d_active = dot(x, w_ref[:, units:])
    cumulative = 0.5 * (1.0 + lax.erf(hidden * 0.7071067811865476))
    density = jnp.exp(-0.5 * hidden * hidden) * 0.3989422804014327
    d_hidden = (d_active * (cumulative + hidden * density)).astype(BF16)
    dhid_ref[...] = d_hidden
    split_out(dot(d_hidden, w_ref[:, :units], 1, 1), keep_ref, near_ref, send_ref)


def give_parts(grad, place_ref, scratch_ref, part_refs):
    if len(part_refs) == 1:
        part_refs[0][...] = grad.astype(BF16)
        return
    scratch_ref[...] = grad.astype(BF16)
    rows = part_refs[0].shape[0]
    for j, part in enumerate(part_refs):
        start = pl.multiple_of((place_ref[0] ^ j) * rows, rows)
        part[...] = scratch_ref[pl.ds(start, rows), :]


def mlp_grad_kernel(place_ref, y_ref, x_ref, dhid_ref, act_ref, *refs):
    part_refs, (vec_ref, scratch_ref) = refs[:-2], refs[-2:]
    y = y_ref[...]
    d_hidden = dhid_ref[...]
    grad = jnp.concatenate([dot(x_ref[...], d_hidden, 0, 0), dot(y, act_ref[...], 0, 0)], axis=1)
    give_parts(grad, place_ref, scratch_ref, part_refs)
    n_dp, length = vec_ref.shape
    piece = HD // n_dp
    cols = y.shape[1] // 4
    down = own_quarter(col_sum(y.astype(F32)), cols, place_ref)
    up = col_sum(d_hidden.astype(F32))
    vec_ref[...] = heads_back(down, 9 * piece, n_dp, length) + units_back(up, 12 * piece, n_dp, length)


def middle_back_kernel(g_ref, mod_ref, keep_ref, core_ref, far_ref, mid_ref, branch_ref, dmid_ref, dbranch_ref, sums_ref):
    mod = mod_ref[...]
    incoming = summed(keep_ref, core_ref, far_ref)
    normed, inverse = normalize(mid_ref[...])
    d_middle = g_ref[...] + norm_back(incoming * (1.0 + mod[4:5]), normed, inverse)
    dmid_ref[...] = d_middle
    dbranch_ref[...] = (d_middle * mod[2:3]).astype(BF16)
    sums_ref[...] = jnp.concatenate(
        [col_sum(d_middle * branch_ref[...]), col_sum(incoming), col_sum(incoming * normed)], axis=0
    )


def attention_back_kernel(x0, x1, x2, x3, w_ref, qkv_ref, x_ref, dqkv_ref, keep_ref, near_ref, send_ref):
    x = rows_of((x0, x1, x2, x3))
    x_ref[...] = x
    cols = w_ref.shape[1] // 4
    qkv = qkv_ref[...]
    scaling = 1.0 / math.sqrt(HD)
    d_att = dot(x, w_ref[:, 3 * cols :]).astype(BF16)
    grads = ([], [], [])
    for head in range(cols // HD):
        at = head * HD
        q = qkv[:, at : at + HD]
        k = qkv[:, cols + at : cols + at + HD]
        v = qkv[:, 2 * cols + at : 2 * cols + at + HD]
        d_out = d_att[:, at : at + HD]
        scores = dot(q, k, 1, 1) * scaling
        expo = jnp.exp(scores - jnp.max(scores, axis=-1, keepdims=True))
        probs = expo / jnp.sum(expo, axis=-1, keepdims=True)
        d_probs = dot(d_out, v, 1, 1)
        d_scores = (probs * (d_probs - jnp.sum(probs * d_probs, axis=-1, keepdims=True))).astype(BF16)
        grads[0].append(dot(d_scores, k) * scaling)
        grads[1].append(dot(d_scores, q, 0, 0) * scaling)
        grads[2].append(dot(probs.astype(BF16), d_out, 0, 0))
    d_qkv = jnp.concatenate(grads[0] + grads[1] + grads[2], axis=1).astype(BF16)
    dqkv_ref[...] = d_qkv
    split_out(dot(d_qkv, w_ref[:, : 3 * cols], 1, 1), keep_ref, near_ref, send_ref)


def attention_grad_kernel(n_parts, place_ref, y_ref, x_ref, dqkv_ref, att_ref, vecs_ref, *refs):
    part_refs, (vec_ref, scratch_ref) = refs[:-2], refs[-2:]
    y = y_ref[...]
    d_qkv = dqkv_ref[...]
    cols = d_qkv.shape[1] // 3
    wide = 4 * cols
    grad = jnp.concatenate([dot(x_ref[...], d_qkv, 0, 0), dot(y, att_ref[...], 0, 0)], axis=1)
    scratch_ref[...] = grad.astype(BF16)
    n_dp, length = vec_ref.shape
    piece = HD // n_dp
    total = col_sum(d_qkv.astype(F32))
    out = own_quarter(col_sum(y.astype(F32)), cols, place_ref)
    vec = vecs_ref[...] + (
        heads_back(total[:, :cols], 0, n_dp, length)
        + heads_back(total[:, 2 * cols :], 3 * piece, n_dp, length)
        + heads_back(out, 6 * piece, n_dp, length)
    )
    vec_ref[...] = vec
    if n_parts == 1:
        part_refs[0][...] = scratch_ref[...]
        return
    rows = scratch_ref.shape[0] // n_parts
    for j, part in enumerate(part_refs):
        at = place_ref[0] ^ j
        part[:rows] = scratch_ref[pl.ds(pl.multiple_of(at * rows, rows), rows), :]


def attention_grad_last_kernel(n_parts, place_ref, y_ref, x_ref, dqkv_ref, att_ref, vecs_ref, high_ref, *refs):
    part_refs, (vec_ref, scratch_ref) = refs[:-2], refs[-2:]
    rows = scratch_ref.shape[0] // n_parts
    attention_grad_kernel(
        n_parts, place_ref, y_ref, x_ref, dqkv_ref, att_ref, vecs_ref, *part_refs, vec_ref, scratch_ref
    )
    low = vec_ref[...]
    n_dp, length = low.shape
    width = scratch_ref.shape[1]
    row = lax.broadcasted_iota(jnp.int32, (16, n_dp), 0)
    col = lax.broadcasted_iota(jnp.int32, (16, n_dp), 1)
    lane = lax.broadcasted_iota(jnp.int32, (length, width), 0)
    place = lax.broadcasted_iota(jnp.int32, (length, width), 1)
    spread = exact(low, (place == lane).astype(F32)) + exact(high_ref[...], (place == lane + length).astype(F32))
    for j, part in enumerate(part_refs):
        part[rows:] = exact((col == 2 * (place_ref[0] ^ j) + row).astype(F32), spread).astype(BF16)


def enter_back(dmid_ref, mod_ref, keep_ref, core_ref, far_ref, res_ref):
    incoming = summed(keep_ref, core_ref, far_ref)
    normed, inverse = normalize(res_ref[...])
    g = dmid_ref[...] + norm_back(incoming * (1.0 + mod_ref[1:2]), normed, inverse)
    return g, col_sum(incoming), col_sum(incoming * normed)


def enter_back_kernel(dmid_ref, mod_ref, keep_ref, core_ref, far_ref, res_ref, g_ref, sums_ref):
    g, shift, scale = enter_back(dmid_ref, mod_ref, keep_ref, core_ref, far_ref, res_ref)
    g_ref[...] = g
    sums_ref[...] = jnp.concatenate([shift, scale], axis=0)


def previous_kernel(
    dmid_ref, mod_ref, keep_ref, core_ref, far_ref, res_ref, mod_prev_ref, out_prev_ref, g_ref, sums_ref, dmlp_ref, dgate_ref
):
    g, shift, scale = enter_back(dmid_ref, mod_ref, keep_ref, core_ref, far_ref, res_ref)
    g_ref[...] = g
    sums_ref[...] = jnp.concatenate([shift, scale], axis=0)
    dmlp_ref[...] = (g * mod_prev_ref[5:6]).astype(BF16)
    dgate_ref[...] = col_sum(g * out_prev_ref[...])


def body(
    tokens,
    condition,
    cotangent,
    mod_weight,
    mod_bias,
    qkv_weight,
    qv_bias,
    out_weight,
    out_bias,
    up_weight,
    up_bias,
    down_weight,
    down_bias,
):
    layers = mod_weight.shape[0]
    n_dp = lax.axis_size("dp")
    n_chips = n_dp // 2
    n_all = n_dp * 4
    dp = lax.axis_index("dp")
    z = lax.axis_index("tensor")
    chip = dp // 2
    core = dp % 2
    half = z // 2
    quarter = 2 * (half ^ core) + z % 2
    cols = mod_weight.shape[3]
    rows = tokens.shape[1]
    shard = qkv_weight.shape[1]
    units = up_weight.shape[2]
    piece = qv_bias.shape[3]

    place = jnp.stack([chip, core, quarter, z]).astype(jnp.int32)

    def move(values, target):
        return lax.ppermute(values, AXES, [(i, target(i)) for i in range(n_all)])

    def xor(values, mask):
        return move(values, lambda i: i ^ mask)

    def swap_core_half(i):
        return i & ~6 | (i & HALF) << 1 | (i & CORE) >> 1

    def to_other(i):
        return i ^ CORE if i & CORE else i ^ CORE ^ HALF

    def from_other(i):
        return i ^ CORE ^ HALF if i & CORE else i ^ CORE

    def to_same(i):
        return i ^ HALF if i & CORE else i

    def pick(values, index):
        return lax.dynamic_index_in_dim(values, index, 0, keepdims=False)

    def chip_gather(values, after=()):
        if n_chips > 8:
            groups = [[2 * i + c for i in range(n_chips)] for c in range(2)]
            return lax.all_gather(values, "dp", axis_index_groups=groups)
        parts = [xor(values, CHIP * j) if j else values for j in range(n_chips)]
        out = sds((n_chips,) + values.shape, values.dtype)
        return call(spread_kernel, [out], *parts, scalars=place, after=after, name="spread")[0]

    def chip_swap(values):
        if n_chips > 8:
            groups = [[2 * i + c for i in range(n_chips)] for c in range(2)]
            got = lax.all_to_all(values, "dp", 0, 0, axis_index_groups=groups, tiled=True)
            return [got[i] for i in range(n_chips)]
        return [xor(pick(values, chip ^ j), CHIP * j) if j else pick(values, chip) for j in range(n_chips)]

    def chip_sum(values):
        return sum(part.astype(F32) for part in chip_swap(values))

    def fetch_near(own, *widths):
        widths = widths or (own.shape[1],)
        return call(
            couple_kernel,
            [sds((2, own.shape[0], width), BF16) for width in widths],
            move(own, to_same),
            move(own, to_other),
            scalars=place,
            kept=tuple(range(len(widths))),
            name="couple",
        )

    def fetch_chips(pair):
        if n_chips > 8:
            return [chip_gather(pair)]
        return send_chips([pair] * n_chips, pair.size < D * 4 * cols // 4 + 32 * D)

    def send_chips(parts, at_once=False):
        if at_once:
            return [parts[0]] + [xor(parts[j], CHIP * j) for j in range(1, n_chips)]
        out = [parts[0]] + [xor(parts[j], CHIP * j) for j in range(1, min(3, n_chips))]
        return out + [xor(gate(parts[j], *out[1:]), CHIP * j) for j in range(3, n_chips)]

    def join(parts):
        if n_chips > 8:
            joined, extra = parts[0][:, :, :shard], parts[0][:, :, shard:]
        else:
            height, width = parts[0].shape[1:]
            out = [sds((n_chips, 2, shard, width), BF16)]
            if height > shard:
                out.append(sds((n_chips, 2, height - shard, width), BF16))
            joined, *extra = place_parts(
                join_moves, out, *parts, scalars=place, name="join", copies=len(out) * n_chips
            )
            extra = extra[0] if extra else None
        return joined.reshape(D, joined.shape[3]), extra

    def give_chips(parts, at_once=False):
        if n_chips > 8:
            return chip_swap(parts[0].reshape(n_chips, -1, parts[0].shape[1]))
        return send_chips(parts, at_once)

    def sum_given(parts, height, *after):
        out = sds((height, 4 * cols + 2 * units), BF16)
        return call(
            functools.partial(sum_parts_kernel, n_chips, shard),
            [out, out],
            *parts,
            scalars=place,
            after=after,
            stored=tuple(range(len(parts))),
            kept=(0, 1),
            name="sum_parts",
        )

    def give_near(low):
        return [move(low[0], to_same), move(low[1], from_other)]

    def all_rows(values):
        other = xor(values, PARITY)
        return (values, other, xor(values, CORE), xor(other, CORE))

    def sum_rows(keep, near, send):
        got = xor(send, CORE)
        return keep, got, xor((near + got[rows:].astype(F32)).astype(BF16), PARITY)

    cond_full = condition.astype(F32)
    cond_act = jax.nn.silu(cond_full).astype(BF16)
    (cond_pair,) = call(
        couple_kernel, [sds((2, 1, D), BF16)], cond_act, xor(cond_act, CORE), scalars=place, name="couple"
    )
    moved = move(jnp.concatenate([tokens[0], cotangent[0]]), swap_core_half)
    qkv_own = jnp.transpose(qkv_weight, (0, 2, 1, 3))
    down_own = jnp.transpose(down_weight, (0, 2, 1))

    bias_len = 12 * piece + up_bias.shape[2]
    bias_vec = jnp.concatenate(
        [
            qv_bias.reshape(layers, 6 * piece),
            out_bias.reshape(layers, 3 * piece),
            down_bias.reshape(layers, 3 * piece),
            up_bias.reshape(layers, -1),
        ],
        axis=1,
    )
    bias_block = lax.dynamic_update_slice(jnp.zeros((16, D), BF16), bias_vec, (0, 0))
    def pack_block(layer):
        return call(
            pack_block_kernel,
            [sds((shard, 4 * cols + 2 * units), BF16)],
            qkv_own[layer],
            out_weight[layer],
            up_weight[layer],
            down_own[layer],
            name="pack_block",
        )[0]

    (own_attention,) = call(
        pack_first_kernel, [sds((shard + 16, 4 * cols), BF16)], qkv_own[0], out_weight[0], bias_block, name="pack_first"
    )
    (own_mlp,) = call(pack_mlp_kernel, [sds((shard, 2 * units), BF16)], up_weight[0], down_own[0], name="pack_mlp")
    (pair_mlp,) = fetch_near(own_mlp)
    attention_weights = [None] * layers
    mlp_weights = [None] * layers
    (pair_attention,) = fetch_near(own_attention)

    cond_every = chip_gather(cond_pair, (pair_attention,)).reshape(n_dp, D)
    cond_slice = lax.dynamic_slice_in_dim(cond_every, dp * shard, shard, 1)
    bias_at = lax.dynamic_update_slice(
        jnp.zeros((layers, 6, cols // HD, HD), F32), mod_bias.astype(F32), (0, 0, 0, dp * piece)
    ).reshape(layers, 6, cols)
    partial_mod = jnp.einsum("ld,ydkc->lykc", cond_slice, mod_weight, preferred_element_type=F32) + bias_at
    mod_sum = chip_sum(partial_mod.reshape((n_chips, 2) + partial_mod.shape[1:]))
    mod_sum = gate(mod_sum, pair_mlp)
    attention_weights[0], bias_every = join(fetch_chips(gate(pair_attention, mod_sum)))
    mod_sum = mod_sum + xor(mod_sum, CORE)
    mod_own = pick(mod_sum, half)
    mod_far = pick(mod_sum, half ^ 1)
    quarters = [xor(mod_far if mask & HALF else mod_own, mask) if mask else mod_own for mask in range(4)]
    (modulation,) = call(
        assemble_kernel,
        [sds((layers, 6, D), F32)],
        *quarters,
        scalars=place,
        name="assemble",
    )

    parts_attention = [None] * layers
    parts_mlp = [None] * layers
    parts_mlp[0] = fetch_chips(gate(pair_mlp, attention_weights[0]))
    qkv_bias_all, wide_bias, up_bias_all = call(
        bias_kernel,
        [sds((layers, 1, 3 * cols), F32), sds((layers, 2, D), F32), sds((layers, 1, units), F32)],
        bias_every.reshape(n_dp * 16, D),
        scalars=place,
        name="bias",
    )
    cotan, d_mlp = call(
        turn_kernel, [sds((rows, D), F32), sds((rows, D), BF16)], moved, modulation[layers - 1], kept=(0,), name="turn"
    )
    d_mlp_rows = all_rows(d_mlp)

    full = 4 * rows
    keep_send = [sds((rows, D), F32), sds((rows, D), F32), sds((full // 2, D), BF16)]
    row_f32 = sds((rows, D), F32)
    row_bf16 = sds((rows, D), BF16)
    line = sds((1, D), F32)
    attention_flops = 2 * full * D * 4 * cols + 4 * full * full * cols
    mlp_flops = 4 * full * D * units

    def parts_of(width, extra=0):
        if n_chips > 8:
            return [sds((D, width), BF16)]
        return [sds((D // n_chips + extra, width), BF16)] * n_chips

    saved = []
    residual, far_residual, attn_in = call(
        enter_kernel,
        [row_f32, row_f32, row_bf16],
        moved,
        modulation[0],
        kept=(1,),
        after=(attention_weights[0],),
        name="enter",
    )
    for layer in range(layers):
        mod = modulation[layer]
        more = layer + 1 < layers
        attn_rows = all_rows(attn_in)
        if more:
            own_block = gate(pack_block(layer + 1), attn_rows[3])
            pair_attention, pair_mlp = fetch_near(own_block, 4 * cols, 2 * units)
            parts_attention[layer + 1] = fetch_chips(gate(pair_attention, parts_mlp[layer][-1]))
            parts_mlp[layer + 1] = fetch_chips(gate(pair_mlp, parts_attention[layer + 1][-1]))
        if layer:
            attention_weights[layer] = join(parts_attention[layer])[0]
        attn_x, qkv, att, *partial = call(
            attention_kernel,
            [sds((full, D), BF16), sds((full, 3 * cols), BF16), sds((full, cols), BF16)] + keep_send,
            *attn_rows,
            attention_weights[layer],
            qkv_bias_all[layer],
            wide_bias[layer, :1],
            flops=attention_flops,
            stored=(4,),
            kept=(0, 1, 2),
            name="attention",
        )
        partial[2] = gate(partial[2], *parts_mlp[layer][1:3])
        branch, far_middle, middle, mlp_in = call(
            middle_kernel,
            [row_f32, row_f32, row_f32, row_bf16],
            residual,
            mod,
            *sum_rows(*partial),
            kept=(0, 1),
            name="middle",
        )
        mlp_in = gate(mlp_in, parts_mlp[layer][-1])
        mlp_rows = all_rows(mlp_in)
        mlp_weights[layer] = join(parts_mlp[layer])[0]
        mlp_x, hidden, act, *partial = call(
            mlp_kernel,
            [sds((full, D), BF16), sds((full, units), F32), sds((full, units), BF16)] + keep_send,
            *mlp_rows,
            mlp_weights[layer],
            up_bias_all[layer],
            wide_bias[layer, 1:],
            flops=mlp_flops,
            stored=(4,),
            kept=(0, 1, 2),
            name="mlp",
        )
        if more:
            partial[2] = gate(partial[2], *parts_attention[layer + 1][1:3])
        arrived = sum_rows(*partial)
        saved.append((far_residual, attn_x, qkv, att, branch, far_middle, mlp_x, hidden, act))
        if more:
            arrived = (gate(arrived[0], parts_attention[layer + 1][-1]),) + arrived[1:]
            mlp_out, far_residual, residual, attn_in = call(
                next_kernel,
                [row_f32, row_f32, row_f32, row_bf16],
                middle,
                mod,
                *arrived,
                modulation[layer + 1],
                kept=(0, 1),
                name="next",
            )
            saved[-1] += (mlp_out,)
        else:
            output, d_gate_two = call(
                last_kernel, [row_bf16, line], middle, mod, *arrived, cotan, stored=(5,), name="last"
            )

    output = move(output, swap_core_half)[None]
    flow = cotan
    mod_lines = [None] * layers
    vecs = [None] * layers
    low = [None] * layers
    near_packs = [None] * layers
    given_attention = [None] * layers
    given_mlp = [None] * layers
    vec_shape = sds((n_dp, bias_len), F32)
    for layer in reversed(range(layers)):
        far_residual, attn_x, qkv, att, branch, far_middle, mlp_x, hidden, act = saved[layer][:9]
        mod = modulation[layer]
        more = layer + 1 < layers
        if more:
            d_mlp_rows = all_rows(d_mlp)
        mlp_y, d_hidden, *partial = call(
            mlp_back_kernel,
            [sds((full, D), BF16), sds((full, units), BF16)] + keep_send,
            *d_mlp_rows,
            mlp_weights[layer],
            hidden,
            flops=mlp_flops,
            stored=(4, 5),
            kept=(0, 1),
            name="mlp_back",
        )
        if more:
            partial[2] = gate(partial[2], *given_mlp[layer + 1][1:3])
        arrived = sum_rows(*partial)
        *grad_mlp, vec_mlp = call(
            mlp_grad_kernel,
            parts_of(2 * units) + [vec_shape],
            mlp_y,
            mlp_x,
            d_hidden,
            act,
            flops=mlp_flops,
            scalars=place,
            scratch=[pltpu.VMEM((D, 2 * units), BF16)],
            stored=(0, 1, 2, 3),
            kept=(0,),
            name="mlp_grad",
        )
        arrived = (gate(arrived[0], grad_mlp[0], *(given_mlp[layer + 1][3:] if more else ())),) + arrived[1:]
        if more:
            grad_mlp = [gate(part, *given_attention[layer + 1][1:]) for part in grad_mlp]
        given_mlp[layer] = give_chips(grad_mlp)
        d_middle, d_branch, sums_mid = call(
            middle_back_kernel,
            [row_f32, row_bf16, sds((3, D), F32)],
            flow,
            mod,
            *arrived,
            far_middle,
            branch,
            stored=(5, 6) if more else (0, 5, 6),
            name="middle_back",
        )
        if more:
            d_branch = gate(d_branch, *given_attention[layer + 1][1:])
            low[layer + 1] = sum_given(list(given_attention[layer + 1]) + list(given_mlp[layer + 1]), shard)
            near_packs[layer + 1] = give_near(low[layer + 1])
        d_branch_rows = all_rows(d_branch)
        attn_y, d_qkv, *partial = call(
            attention_back_kernel,
            [sds((full, D), BF16), sds((full, 3 * cols), BF16)] + keep_send,
            *d_branch_rows,
            attention_weights[layer],
            qkv,
            flops=attention_flops * 2,
            stored=(4, 5),
            kept=(0, 1),
            name="attention_back",
        )
        if more:
            partial[2] = gate(partial[2], *given_mlp[layer][1:3], near_packs[layer + 1][0])
        arrived = sum_rows(*partial)
        *grad_attention, vecs[layer] = call(
            functools.partial(
                attention_grad_kernel if layer or n_chips > 8 else attention_grad_last_kernel,
                1 if n_chips > 8 else n_chips,
            ),
            parts_of(4 * cols, 0 if layer else 16) + [vec_shape],
            attn_y,
            attn_x,
            d_qkv,
            att,
            vec_mlp,
            *(() if layer or n_chips > 8 else (vecs[1],)),
            flops=attention_flops,
            scalars=place,
            scratch=[pltpu.VMEM((D, 4 * cols), BF16)],
            stored=(0, 1, 2, 3),
            kept=(0,),
            name="attention_grad",
        )
        after = (grad_attention[0],)
        if layer == 0:
            after = after + tuple(given_mlp[0][3:]) + tuple(near_packs[upper][1] for upper in range(1, layers))
        if layer == 0:
            height = 2 * shard + 16
            if n_chips > 8:
                rows_bias = jnp.concatenate([vecs[i] for i in range(layers)], axis=1).astype(BF16)
                rows_bias = jnp.pad(
                    rows_bias.reshape(n_chips, 2, -1), ((0, 0), (0, 14), (0, 4 * cols - layers * bias_len))
                )
                rows_all = jnp.concatenate(
                    [grad_attention[0].reshape(n_chips, 2 * shard, 4 * cols), rows_bias], axis=1
                )
                grad_attention = [rows_all.reshape(n_chips * height, 4 * cols)]
        given_attention[layer] = give_chips([gate(part, *given_mlp[layer][1:]) for part in grad_attention], True)
        if layer:
            flow, sums_in, d_mlp, gate_next = call(
                previous_kernel,
                [row_f32, sds((2, D), F32), row_bf16, line],
                d_middle,
                mod,
                *arrived,
                far_residual,
                modulation[layer - 1],
                saved[layer - 1][9],
                stored=(5, 7),
                after=after,
                name="previous",
            )
        else:
            flow, sums_in = call(
                enter_back_kernel,
                [row_f32, sds((2, D), F32)],
                d_middle,
                mod,
                *arrived,
                far_residual,
                stored=(5,),
                after=after,
                name="enter_back",
            )
            gate_next = None
        mod_lines[layer] = jnp.concatenate([sums_in, sums_mid, d_gate_two], axis=0)
        d_gate_two = gate_next

    d_mod = jnp.stack(mod_lines)
    d_mod = d_mod + xor(d_mod, CORE)
    d_mod = (d_mod + xor(d_mod, PARITY)).astype(BF16).reshape(layers * 6, 4, cols)
    d_mod = jnp.transpose(d_mod, (1, 0, 2))
    mine = pick(d_mod, z)
    far = xor(pick(d_mod, z ^ HALF), HALF)
    d_mod_pair = jnp.where(half == 0, jnp.stack([mine, far]), jnp.stack([far, mine]))
    low[0] = sum_given(list(given_attention[0]) + list(given_mlp[0]), shard + 16)
    near_packs[0] = give_near(low[0])
    d_mod_every = chip_gather(d_mod_pair).reshape(n_dp, layers, 6, cols)
    grad_mod_w = jnp.einsum("ld,lykc->ydkc", cond_slice, d_mod_every, preferred_element_type=F32)
    grad_mod_b = jnp.sum(d_mod_every.astype(F32), axis=0).reshape(layers, 6, cols // HD, HD)
    grad_mod_b = lax.dynamic_slice_in_dim(grad_mod_b, dp * piece, piece, 3)
    cond_pieces = jnp.einsum("lykc,ydkc->ld", d_mod_every, mod_weight, preferred_element_type=F32)
    cond_pieces = gate(cond_pieces, *given_attention[0][1:])
    mixed = jnp.stack(chip_swap(cond_pieces.reshape(n_chips, 2, shard)))
    if n_chips <= 8:
        mixed = jnp.take(mixed, chip ^ jnp.arange(n_chips), axis=0)
    cond_pieces = jnp.transpose(mixed, (1, 0, 2))
    cond_pieces = gate(cond_pieces, *low[0])
    cond_mine = pick(cond_pieces, core)
    cond_sent = xor(pick(cond_pieces, core ^ 1), CORE)
    cond_total = jnp.where(
        core == 0, jnp.stack([cond_mine, cond_sent], axis=1), jnp.stack([cond_sent, cond_mine], axis=1)
    ).reshape(1, D)
    cond_total = cond_total + xor(cond_total, PARITY)
    cond_total = cond_total + xor(cond_total, HALF)
    sigmoid_cond = jax.nn.sigmoid(cond_full)
    grad_condition = cond_total * sigmoid_cond * (1.0 + cond_full * (1.0 - sigmoid_cond))

    grad_tokens = move(flow, swap_core_half)[None]
    grad_qkv, grad_out, grad_up, grad_down, vec = call(
        finish_kernel,
        [
            sds((layers, 3, shard, cols), F32),
            sds((layers, cols, shard), F32),
            sds((layers, shard, units), F32),
            sds((layers, shard, units), F32),
            sds((8, 4 * cols), F32),
        ],
        *[part for layer in range(layers) for part in near_packs[layer]],
        kept=(0, 1, 2, 3),
        name="finish",
    )
    vec = vec[0, : layers * bias_len].reshape(layers, bias_len)
    vec_heads = vec[:, : 12 * piece].reshape(layers, 4, 3, piece)
    return (
        output,
        grad_tokens,
        grad_condition,
        grad_mod_w,
        grad_mod_b,
        jnp.transpose(grad_qkv, (0, 2, 1, 3)),
        vec_heads[:, :2],
        grad_out,
        vec_heads[:, 2],
        grad_up,
        vec[:, 12 * piece :].reshape(layers, 1, -1),
        jnp.transpose(grad_down, (0, 2, 1)),
        vec_heads[:, 3],
    )


def solution(mesh):
    in_specs = (
        P("dp", "tensor", None),
        P("dp", None),
        P("dp", "tensor", None),
        P(None, "dp", None, "tensor"),
        P(None, None, "tensor", "dp"),
        P(None, "dp", None, "tensor"),
        P(None, None, "tensor", "dp"),
        P(None, "tensor", "dp"),
        P(None, "tensor", "dp"),
        P(None, "dp", "tensor"),
        P(None, "tensor", "dp"),
        P(None, "tensor", "dp"),
        P(None, "tensor", "dp"),
    )
    out_specs = (
        P("dp", "tensor", None),
        P("dp", "tensor", None),
        P("dp", None),
        P(None, "dp", None, "tensor"),
        P(None, None, "tensor", "dp"),
        P(None, "dp", None, "tensor"),
        P(None, None, "tensor", "dp"),
        P(None, "tensor", "dp"),
        P(None, "tensor", "dp"),
        P(None, "dp", "tensor"),
        P(None, "tensor", "dp"),
        P(None, "tensor", "dp"),
        P(None, "tensor", "dp"),
    )
    return jax.shard_map(body, mesh=mesh, in_specs=in_specs, out_specs=out_specs, check_vma=False)
```

time: 438 us -> 353 us (0.81)
  local copies, waits for them, and re-layouts: 87.3 us -> 21.6 us
  Pallas kernels: 30.6 us -> 61.9 us
  waiting for transfers between devices: 146 us -> 116 us
  other arithmetic: 24.2 us -> 4.45 us
    pallas_call x21 -> x40, Pallas kernels: 30.6 us -> 61.9 us  [the longest x36 58 us: call(): pl.pallas_call(run, out_shape=out_shape, in_specs=in_specs, out_specs=out...]
    ppermute x106 -> x100, waiting for transfers between devices: 146 us -> 116 us  [move(): return lax.ppermute(values, AXES, [(i, target(i)) for i in range(n_all)])]
    unnamed x243 -> x50, local copies, waits for them, and re-layouts: 35.1 us -> 14.4 us
    dynamic_update_slice x26 -> x0, local copies, waits for them, and re-layouts: 19.3 us -> none  [the longest x21 18.6 us: chip_gather(): out = lax.dynamic_update_index_in_dim(out, got, chip ^ j, 0)]
    broadcast_in_dim x13 -> x0, local copies, waits for them, and re-layouts: 8.62 us -> none  [the longest x4 6.06 us: chip_gather(): out = lax.dynamic_update_index_in_dim(out, got, chip ^ j, 0)]
    reshape x8 -> x1, local copies, waits for them, and re-layouts: 4.72 us -> 0.01 us  [body(): cond_every = chip_gather(cond_pair, (pair_attention,)).reshape(n_dp, D)]
    ppermute x106 -> x100, starting transfers between devices: 137 us -> 139 us  [move(): return lax.ppermute(values, AXES, [(i, target(i)) for i in range(n_all)])]
  transfers between devices with their start and end apart: 106 -> 100, of which waited for: 44 -> 40; matrix products, arithmetic and copies ran while one was open for 17% -> 3% of each run, Pallas kernels for 4% -> 16%
where the time goes in v2:
time: 353 us; the launch traced here: 347 us
  starting transfers between devices  139 us (39%)
  waiting for transfers between devices  116 us (33%)
  Pallas kernels  61.9 us (18%)
  local copies, waits for them, and re-layouts  21.6 us (6%)
  other arithmetic  4.45 us (1%)
    ppermute x100, starting transfers between devices, move(): return lax.ppermute(values, AXES, [(i, target(i)) for i in range(n_all)])  139 us
    ppermute x100, waiting for transfers between devices, move(): return lax.ppermute(values, AXES, [(i, target(i)) for i in range(n_all)])  116 us
    pallas_call x36, Pallas kernels, call(): pl.pallas_call(run, out_shape=out_shape, in_specs=in_specs, out_specs=out...  58 us
    unnamed x50, local copies, waits for them, and re-layouts  14.4 us
  transfers between devices with their start and end apart: 100, of which 40 were waited for; matrix products, arithmetic and copies ran while one was open for 3% of the time, Pallas kernels for 16%

profile of v2, /device:TPU:0, one launch (start us, length us, event | category | flops | bytes accessed | tf_op | source)
XLA Modules:
  0.0 347.1 jit_solution(1824789166290660040)
XLA Ops:
  6.5 4.8 %collective-permute-start.2 = (bf16[112,768]{1,0:T(8,128)(2,1)S(1)}, bf16[112,768]{1,0:T(8,128)(2,1)S(1)}, u32[]{:S(2)}, u32[]{:S(2)}) collective-permute-start(bf16[112,768]{1,0:T(8,128)(2,1)S(1)} %pack_first.1), channel_id=1, source_target_pairs={{0,6},{1,7},{2,4},{3,5},{4,0},{5,1},{6,2},{7,3},{8,14},{9,15},{10,... | collective-permute-start | bytes 516104 | tf_op jit(solution)/shard_map/ppermute | solution.py:611
  18.4 4.5 %collective-permute-start.11 = (bf16[96,1536]{1,0:T(8,128)(2,1)S(1)}, bf16[96,1536]{1,0:T(8,128)(2,1)S(1)}, u32[]{:S(2)}, u32[]{:S(2)}) collective-permute-start(bf16[96,1536]{1,0:T(8,128)(2,1)S(1)} %pack_mlp.1), channel_id=1, source_target_pairs={{0,6},{1,7},{2,4},{3,5},{4,0},{5,1},{6,2},{7,3},{8,14},{9,15},{10,... | collective-permute-start | bytes 884744 | tf_op jit(solution)/shard_map/ppermute | solution.py:611
  34.6 5.2 %collective-permute-done.12.refs_1_ = bf16[2,112,768]{2,1,0:T(8,128)(2,1)S(1)} collective-permute-done((bf16[2,112,768]{2,1,0:T(8,128)(2,1)S(1)}, bf16[2,112,768]{2,1,0:T(8,128)(2,1)S(1)}, u32[]{:S(2)}, u32[]{:S(2)}) %collective-permute-start.12) | collective-permute-done | bytes 344096 | tf_op jit(solution)/shard_map/ppermute | solution.py:611
  42.8 5.8 %collective-permute-start.15 = (f32[2,2,6,192]{3,2,1,0:T(8,128)S(1)}, f32[2,2,6,192]{3,2,1,0:T(8,128)S(1)}, u32[]{:S(2)}, u32[]{:S(2)}) collective-permute-start(f32[2,2,6,192]{3,2,1,0:T(8,128)S(1)} %fusion.8), channel_id=1, source_target_pairs={{0,4},{1,5},{2,6},{3,7},{4,0},{5,1},{6,2},{7,3},{8,12},{9,13},{10,... | collective-permute-start | bytes 55304 | tf_op jit(solution)/shard_map/ppermute | solution.py:611
  53.7 4.3 %collective-permute-start.17 = (f32[2,6,192]{2,1,0:T(8,128)S(1)}, f32[2,6,192]{2,1,0:T(8,128)S(1)}, u32[]{:S(2)}, u32[]{:S(2)}) collective-permute-start(f32[2,6,192]{2,1,0:T(8,128)S(1)} %get-tuple-element.368), channel_id=1, source_target_pairs={{0,2},{1,3},{2,0},{3,1},{4,6},{5,7},{6,4},{7,5},{8,10},{9,11},{10,... | collective-permute-start | bytes 27656 | tf_op jit(solution)/shard_map/ppermute | solution.py:611
  58.0 6.7 %collective-permute-start.18 = (f32[2,6,192]{2,1,0:T(8,128)S(1)}, f32[2,6,192]{2,1,0:T(8,128)S(1)}, u32[]{:S(2)}, u32[]{:S(2)}) collective-permute-start(f32[2,6,192]{2,1,0:T(8,128)S(1)} %get-tuple-element.368), channel_id=1, source_target_pairs={{0,3},{1,2},{2,1},{3,0},{4,7},{5,6},{6,5},{7,4},{8,11},{9,10},{10,... | collective-permute-start | bytes 27656 | tf_op jit(solution)/shard_map/ppermute | solution.py:611
  64.7 3.7 %collective-permute-done.16.refs_2_ = f32[2,6,192]{2,1,0:T(8,128)S(1)} collective-permute-done((f32[2,6,192]{2,1,0:T(8,128)S(1)}, f32[2,6,192]{2,1,0:T(8,128)S(1)}, u32[]{:S(2)}, u32[]{:S(2)}) %collective-permute-start.16) | collective-permute-done | bytes 9248 | tf_op jit(solution)/shard_map/ppermute | solution.py:611
  70.5 5.5 %collective-permute-start.20 = (bf16[64,768]{1,0:T(8,128)(2,1)S(1)}, bf16[64,768]{1,0:T(8,128)(2,1)S(1)}, u32[]{:S(2)}, u32[]{:S(2)}) collective-permute-start(bf16[64,768]{1,0:T(8,128)(2,1)S(1)} %get-tuple-element.170.refs_0_), channel_id=1, source_target_pairs={{0,4},{1,5},{2,6},{3,7},{4,0},{5,1},{6,2},{7,3},{8,12},{9,13},{10,... | collective-permute-start | bytes 294920 | tf_op jit(solution)/shard_map/ppermute | solution.py:611
  83.9 4.6 %collective-permute-start.31 = (bf16[96,2304]{1,0:T(8,128)(2,1)S(1)}, bf16[96,2304]{1,0:T(8,128)(2,1)S(1)}, u32[]{:S(2)}, u32[]{:S(2)}) collective-permute-start(bf16[96,2304]{1,0:T(8,128)(2,1)S(1)} %pack_block.1), channel_id=1, source_target_pairs={{0,6},{1,7},{2,4},{3,5},{4,0},{5,1},{6,2},{7,3},{8,14},{9,15},{10,... | collective-permute-start | bytes 1327112 | tf_op jit(solution)/shard_map/ppermute | solution.py:611
  90.7 9.8 %collective-permute-done.25.refs_4_ = bf16[64,768]{1,0:T(8,128)(2,1)S(1)} collective-permute-done((bf16[64,768]{1,0:T(8,128)(2,1)S(1)}, bf16[64,768]{1,0:T(8,128)(2,1)S(1)}, u32[]{:S(2)}, u32[]{:S(2)}) %collective-permute-start.25) | collective-permute-done | bytes 98336 | tf_op jit(solution)/shard_map/ppermute | solution.py:611
  106.8 4.1 %collective-permute-start.28 = (bf16[64,768]{1,0:T(8,128)(2,1)S(1)}, bf16[64,768]{1,0:T(8,128)(2,1)S(1)}, u32[]{:S(2)}, u32[]{:S(2)}) collective-permute-start(bf16[64,768]{1,0:T(8,128)(2,1)S(1)} %get-tuple-element.182.refs_0_), channel_id=1, source_target_pairs={{0,4},{1,5},{2,6},{3,7},{4,0},{5,1},{6,2},{7,3},{8,12},{9,13},{10,... | collective-permute-start | bytes 294920 | tf_op jit(solution)/shard_map/ppermute | solution.py:611
  115.6 5.3 %collective-permute-start.35 = (bf16[128,768]{1,0:T(8,128)(2,1)S(1)}, bf16[128,768]{1,0:T(8,128)(2,1)S(1)}, u32[]{:S(2)}, u32[]{:S(2)}) collective-permute-start(bf16[128,768]{1,0:T(8,128)(2,1)S(1)} %get-tuple-element.190), channel_id=1, source_target_pairs={{0,4},{1,5},{2,6},{3,7},{4,0},{5,1},{6,2},{7,3},{8,12},{9,13},{10,... | collective-permute-start | bytes 589832 | tf_op jit(solution)/shard_map/ppermute | solution.py:611
  124.5 4.3 %collective-permute-start.36 = (bf16[64,768]{1,0:T(8,128)(2,1)S(1)}, bf16[64,768]{1,0:T(8,128)(2,1)S(1)}, u32[]{:S(2)}, u32[]{:S(2)}) collective-permute-start(bf16[64,768]{1,0:T(8,128)(2,1)S(1)} %add_convert_fusion.6), channel_id=1, source_target_pairs={{0,1},{1,0},{2,3},{3,2},{4,5},{5,4},{6,7},{7,6},{8,9},{9,8},{10,11... | collective-permute-start | bytes 294920 | tf_op jit(solution)/shard_map/ppermute | solution.py:611
  144.4 4.8 %collective-permute-start.43 = (bf16[64,768]{1,0:T(8,128)(2,1)S(1)}, bf16[64,768]{1,0:T(8,128)(2,1)S(1)}, u32[]{:S(2)}, u32[]{:S(2)}) collective-permute-start(bf16[64,768]{1,0:T(8,128)(2,1)S(1)} %add_convert_fusion.5), channel_id=1, source_target_pairs={{0,1},{1,0},{2,3},{3,2},{4,5},{5,4},{6,7},{7,6},{8,9},{9,8},{10,11... | collective-permute-start | bytes 294920 | tf_op jit(solution)/shard_map/ppermute | solution.py:611
  153.8 4.3 %collective-permute-start.45 = (bf16[64,768]{1,0:T(8,128)(2,1)S(1)}, bf16[64,768]{1,0:T(8,128)(2,1)S(1)}, u32[]{:S(2)}, u32[]{:S(2)}) collective-permute-start(bf16[64,768]{1,0:T(8,128)(2,1)S(1)} %get-tuple-element.203.refs_0_), channel_id=1, source_target_pairs={{0,1},{1,0},{2,3},{3,2},{4,5},{5,4},{6,7},{7,6},{8,9},{9,8},{10,11... | collective-permute-start | bytes 294920 | tf_op jit(solution)/shard_map/ppermute | solution.py:611
  168.8 4.7 %mlp_grad.2 = (bf16[192,1536]{1,0:T(8,128)(2,1)S(1)}, bf16[192,1536]{1,0:T(8,128)(2,1)S(1)}, bf16[192,1536]{1,0:T(8,128)(2,1)S(1)}, bf16[192,1536]{1,0:T(8,128)(2,1)S(1)}, f32[8,192]{1,0:T(8,128)S(1)}) custom-call(s32[4]{0:T(128)S(1)} %pad_add_fusion.refs_0_.place_ref, bf16[256,768]{1,0:T(8,128)(2,1)S(1)} %get-tuple-element.212.refs_1_, ...), custom_call_target="tpu_custom_call" | custom-call | flops 603979776 | bytes 3938304 | tf_op jit(solution)/shard_map/mlp_grad/pallas_call | solution.py:94
  176.4 3.9 %collective-permute-done.55.refs_4_ = bf16[64,768]{1,0:T(8,128)(2,1)S(1)} collective-permute-done((bf16[64,768]{1,0:T(8,128)(2,1)S(1)}, bf16[64,768]{1,0:T(8,128)(2,1)S(1)}, u32[]{:S(2)}, u32[]{:S(2)}) %collective-permute-start.55) | collective-permute-done | bytes 98336 | tf_op jit(solution)/shard_map/ppermute | solution.py:611
  182.3 3.9 %collective-permute-done.56.refs_1_ = bf16[64,768]{1,0:T(8,128)(2,1)S(1)} collective-permute-done((bf16[64,768]{1,0:T(8,128)(2,1)S(1)}, bf16[64,768]{1,0:T(8,128)(2,1)S(1)}, u32[]{:S(2)}, u32[]{:S(2)}) %collective-permute-start.56) | collective-permute-done | bytes 98336 | tf_op jit(solution)/shard_map/ppermute | solution.py:611
  187.5 3.6 %attention_back.2 = (bf16[256,768]{1,0:T(8,128)(2,1)S(1)}, bf16[256,576]{1,0:T(8,128)(2,1)S(1)}, f32[64,768]{1,0:T(8,128)S(1)}, f32[64,768]{1,0:T(8,128)S(1)}, bf16[128,768]{1,0:T(8,128)(2,1)S(1)}) custom-call(bf16[64,768]{1,0:T(8,128)(2,1)S(1)} %get-tuple-element.223.refs_0_, bf16[64,768]{1,0:T(8,128)(2,1)S(1)} %collective-permute-done.56.refs_1_, ...), custom_call_target="tpu_custom_call" | custom-call | flops 704643072 | bytes 3145728 | tf_op jit(solution)/shard_map/attention_back/pallas_call | solution.py:94
  199.2 3.9 %collective-permute-done.61.refs_1_ = bf16[64,768]{1,0:T(8,128)(2,1)S(1)} collective-permute-done((bf16[64,768]{1,0:T(8,128)(2,1)S(1)}, bf16[64,768]{1,0:T(8,128)(2,1)S(1)}, u32[]{:S(2)}, u32[]{:S(2)}) %collective-permute-start.61) | collective-permute-done | bytes 98336 | tf_op jit(solution)/shard_map/ppermute | solution.py:611
  203.2 4.7 %collective-permute-done.66.refs_8_ = bf16[192,1536]{1,0:T(8,128)(2,1)S(1)} collective-permute-done((bf16[192,1536]{1,0:T(8,128)(2,1)S(1)}, bf16[192,1536]{1,0:T(8,128)(2,1)S(1)}, u32[]{:S(2)}, u32[]{:S(2)}) %collective-permute-start.66) | collective-permute-done | bytes 589856 | tf_op jit(solution)/shard_map/ppermute | solution.py:611
  213.3 4.7 %mlp_grad.3 = (bf16[192,1536]{1,0:T(8,128)(2,1)S(1)}, bf16[192,1536]{1,0:T(8,128)(2,1)S(1)}, bf16[192,1536]{1,0:T(8,128)(2,1)S(1)}, bf16[192,1536]{1,0:T(8,128)(2,1)S(1)}, f32[8,192]{1,0:T(8,128)S(1)}) custom-call(s32[4]{0:T(128)S(1)} %pad_add_fusion.refs_0_.place_ref, bf16[256,768]{1,0:T(8,128)(2,1)S(1)} %get-tuple-element.241.refs_1_, ...), custom_call_target="tpu_custom_call" | custom-call | flops 603979776 | bytes 3938304 | tf_op jit(solution)/shard_map/mlp_grad/pallas_call | solution.py:94
  218.0 5.8 %collective-permute-done.70.refs_3_ = bf16[192,768]{1,0:T(8,128)(2,1)S(1)} collective-permute-done((bf16[192,768]{1,0:T(8,128)(2,1)S(1)}, bf16[192,768]{1,0:T(8,128)(2,1)S(1)}, u32[]{:S(2)}, u32[]{:S(2)}) %collective-permute-start.70) | collective-permute-done | bytes 294944 | tf_op jit(solution)/shard_map/ppermute | solution.py:611
  229.7 4.2 %collective-permute-done.68.refs_4_ = bf16[64,768]{1,0:T(8,128)(2,1)S(1)} collective-permute-done((bf16[64,768]{1,0:T(8,128)(2,1)S(1)}, bf16[64,768]{1,0:T(8,128)(2,1)S(1)}, u32[]{:S(2)}, u32[]{:S(2)}) %collective-permute-start.68) | collective-permute-done | bytes 98336 | tf_op jit(solution)/shard_map/ppermute | solution.py:611
  239.0 4.1 %collective-permute-done.72.refs_1_ = bf16[64,768]{1,0:T(8,128)(2,1)S(1)} collective-permute-done((bf16[64,768]{1,0:T(8,128)(2,1)S(1)}, bf16[64,768]{1,0:T(8,128)(2,1)S(1)}, u32[]{:S(2)}, u32[]{:S(2)}) %collective-permute-start.72) | collective-permute-done | bytes 98336 | tf_op jit(solution)/shard_map/ppermute | solution.py:611
  244.8 3.4 attention_back.3
  249.6 6.1 %collective-permute-done.49.refs_4_ = bf16[64,768]{1,0:T(8,128)(2,1)S(1)} collective-permute-done((bf16[64,768]{1,0:T(8,128)(2,1)S(1)}, bf16[64,768]{1,0:T(8,128)(2,1)S(1)}, u32[]{:S(2)}, u32[]{:S(2)}) %collective-permute-start.49) | collective-permute-done | bytes 98336 | tf_op jit(solution)/shard_map/ppermute | solution.py:611
  256.6 4.6 %attention_grad.3 = (bf16[208,768]{1,0:T(8,128)(2,1)S(1)}, bf16[208,768]{1,0:T(8,128)(2,1)S(1)}, bf16[208,768]{1,0:T(8,128)(2,1)S(1)}, bf16[208,768]{1,0:T(8,128)(2,1)S(1)}, f32[8,192]{1,0:T(8,128)}) custom-call(s32[4]{0:T(128)S(1)} %pad_add_fusion.refs_0_.place_ref, bf16[256,768]{1,0:T(8,128)(2,1)S(1)} %get-tuple-element.266.refs_1_, ...), custom_call_target="tpu_custom_call" | custom-call | flops 352321536 | bytes 2476032 | tf_op jit(solution)/shard_map/attention_grad/pallas_call | solution.py:94
  267.8 3.7 %collective-permute-done.84 = f32[2,6,768]{2,1,0:T(8,128)} collective-permute-done((f32[2,6,768]{2,1,0:T(8,128)S(1)}, f32[2,6,768]{2,1,0:T(8,128)}, u32[]{:S(2)}, u32[]{:S(2)}) %collective-permute-start.84) | collective-permute-done | bytes 36896 | tf_op jit(solution)/shard_map/ppermute | solution.py:611
  279.1 9.5 %collective-permute-done.86.refs_2_ = bf16[2,12,192]{2,1,0:T(8,128)(2,1)S(1)} collective-permute-done((bf16[2,12,192]{2,1,0:T(8,128)(2,1)S(1)}, bf16[2,12,192]{2,1,0:T(8,128)(2,1)S(1)}, u32[]{:S(2)}, u32[]{:S(2)}) %collective-permute-start.86) | collective-permute-done | bytes 9248 | tf_op jit(solution)/shard_map/ppermute | solution.py:611
  323.5 5.3 %collective-permute-done.97 = f32[1,768]{1,0:T(1,128)S(1)} collective-permute-done((f32[1,768]{1,0:T(1,128)S(1)}, f32[1,768]{1,0:T(1,128)S(1)}, u32[]{:S(2)}, u32[]{:S(2)}) %collective-permute-start.97) | collective-permute-done | bytes 3104 | tf_op jit(solution)/shard_map/ppermute | solution.py:611
  329.4 10.0 %collective-permute-done.99.refs_1_ = bf16[112,2304]{1,0:T(8,128)(2,1)S(1)} collective-permute-done((bf16[112,2304]{1,0:T(8,128)(2,1)S(1)}, bf16[112,2304]{1,0:T(8,128)(2,1)S(1)}, u32[]{:S(2)}, u32[]{:S(2)}) %collective-permute-start.99) | collective-permute-done | bytes 516128 | tf_op jit(solution)/shard_map/ppermute | solution.py:611
  (331 shorter events, 181.3 us)
Async XLA Ops:
  6.5 11.9 %collective-permute-start.2 = (bf16[112,768]{1,0:T(8,128)(2,1)S(1)}, bf16[112,768]{1,0:T(8,128)(2,1)S(1)}, u32[]{:S(2)}, u32[]{:S(2)}) collective-permute-start(bf16[112,768]{1,0:T(8,128)(2,1)S(1)} %pack_first.1), channel_id=1, source_target_pairs={{0,6},{1,7},{2,4},{3,5},{4,0},{5,1},{6,2},{7,3},{8,14},{9,15},{10,... | collective-permute-start | bytes 516104 | tf_op jit(solution)/shard_map/ppermute | solution.py:611
  17.7 14.0 %collective-permute-start.10 = (bf16[96,1536]{1,0:T(8,128)(2,1)S(1)}, bf16[96,1536]{1,0:T(8,128)(2,1)S(1)}, u32[]{:S(2)}, u32[]{:S(2)}) collective-permute-start(bf16[96,1536]{1,0:T(8,128)(2,1)S(1)} %pack_mlp.1), channel_id=1, source_target_pairs={{0,0},{1,1},{2,2},{3,3},{4,6},{5,7},{6,4},{7,5},{8,8},{9,9},{10,10... | collective-permute-start | bytes 884744 | tf_op jit(solution)/shard_map/ppermute | solution.py:611
  18.4 13.3 %collective-permute-start.11 = (bf16[96,1536]{1,0:T(8,128)(2,1)S(1)}, bf16[96,1536]{1,0:T(8,128)(2,1)S(1)}, u32[]{:S(2)}, u32[]{:S(2)}) collective-permute-start(bf16[96,1536]{1,0:T(8,128)(2,1)S(1)} %pack_mlp.1), channel_id=1, source_target_pairs={{0,6},{1,7},{2,4},{3,5},{4,0},{5,1},{6,2},{7,3},{8,14},{9,15},{10,... | collective-permute-start | bytes 884744 | tf_op jit(solution)/shard_map/ppermute | solution.py:611
  50.4 28.7 %collective-permute-start.22 = (bf16[2,96,1536]{2,1,0:T(8,128)(2,1)S(1)}, bf16[2,96,1536]{2,1,0:T(8,128)(2,1)S(1)}, u32[]{:S(2)}, u32[]{:S(2)}) collective-permute-start(bf16[2,96,1536]{2,1,0:T(8,128)(2,1)S(1)} %couple.6.refs_0_), channel_id=1, source_target_pairs={{0,8},{1,9},{2,10},{3,11},{4,12},{5,13},{6,14},{7,15},{8,0},{9,1},... | collective-permute-start | bytes 1769480 | tf_op jit(solution)/shard_map/ppermute | solution.py:611
  52.2 26.9 %collective-permute-start.23 = (bf16[2,96,1536]{2,1,0:T(8,128)(2,1)S(1)}, bf16[2,96,1536]{2,1,0:T(8,128)(2,1)S(1)}, u32[]{:S(2)}, u32[]{:S(2)}) collective-permute-start(bf16[2,96,1536]{2,1,0:T(8,128)(2,1)S(1)} %couple.6.refs_0_), channel_id=1, source_target_pairs={{0,16},{1,17},{2,18},{3,19},{4,20},{5,21},{6,22},{7,23},{8,24},{9,... | collective-permute-start | bytes 1769480 | tf_op jit(solution)/shard_map/ppermute | solution.py:611
  53.7 15.4 %collective-permute-start.17 = (f32[2,6,192]{2,1,0:T(8,128)S(1)}, f32[2,6,192]{2,1,0:T(8,128)S(1)}, u32[]{:S(2)}, u32[]{:S(2)}) collective-permute-start(f32[2,6,192]{2,1,0:T(8,128)S(1)} %get-tuple-element.368), channel_id=1, source_target_pairs={{0,2},{1,3},{2,0},{3,1},{4,6},{5,7},{6,4},{7,5},{8,10},{9,11},{10,... | collective-permute-start | bytes 27656 | tf_op jit(solution)/shard_map/ppermute | solution.py:611
  79.1 22.1 %collective-permute-start.26 = (bf16[2,96,1536]{2,1,0:T(8,128)(2,1)S(1)}, bf16[2,96,1536]{2,1,0:T(8,128)(2,1)S(1)}, u32[]{:S(2)}, u32[]{:S(2)}) collective-permute-start(bf16[2,96,1536]{2,1,0:T(8,128)(2,1)S(1)} %couple.6.refs_0_), channel_id=1, source_target_pairs={{0,24},{1,25},{2,26},{3,27},{4,28},{5,29},{6,30},{7,31},{8,16},{9,... | collective-permute-start | bytes 1769480 | tf_op jit(solution)/shard_map/ppermute | solution.py:611
  83.2 20.6 %collective-permute-start.30 = (bf16[96,2304]{1,0:T(8,128)(2,1)S(1)}, bf16[96,2304]{1,0:T(8,128)(2,1)S(1)}, u32[]{:S(2)}, u32[]{:S(2)}) collective-permute-start(bf16[96,2304]{1,0:T(8,128)(2,1)S(1)} %pack_block.1), channel_id=1, source_target_pairs={{0,0},{1,1},{2,2},{3,3},{4,6},{5,7},{6,4},{7,5},{8,8},{9,9},{10,10... | collective-permute-start | bytes 1327112 | tf_op jit(solution)/shard_map/ppermute | solution.py:611
  83.9 19.9 %collective-permute-start.31 = (bf16[96,2304]{1,0:T(8,128)(2,1)S(1)}, bf16[96,2304]{1,0:T(8,128)(2,1)S(1)}, u32[]{:S(2)}, u32[]{:S(2)}) collective-permute-start(bf16[96,2304]{1,0:T(8,128)(2,1)S(1)} %pack_block.1), channel_id=1, source_target_pairs={{0,6},{1,7},{2,4},{3,5},{4,0},{5,1},{6,2},{7,3},{8,14},{9,15},{10,... | collective-permute-start | bytes 1327112 | tf_op jit(solution)/shard_map/ppermute | solution.py:611
  88.6 11.8 %collective-permute-start.25 = (bf16[64,768]{1,0:T(8,128)(2,1)S(1)}, bf16[64,768]{1,0:T(8,128)(2,1)S(1)}, u32[]{:S(2)}, u32[]{:S(2)}) collective-permute-start(bf16[64,768]{1,0:T(8,128)(2,1)S(1)} %add_convert_fusion.7), channel_id=1, source_target_pairs={{0,1},{1,0},{2,3},{3,2},{4,5},{5,4},{6,7},{7,6},{8,9},{9,8},{10,11... | collective-permute-start | bytes 294920 | tf_op jit(solution)/shard_map/ppermute | solution.py:611
  121.8 15.7 %collective-permute-start.40 = (bf16[2,96,1536]{2,1,0:T(8,128)(2,1)S(1)}, bf16[2,96,1536]{2,1,0:T(8,128)(2,1)S(1)}, u32[]{:S(2)}, u32[]{:S(2)}) collective-permute-start(bf16[2,96,1536]{2,1,0:T(8,128)(2,1)S(1)} %get-tuple-element.202.refs_0_), channel_id=1, source_target_pairs={{0,8},{1,9},{2,10},{3,11},{4,12},{5,13},{6,14},{7,15},{8,0},{9,1},... | collective-permute-start | bytes 1769480 | tf_op jit(solution)/shard_map/ppermute | solution.py:611
  123.1 15.0 %collective-permute-start.41 = (bf16[2,96,1536]{2,1,0:T(8,128)(2,1)S(1)}, bf16[2,96,1536]{2,1,0:T(8,128)(2,1)S(1)}, u32[]{:S(2)}, u32[]{:S(2)}) collective-permute-start(bf16[2,96,1536]{2,1,0:T(8,128)(2,1)S(1)} %get-tuple-element.202.refs_0_), channel_id=1, source_target_pairs={{0,16},{1,17},{2,18},{3,19},{4,20},{5,21},{6,22},{7,23},{8,24},{9,... | collective-permute-start | bytes 1769480 | tf_op jit(solution)/shard_map/ppermute | solution.py:611
  138.1 15.8 %collective-permute-start.44 = (bf16[2,96,1536]{2,1,0:T(8,128)(2,1)S(1)}, bf16[2,96,1536]{2,1,0:T(8,128)(2,1)S(1)}, u32[]{:S(2)}, u32[]{:S(2)}) collective-permute-start(bf16[2,96,1536]{2,1,0:T(8,128)(2,1)S(1)} %get-tuple-element.202.refs_0_), channel_id=1, source_target_pairs={{0,24},{1,25},{2,26},{3,27},{4,28},{5,29},{6,30},{7,31},{8,16},{9,... | collective-permute-start | bytes 1769480 | tf_op jit(solution)/shard_map/ppermute | solution.py:611
  173.5 17.9 %collective-permute-start.64 = (bf16[192,1536]{1,0:T(8,128)(2,1)S(1)}, bf16[192,1536]{1,0:T(8,128)(2,1)S(1)}, u32[]{:S(2)}, u32[]{:S(2)}) collective-permute-start(bf16[192,1536]{1,0:T(8,128)(2,1)S(1)} %get-tuple-element.247), channel_id=1, source_target_pairs={{0,8},{1,9},{2,10},{3,11},{4,12},{5,13},{6,14},{7,15},{8,0},{9,1},... | collective-permute-start | bytes 1769480 | tf_op jit(solution)/shard_map/ppermute | solution.py:611
  174.1 17.3 %collective-permute-start.65 = (bf16[192,1536]{1,0:T(8,128)(2,1)S(1)}, bf16[192,1536]{1,0:T(8,128)(2,1)S(1)}, u32[]{:S(2)}, u32[]{:S(2)}) collective-permute-start(bf16[192,1536]{1,0:T(8,128)(2,1)S(1)} %get-tuple-element.248), channel_id=1, source_target_pairs={{0,16},{1,17},{2,18},{3,19},{4,20},{5,21},{6,22},{7,23},{8,24},{9,... | collective-permute-start | bytes 1769480 | tf_op jit(solution)/shard_map/ppermute | solution.py:611
  191.4 16.5 %collective-permute-start.66 = (bf16[192,1536]{1,0:T(8,128)(2,1)S(1)}, bf16[192,1536]{1,0:T(8,128)(2,1)S(1)}, u32[]{:S(2)}, u32[]{:S(2)}) collective-permute-start(bf16[192,1536]{1,0:T(8,128)(2,1)S(1)} %get-tuple-element.249), channel_id=1, source_target_pairs={{0,24},{1,25},{2,26},{3,27},{4,28},{5,29},{6,30},{7,31},{8,16},{9,... | collective-permute-start | bytes 1769480 | tf_op jit(solution)/shard_map/ppermute | solution.py:611
  199.2 12.1 %collective-permute-start.62 = (bf16[64,768]{1,0:T(8,128)(2,1)S(1)}, bf16[64,768]{1,0:T(8,128)(2,1)S(1)}, u32[]{:S(2)}, u32[]{:S(2)}) collective-permute-start(bf16[64,768]{1,0:T(8,128)(2,1)S(1)} %get-tuple-element.238.refs_0_), channel_id=1, source_target_pairs={{0,4},{1,5},{2,6},{3,7},{4,0},{5,1},{6,2},{7,3},{8,12},{9,13},{10,... | collective-permute-start | bytes 294920 | tf_op jit(solution)/shard_map/ppermute | solution.py:611
  209.3 14.5 %collective-permute-start.70 = (bf16[192,768]{1,0:T(8,128)(2,1)S(1)}, bf16[192,768]{1,0:T(8,128)(2,1)S(1)}, u32[]{:S(2)}, u32[]{:S(2)}) collective-permute-start(bf16[192,768]{1,0:T(8,128)(2,1)S(1)} %get-tuple-element.261), channel_id=1, source_target_pairs={{0,16},{1,17},{2,18},{3,19},{4,20},{5,21},{6,22},{7,23},{8,24},{9,... | collective-permute-start | bytes 884744 | tf_op jit(solution)/shard_map/ppermute | solution.py:611
  209.8 14.0 %collective-permute-start.71 = (bf16[192,768]{1,0:T(8,128)(2,1)S(1)}, bf16[192,768]{1,0:T(8,128)(2,1)S(1)}, u32[]{:S(2)}, u32[]{:S(2)}) collective-permute-start(bf16[192,768]{1,0:T(8,128)(2,1)S(1)} %get-tuple-element.263), channel_id=1, source_target_pairs={{0,24},{1,25},{2,26},{3,27},{4,28},{5,29},{6,30},{7,31},{8,16},{9,... | collective-permute-start | bytes 884744 | tf_op jit(solution)/shard_map/ppermute | solution.py:611
  213.3 15.7 %collective-permute-start.67 = (bf16[128,768]{1,0:T(8,128)(2,1)S(1)}, bf16[128,768]{1,0:T(8,128)(2,1)S(1)}, u32[]{:S(2)}, u32[]{:S(2)}) collective-permute-start(bf16[128,768]{1,0:T(8,128)(2,1)S(1)} %get-tuple-element.252), channel_id=1, source_target_pairs={{0,4},{1,5},{2,6},{3,7},{4,0},{5,1},{6,2},{7,3},{8,12},{9,13},{10,... | collective-permute-start | bytes 589832 | tf_op jit(solution)/shard_map/ppermute | solution.py:611
  223.8 24.4 %collective-permute-start.75 = (bf16[192,1536]{1,0:T(8,128)(2,1)S(1)}, bf16[192,1536]{1,0:T(8,128)(2,1)S(1)}, u32[]{:S(2)}, u32[]{:S(2)}) collective-permute-start(bf16[192,1536]{1,0:T(8,128)(2,1)S(1)} %get-tuple-element.276), channel_id=1, source_target_pairs={{0,8},{1,9},{2,10},{3,11},{4,12},{5,13},{6,14},{7,15},{8,0},{9,1},... | collective-permute-start | bytes 1769480 | tf_op jit(solution)/shard_map/ppermute | solution.py:611
  224.4 23.8 %collective-permute-start.76 = (bf16[192,1536]{1,0:T(8,128)(2,1)S(1)}, bf16[192,1536]{1,0:T(8,128)(2,1)S(1)}, u32[]{:S(2)}, u32[]{:S(2)}) collective-permute-start(bf16[192,1536]{1,0:T(8,128)(2,1)S(1)} %get-tuple-element.278), channel_id=1, source_target_pairs={{0,16},{1,17},{2,18},{3,19},{4,20},{5,21},{6,22},{7,23},{8,24},{9,... | collective-permute-start | bytes 1769480 | tf_op jit(solution)/shard_map/ppermute | solution.py:611
  228.2 20.7 %collective-permute-start.79 = (bf16[96,2304]{1,0:T(8,128)(2,1)S(1)}, bf16[96,2304]{1,0:T(8,128)(2,1)S(1)}, u32[]{:S(2)}, u32[]{:S(2)}) collective-permute-start(bf16[96,2304]{1,0:T(8,128)(2,1)S(1)} %get-tuple-element.285), channel_id=1, source_target_pairs={{0,0},{1,1},{2,2},{3,3},{4,6},{5,7},{6,4},{7,5},{8,8},{9,9},{10,10... | collective-permute-start | bytes 1327112 | tf_op jit(solution)/shard_map/ppermute | solution.py:611
  248.2 16.4 %collective-permute-start.77 = (bf16[192,1536]{1,0:T(8,128)(2,1)S(1)}, bf16[192,1536]{1,0:T(8,128)(2,1)S(1)}, u32[]{:S(2)}, u32[]{:S(2)}) collective-permute-start(bf16[192,1536]{1,0:T(8,128)(2,1)S(1)} %get-tuple-element.279), channel_id=1, source_target_pairs={{0,24},{1,25},{2,26},{3,27},{4,28},{5,29},{6,30},{7,31},{8,16},{9,... | collective-permute-start | bytes 1769480 | tf_op jit(solution)/shard_map/ppermute | solution.py:611
  249.0 14.3 %collective-permute-start.78 = (bf16[96,2304]{1,0:T(8,128)(2,1)S(1)}, bf16[96,2304]{1,0:T(8,128)(2,1)S(1)}, u32[]{:S(2)}, u32[]{:S(2)}) collective-permute-start(bf16[96,2304]{1,0:T(8,128)(2,1)S(1)} %get-tuple-element.281), channel_id=1, source_target_pairs={{0,4},{1,5},{2,6},{3,7},{4,2},{5,3},{6,0},{7,1},{8,12},{9,13},{10,... | collective-permute-start | bytes 1327112 | tf_op jit(solution)/shard_map/ppermute | solution.py:611
  273.0 22.6 %collective-permute-start.89 = (bf16[208,768]{1,0:T(8,128)(2,1)}, bf16[208,768]{1,0:T(8,128)(2,1)}, u32[]{:S(2)}, u32[]{:S(2)}) collective-permute-start(bf16[208,768]{1,0:T(8,128)(2,1)} %copy-done.9), channel_id=1, source_target_pairs={{0,8},{1,9},{2,10},{3,11},{4,12},{5,13},{6,14},{7,15},{8,0},{9,1},... | collective-permute-start | bytes 958472 | tf_op jit(solution)/shard_map/ppermute | solution.py:611
  273.6 21.9 %collective-permute-start.90 = (bf16[208,768]{1,0:T(8,128)(2,1)}, bf16[208,768]{1,0:T(8,128)(2,1)}, u32[]{:S(2)}, u32[]{:S(2)}) collective-permute-start(bf16[208,768]{1,0:T(8,128)(2,1)} %copy-done.8), channel_id=1, source_target_pairs={{0,16},{1,17},{2,18},{3,19},{4,20},{5,21},{6,22},{7,23},{8,24},{9,... | collective-permute-start | bytes 958472 | tf_op jit(solution)/shard_map/ppermute | solution.py:611
  274.6 21.0 %collective-permute-start.91 = (bf16[208,768]{1,0:T(8,128)(2,1)}, bf16[208,768]{1,0:T(8,128)(2,1)}, u32[]{:S(2)}, u32[]{:S(2)}) collective-permute-start(bf16[208,768]{1,0:T(8,128)(2,1)} %copy-done.7), channel_id=1, source_target_pairs={{0,24},{1,25},{2,26},{3,27},{4,28},{5,29},{6,30},{7,31},{8,16},{9,... | collective-permute-start | bytes 958472 | tf_op jit(solution)/shard_map/ppermute | solution.py:611
  277.8 12.6 %collective-permute-start.87 = (bf16[2,12,192]{2,1,0:T(8,128)(2,1)S(1)}, bf16[2,12,192]{2,1,0:T(8,128)(2,1)S(1)}, u32[]{:S(2)}, u32[]{:S(2)}) collective-permute-start(bf16[2,12,192]{2,1,0:T(8,128)(2,1)S(1)} %maximum_select_fusion.refs_1_), channel_id=1, source_target_pairs={{0,16},{1,17},{2,18},{3,19},{4,20},{5,21},{6,22},{7,23},{8,24},{9,... | collective-permute-start | bytes 27656 | tf_op jit(solution)/shard_map/ppermute | solution.py:611
  299.2 24.3 %collective-permute-start.82 = (f32[64,768]{1,0:T(8,128)}, f32[64,768]{1,0:T(8,128)}, u32[]{:S(2)}, u32[]{:S(2)}) collective-permute-start(f32[64,768]{1,0:T(8,128)} %copy-done.10), channel_id=1, source_target_pairs={{0,0},{1,1},{2,4},{3,5},{4,2},{5,3},{6,6},{7,7},{8,8},{9,9},{10,12... | collective-permute-start | bytes 589832 | tf_op jit(solution)/shard_map/ppermute | solution.py:611
  311.6 17.8 %collective-permute-start.98 = (bf16[112,2304]{1,0:T(8,128)(2,1)}, bf16[112,2304]{1,0:T(8,128)(2,1)S(1)}, u32[]{:S(2)}, u32[]{:S(2)}) collective-permute-start(bf16[112,2304]{1,0:T(8,128)(2,1)} %get-tuple-element.305), channel_id=1, source_target_pairs={{0,0},{1,1},{2,2},{3,3},{4,6},{5,7},{6,4},{7,5},{8,8},{9,9},{10,10... | collective-permute-start | bytes 1548296 | tf_op jit(solution)/shard_map/ppermute | solution.py:611
  313.3 26.1 %collective-permute-start.99 = (bf16[112,2304]{1,0:T(8,128)(2,1)S(1)}, bf16[112,2304]{1,0:T(8,128)(2,1)S(1)}, u32[]{:S(2)}, u32[]{:S(2)}) collective-permute-start(bf16[112,2304]{1,0:T(8,128)(2,1)S(1)} %copy-done.6), channel_id=1, source_target_pairs={{0,4},{1,5},{2,6},{3,7},{4,2},{5,3},{6,0},{7,1},{8,12},{9,13},{10,... | collective-permute-start | bytes 1548296 | tf_op jit(solution)/shard_map/ppermute | solution.py:611
  (88 other events, 631.2 us)

commit v3 on v2

--- a/solution.py
+++ b/solution.py
@@ -180,29 +180,29 @@
     return keep_ref[...] + core_ref[: keep_ref.shape[0]].astype(F32) + far_ref[...].astype(F32)
 
 
-def attention_pack(qkv_ref, out_ref):
-    out = out_ref[...].astype(F32).T.astype(BF16)
-    return jnp.concatenate([qkv_ref[0], qkv_ref[1], qkv_ref[2], out], axis=1)
-
-
-def pack_block_kernel(qkv_ref, out_ref, up_ref, down_ref, pack_ref):
-    wide = 4 * out_ref.shape[0]
-    units = up_ref.shape[1]
-    pack_ref[:, :wide] = attention_pack(qkv_ref, out_ref)
-    pack_ref[:, wide : wide + units] = up_ref[...]
-    pack_ref[:, wide + units :] = down_ref[...]
+def attention_pack(layer, qkv_ref, out_ref):
+    out = out_ref[layer].astype(F32).T.astype(BF16)
+    return jnp.concatenate([qkv_ref[layer, 0], qkv_ref[layer, 1], qkv_ref[layer, 2], out], axis=1)
+
+
+def pack_block_kernel(layer, qkv_ref, out_ref, up_ref, down_ref, pack_ref):
+    wide = 4 * out_ref.shape[1]
+    units = up_ref.shape[2]
+    pack_ref[:, :wide] = attention_pack(layer, qkv_ref, out_ref)
+    pack_ref[:, wide : wide + units] = up_ref[layer]
+    pack_ref[:, wide + units :] = down_ref[layer]
 
 
 def pack_first_kernel(qkv_ref, out_ref, bias_ref, pack_ref):
-    shard = out_ref.shape[1]
-    pack_ref[:shard] = attention_pack(qkv_ref, out_ref)
+    shard = out_ref.shape[2]
+    pack_ref[:shard] = attention_pack(0, qkv_ref, out_ref)
     pack_ref[shard:] = bias_ref[...]
 
 
 def pack_mlp_kernel(up_ref, down_ref, pack_ref):
-    units = up_ref.shape[1]
-    pack_ref[:, :units] = up_ref[...]
-    pack_ref[:, units:] = down_ref[...]
+    units = up_ref.shape[2]
+    pack_ref[:, :units] = up_ref[0]
+    pack_ref[:, units:] = down_ref[0]
 
 
 def join_moves(place_ref, ins, outs):
@@ -338,23 +338,27 @@
             mine, far = low[2 * shard : 2 * shard + 1], low[2 * shard + 1 : 2 * shard + 2]
             same_ref[shard:, at:end] = jnp.broadcast_to(jnp.where(first, mine, far), (16, end - at)).astype(BF16)
             other_ref[shard:, at:end] = jnp.broadcast_to(jnp.where(first, far, mine), (16, end - at)).astype(BF16)
-            same_ref[shard:, end:] = jnp.zeros((16, same_ref.shape[1] - end), BF16)
-            other_ref[shard:, end:] = jnp.zeros((16, same_ref.shape[1] - end), BF16)
         at = end
 
 
-def finish_kernel(*refs):
-    parts, (qkv_ref, out_ref, up_ref, down_ref, vec_ref) = refs[:-5], refs[-5:]
+def finish_kernel(last_ref, flow_ref, *refs):
+    parts, (last_out_ref, flow_out_ref, qkv_ref, out_ref, up_ref, down_ref, vec_ref) = refs[:-7], refs[-7:]
+    last_out_ref[...] = last_ref[...]
+    flow_out_ref[...] = flow_ref[...]
     shard, cols, units = up_ref.shape[1], out_ref.shape[1], up_ref.shape[2]
     for layer in range(qkv_ref.shape[0]):
-        total = parts[2 * layer][...].astype(F32) + parts[2 * layer + 1][...].astype(F32)
+        if layer == 0:
+            total = parts[0][...].astype(F32) + parts[1][...].astype(F32)
+            vec_ref[...] = total[shard : shard + 8]
+            mlp = parts[2][...].astype(F32) + parts[3][...].astype(F32)
+        else:
+            total = parts[2 * layer + 2][...].astype(F32) + parts[2 * layer + 3][...].astype(F32)
+            mlp = total[:, 4 * cols :]
         for i in range(3):
             qkv_ref[layer, i] = total[:shard, i * cols : (i + 1) * cols]
         out_ref[layer] = total[:shard, 3 * cols : 4 * cols].T
-        up_ref[layer] = total[:shard, 4 * cols : 4 * cols + units]
-        down_ref[layer] = total[:shard, 4 * cols + units :]
-        if layer == 0:
-            vec_ref[...] = total[shard : shard + 8, : 4 * cols]
+        up_ref[layer] = mlp[:, :units]
+        down_ref[layer] = mlp[:, units:]
 
 
 def enter_kernel(moved_ref, mod_ref, res_ref, far_res_ref, in_ref):
@@ -661,7 +665,7 @@
     def fetch_chips(pair):
         if n_chips > 8:
             return [chip_gather(pair)]
-        return send_chips([pair] * n_chips, pair.size < D * 4 * cols // 4 + 32 * D)
+        return send_chips([pair] * n_chips, pair.shape[2] < 2 * units)
 
     def send_chips(parts, at_once=False):
         if at_once:
@@ -689,7 +693,8 @@
         return send_chips(parts, at_once)
 
     def sum_given(parts, height, *after):
-        out = sds((height, 4 * cols + 2 * units), BF16)
+        width = sum(part.shape[1] for part in parts) // n_chips
+        out = sds((height, width), BF16)
         return call(
             functools.partial(sum_parts_kernel, n_chips, shard),
             [out, out],
@@ -717,6 +722,10 @@
     (cond_pair,) = call(
         couple_kernel, [sds((2, 1, D), BF16)], cond_act, xor(cond_act, CORE), scalars=place, name="couple"
     )
+    cond_every = chip_gather(cond_pair).reshape(n_dp, D)
+    qv_bias, out_bias, down_bias, up_bias, up_weight, _ = lax.optimization_barrier(
+        (qv_bias, out_bias, down_bias, up_bias, up_weight, cond_every)
+    )
     moved = move(jnp.concatenate([tokens[0], cotangent[0]]), swap_core_half)
     qkv_own = jnp.transpose(qkv_weight, (0, 2, 1, 3))
     down_own = jnp.transpose(down_weight, (0, 2, 1))
@@ -734,33 +743,33 @@
     bias_block = lax.dynamic_update_slice(jnp.zeros((16, D), BF16), bias_vec, (0, 0))
     def pack_block(layer):
         return call(
-            pack_block_kernel,
+            functools.partial(pack_block_kernel, layer),
             [sds((shard, 4 * cols + 2 * units), BF16)],
-            qkv_own[layer],
-            out_weight[layer],
-            up_weight[layer],
-            down_own[layer],
+            qkv_own,
+            out_weight,
+            up_weight,
+            down_own,
             name="pack_block",
         )[0]
 
     (own_attention,) = call(
-        pack_first_kernel, [sds((shard + 16, 4 * cols), BF16)], qkv_own[0], out_weight[0], bias_block, name="pack_first"
-    )
-    (own_mlp,) = call(pack_mlp_kernel, [sds((shard, 2 * units), BF16)], up_weight[0], down_own[0], name="pack_mlp")
+        pack_first_kernel, [sds((shard + 16, 4 * cols), BF16)], qkv_own, out_weight, bias_block, name="pack_first"
+    )
+    (own_mlp,) = call(pack_mlp_kernel, [sds((shard, 2 * units), BF16)], up_weight, down_own, name="pack_mlp")
     (pair_mlp,) = fetch_near(own_mlp)
     attention_weights = [None] * layers
     mlp_weights = [None] * layers
     (pair_attention,) = fetch_near(own_attention)
 
-    cond_every = chip_gather(cond_pair, (pair_attention,)).reshape(n_dp, D)
     cond_slice = lax.dynamic_slice_in_dim(cond_every, dp * shard, shard, 1)
     bias_at = lax.dynamic_update_slice(
         jnp.zeros((layers, 6, cols // HD, HD), F32), mod_bias.astype(F32), (0, 0, 0, dp * piece)
     ).reshape(layers, 6, cols)
     partial_mod = jnp.einsum("ld,ydkc->lykc", cond_slice, mod_weight, preferred_element_type=F32) + bias_at
     mod_sum = chip_sum(partial_mod.reshape((n_chips, 2) + partial_mod.shape[1:]))
+    parts_first = fetch_chips(gate(pair_attention, partial_mod))
     mod_sum = gate(mod_sum, pair_mlp)
-    attention_weights[0], bias_every = join(fetch_chips(gate(pair_attention, mod_sum)))
+    attention_weights[0], bias_every = join(parts_first)
     mod_sum = mod_sum + xor(mod_sum, CORE)
     mod_own = pick(mod_sum, half)
     mod_far = pick(mod_sum, half ^ 1)
@@ -770,12 +779,13 @@
         [sds((layers, 6, D), F32)],
         *quarters,
         scalars=place,
+        after=(pair_mlp,) + tuple(parts_first[1:]),
         name="assemble",
     )
 
     parts_attention = [None] * layers
     parts_mlp = [None] * layers
-    parts_mlp[0] = fetch_chips(gate(pair_mlp, attention_weights[0]))
+    parts_mlp[0] = fetch_chips(gate(pair_mlp, modulation))
     qkv_bias_all, wide_bias, up_bias_all = call(
         bias_kernel,
         [sds((layers, 1, 3 * cols), F32), sds((layers, 2, D), F32), sds((layers, 1, units), F32)],
@@ -844,7 +854,6 @@
             kept=(0, 1),
             name="middle",
         )
-        mlp_in = gate(mlp_in, parts_mlp[layer][-1])
         mlp_rows = all_rows(mlp_in)
         mlp_weights[layer] = join(parts_mlp[layer])[0]
         mlp_x, hidden, act, *partial = call(
@@ -881,7 +890,7 @@
                 last_kernel, [row_bf16, line], middle, mod, *arrived, cotan, stored=(5,), name="last"
             )
 
-    output = move(output, swap_core_half)[None]
+    output = move(output, swap_core_half)
     flow = cotan
     mod_lines = [None] * layers
     vecs = [None] * layers
@@ -1029,48 +1038,56 @@
     mine = pick(d_mod, z)
     far = xor(pick(d_mod, z ^ HALF), HALF)
     d_mod_pair = jnp.where(half == 0, jnp.stack([mine, far]), jnp.stack([far, mine]))
-    low[0] = sum_given(list(given_attention[0]) + list(given_mlp[0]), shard + 16)
-    near_packs[0] = give_near(low[0])
-    d_mod_every = chip_gather(d_mod_pair).reshape(n_dp, layers, 6, cols)
-    grad_mod_w = jnp.einsum("ld,lykc->ydkc", cond_slice, d_mod_every, preferred_element_type=F32)
+    low_attention = sum_given(list(given_attention[0]), shard + 16)
+    near_attention = give_near(low_attention)
+    near_mlp = give_near(sum_given(list(given_mlp[0]), shard))
+    near_packs[0] = near_attention + near_mlp
+    d_mod_pair = gate(d_mod_pair, *given_attention[0][1:])
+    d_mod_every = gate(chip_gather(d_mod_pair), *near_mlp).reshape(n_dp, layers, 6, cols)
+    grad_mod_w = jnp.einsum("ld,lykc->ykdc", cond_slice, d_mod_every, preferred_element_type=F32)
+    grad_mod_w = jnp.transpose(grad_mod_w, (0, 2, 1, 3))
     grad_mod_b = jnp.sum(d_mod_every.astype(F32), axis=0).reshape(layers, 6, cols // HD, HD)
     grad_mod_b = lax.dynamic_slice_in_dim(grad_mod_b, dp * piece, piece, 3)
     cond_pieces = jnp.einsum("lykc,ydkc->ld", d_mod_every, mod_weight, preferred_element_type=F32)
-    cond_pieces = gate(cond_pieces, *given_attention[0][1:])
     mixed = jnp.stack(chip_swap(cond_pieces.reshape(n_chips, 2, shard)))
     if n_chips <= 8:
         mixed = jnp.take(mixed, chip ^ jnp.arange(n_chips), axis=0)
     cond_pieces = jnp.transpose(mixed, (1, 0, 2))
-    cond_pieces = gate(cond_pieces, *low[0])
+    cond_pieces = gate(cond_pieces, *low_attention)
     cond_mine = pick(cond_pieces, core)
     cond_sent = xor(pick(cond_pieces, core ^ 1), CORE)
     cond_total = jnp.where(
         core == 0, jnp.stack([cond_mine, cond_sent], axis=1), jnp.stack([cond_sent, cond_mine], axis=1)
     ).reshape(1, D)
+    cond_total = gate(cond_total, *near_attention)
     cond_total = cond_total + xor(cond_total, PARITY)
     cond_total = cond_total + xor(cond_total, HALF)
     sigmoid_cond = jax.nn.sigmoid(cond_full)
     grad_condition = cond_total * sigmoid_cond * (1.0 + cond_full * (1.0 - sigmoid_cond))
 
-    grad_tokens = move(flow, swap_core_half)[None]
-    grad_qkv, grad_out, grad_up, grad_down, vec = call(
+    grad_tokens = move(flow, swap_core_half)
+    output, grad_tokens, grad_qkv, grad_out, grad_up, grad_down, vec = call(
         finish_kernel,
         [
+            row_bf16,
+            row_f32,
             sds((layers, 3, shard, cols), F32),
             sds((layers, cols, shard), F32),
             sds((layers, shard, units), F32),
             sds((layers, shard, units), F32),
             sds((8, 4 * cols), F32),
         ],
+        output,
+        grad_tokens,
         *[part for layer in range(layers) for part in near_packs[layer]],
-        kept=(0, 1, 2, 3),
+        kept=(0, 1, 2, 3, 4, 5),
         name="finish",
     )
     vec = vec[0, : layers * bias_len].reshape(layers, bias_len)
     vec_heads = vec[:, : 12 * piece].reshape(layers, 4, 3, piece)
     return (
-        output,
-        grad_tokens,
+        output[None],
+        grad_tokens[None],
         grad_condition,
         grad_mod_w,
         grad_mod_b,

time: 353 us -> 315 us (0.89)
  waiting for transfers between devices: 116 us -> 83.9 us
  local copies, waits for them, and re-layouts: 21.6 us -> 16.3 us
    ppermute x100 -> x102, waiting for transfers between devices: 116 us -> 83.9 us  [move(): return lax.ppermute(values, AXES, [(i, target(i)) for i in range(n_all)])]
    unnamed x50 -> x55, local copies, waits for them, and re-layouts: 14.4 us -> 10.2 us
    ppermute x100 -> x102, starting transfers between devices: 139 us -> 137 us  [move(): return lax.ppermute(values, AXES, [(i, target(i)) for i in range(n_all)])]
    pallas_call x36 -> x37, Pallas kernels: 58 us -> 59.5 us  [call(): pl.pallas_call(run, out_shape=out_shape, in_specs=in_specs, out_specs=out...]
  transfers between devices with their start and end apart: 100 -> 102, of which waited for: 40 -> 39; matrix products, arithmetic and copies ran while one was open for 3% -> 4% of each run, Pallas kernels for 16% -> 19%
where the time goes in v3:
time: 315 us; the launch traced here: 310 us
  starting transfers between devices  137 us (43%)
  waiting for transfers between devices  83.9 us (27%)
  Pallas kernels  63.4 us (20%)
  local copies, waits for them, and re-layouts  16.3 us (5%)
  other arithmetic  4.52 us (1%)
    ppermute x102, starting transfers between devices, move(): return lax.ppermute(values, AXES, [(i, target(i)) for i in range(n_all)])  137 us
    ppermute x102, waiting for transfers between devices, move(): return lax.ppermute(values, AXES, [(i, target(i)) for i in range(n_all)])  83.9 us
    pallas_call x37, Pallas kernels, call(): pl.pallas_call(run, out_shape=out_shape, in_specs=in_specs, out_specs=out...  59.5 us
    unnamed x55, local copies, waits for them, and re-layouts  10.2 us
  transfers between devices with their start and end apart: 102, of which 39 were waited for; matrix products, arithmetic and copies ran while one was open for 4% of the time, Pallas kernels for 19%

profile of v3, /device:TPU:0, one launch (start us, length us, event | category | flops | bytes accessed | tf_op | source)
XLA Modules:
  0.0 309.6 jit_solution(2022966704162007228)
XLA Ops:
  3.8 2.9 collective-permute-start.2
  22.1 3.6 %collective-permute-start.14 = (bf16[96,1536]{1,0:T(8,128)(2,1)S(1)}, bf16[96,1536]{1,0:T(8,128)(2,1)S(1)}, u32[]{:S(2)}, u32[]{:S(2)}) collective-permute-start(bf16[96,1536]{1,0:T(8,128)(2,1)S(1)} %pack_mlp.1), channel_id=1, source_target_pairs={{0,6},{1,7},{2,4},{3,5},{4,0},{5,1},{6,2},{7,3},{8,14},{9,15},{10,... | collective-permute-start | bytes 884744 | tf_op jit(solution)/shard_map/ppermute | solution.py:615
  35.2 8.2 %collective-permute-start.15 = (f32[2,2,6,192]{3,2,1,0:T(8,128)S(1)}, f32[2,2,6,192]{3,2,1,0:T(8,128)S(1)}, u32[]{:S(2)}, u32[]{:S(2)}) collective-permute-start(f32[2,2,6,192]{3,2,1,0:T(8,128)S(1)} %fusion.9), channel_id=1, source_target_pairs={{0,4},{1,5},{2,6},{3,7},{4,0},{5,1},{6,2},{7,3},{8,12},{9,13},{10,... | collective-permute-start | bytes 55304 | tf_op jit(solution)/shard_map/ppermute | solution.py:615
  45.0 4.0 %collective-permute-start.18 = (f32[2,6,192]{2,1,0:T(8,128)S(1)}, f32[2,6,192]{2,1,0:T(8,128)S(1)}, u32[]{:S(2)}, u32[]{:S(2)}) collective-permute-start(f32[2,6,192]{2,1,0:T(8,128)S(1)} %get-tuple-element.376), channel_id=1, source_target_pairs={{0,3},{1,2},{2,1},{3,0},{4,7},{5,6},{6,5},{7,4},{8,11},{9,10},{10,... | collective-permute-start | bytes 27656 | tf_op jit(solution)/shard_map/ppermute | solution.py:615
  56.9 5.7 %collective-permute-start.19 = (bf16[64,768]{1,0:T(8,128)(2,1)S(1)}, bf16[64,768]{1,0:T(8,128)(2,1)S(1)}, u32[]{:S(2)}, u32[]{:S(2)}) collective-permute-start(bf16[64,768]{1,0:T(8,128)(2,1)S(1)} %get-tuple-element.182.refs_0_), channel_id=1, source_target_pairs={{0,1},{1,0},{2,3},{3,2},{4,5},{5,4},{6,7},{7,6},{8,9},{9,8},{10,11... | collective-permute-start | bytes 294920 | tf_op jit(solution)/shard_map/ppermute | solution.py:615
  72.7 3.6 %collective-permute-start.31 = (bf16[96,2304]{1,0:T(8,128)(2,1)S(1)}, bf16[96,2304]{1,0:T(8,128)(2,1)S(1)}, u32[]{:S(2)}, u32[]{:S(2)}) collective-permute-start(bf16[96,2304]{1,0:T(8,128)(2,1)S(1)} %pack_block.1), channel_id=1, source_target_pairs={{0,6},{1,7},{2,4},{3,5},{4,0},{5,1},{6,2},{7,3},{8,14},{9,15},{10,... | collective-permute-start | bytes 1327112 | tf_op jit(solution)/shard_map/ppermute | solution.py:615
  76.3 5.1 %collective-permute-start.25 = (bf16[64,768]{1,0:T(8,128)(2,1)S(1)}, bf16[64,768]{1,0:T(8,128)(2,1)S(1)}, u32[]{:S(2)}, u32[]{:S(2)}) collective-permute-start(bf16[64,768]{1,0:T(8,128)(2,1)S(1)} %add_convert_fusion.7), channel_id=1, source_target_pairs={{0,1},{1,0},{2,3},{3,2},{4,5},{5,4},{6,7},{7,6},{8,9},{9,8},{10,11... | collective-permute-start | bytes 294920 | tf_op jit(solution)/shard_map/ppermute | solution.py:615
  81.4 6.0 %collective-permute-done.25.refs_4_ = bf16[64,768]{1,0:T(8,128)(2,1)S(1)} collective-permute-done((bf16[64,768]{1,0:T(8,128)(2,1)S(1)}, bf16[64,768]{1,0:T(8,128)(2,1)S(1)}, u32[]{:S(2)}, u32[]{:S(2)}) %collective-permute-start.25) | collective-permute-done | bytes 98336 | tf_op jit(solution)/shard_map/ppermute | solution.py:615
  93.6 5.9 %collective-permute-start.27 = (bf16[64,768]{1,0:T(8,128)(2,1)S(1)}, bf16[64,768]{1,0:T(8,128)(2,1)S(1)}, u32[]{:S(2)}, u32[]{:S(2)}) collective-permute-start(bf16[64,768]{1,0:T(8,128)(2,1)S(1)} %get-tuple-element.192.refs_0_), channel_id=1, source_target_pairs={{0,4},{1,5},{2,6},{3,7},{4,0},{5,1},{6,2},{7,3},{8,12},{9,13},{10,... | collective-permute-start | bytes 294920 | tf_op jit(solution)/shard_map/ppermute | solution.py:615
  104.1 5.4 %collective-permute-start.35 = (bf16[128,768]{1,0:T(8,128)(2,1)S(1)}, bf16[128,768]{1,0:T(8,128)(2,1)S(1)}, u32[]{:S(2)}, u32[]{:S(2)}) collective-permute-start(bf16[128,768]{1,0:T(8,128)(2,1)S(1)} %get-tuple-element.201), channel_id=1, source_target_pairs={{0,4},{1,5},{2,6},{3,7},{4,0},{5,1},{6,2},{7,3},{8,12},{9,13},{10,... | collective-permute-start | bytes 589832 | tf_op jit(solution)/shard_map/ppermute | solution.py:615
  115.9 2.8 collective-permute-done.36.refs_4_
  121.4 2.8 collective-permute-done.37.refs_1_
  131.9 3.0 collective-permute-done.43.refs_4_
  138.2 3.2 %collective-permute-done.44.refs_1_ = bf16[64,768]{1,0:T(8,128)(2,1)S(1)} collective-permute-done((bf16[64,768]{1,0:T(8,128)(2,1)S(1)}, bf16[64,768]{1,0:T(8,128)(2,1)S(1)}, u32[]{:S(2)}, u32[]{:S(2)}) %collective-permute-start.44) | collective-permute-done | bytes 98336 | tf_op jit(solution)/shard_map/ppermute | solution.py:615
  149.8 4.7 %mlp_grad.2 = (bf16[192,1536]{1,0:T(8,128)(2,1)S(1)}, bf16[192,1536]{1,0:T(8,128)(2,1)S(1)}, bf16[192,1536]{1,0:T(8,128)(2,1)S(1)}, bf16[192,1536]{1,0:T(8,128)(2,1)S(1)}, f32[8,192]{1,0:T(8,128)S(1)}) custom-call(s32[4]{0:T(128)S(1)} %pad_add_fusion.refs_0_.place_ref, bf16[256,768]{1,0:T(8,128)(2,1)S(1)} %get-tuple-element.222.refs_1_, ...), custom_call_target="tpu_custom_call" | custom-call | flops 603979776 | bytes 3938304 | tf_op jit(solution)/shard_map/mlp_grad/pallas_call | solution.py:94
  158.8 2.9 collective-permute-done.55.refs_4_
  164.7 2.9 collective-permute-done.56.refs_1_
  168.9 3.6 %attention_back.2 = (bf16[256,768]{1,0:T(8,128)(2,1)S(1)}, bf16[256,576]{1,0:T(8,128)(2,1)S(1)}, f32[64,768]{1,0:T(8,128)S(1)}, f32[64,768]{1,0:T(8,128)S(1)}, bf16[128,768]{1,0:T(8,128)(2,1)S(1)}) custom-call(bf16[64,768]{1,0:T(8,128)(2,1)S(1)} %get-tuple-element.233.refs_0_, bf16[64,768]{1,0:T(8,128)(2,1)S(1)} %collective-permute-done.56.refs_1_, ...), custom_call_target="tpu_custom_call" | custom-call | flops 704643072 | bytes 3145728 | tf_op jit(solution)/shard_map/attention_back/pallas_call | solution.py:94
  175.9 3.2 %attention_grad.2 = (bf16[192,768]{1,0:T(8,128)(2,1)S(1)}, bf16[192,768]{1,0:T(8,128)(2,1)S(1)}, bf16[192,768]{1,0:T(8,128)(2,1)S(1)}, bf16[192,768]{1,0:T(8,128)(2,1)S(1)}, f32[8,192]{1,0:T(8,128)S(1)}) custom-call(s32[4]{0:T(128)S(1)} %pad_add_fusion.refs_0_.place_ref, bf16[256,768]{1,0:T(8,128)(2,1)S(1)} %get-tuple-element.235.refs_1_, ...), custom_call_target="tpu_custom_call" | custom-call | flops 352321536 | bytes 2371584 | tf_op jit(solution)/shard_map/attention_grad/pallas_call | solution.py:94
  181.6 3.1 collective-permute-done.61.refs_1_
  184.7 4.5 %collective-permute-done.66.refs_8_ = bf16[192,1536]{1,0:T(8,128)(2,1)S(1)} collective-permute-done((bf16[192,1536]{1,0:T(8,128)(2,1)S(1)}, bf16[192,1536]{1,0:T(8,128)(2,1)S(1)}, u32[]{:S(2)}, u32[]{:S(2)}) %collective-permute-start.66) | collective-permute-done | bytes 589856 | tf_op jit(solution)/shard_map/ppermute | solution.py:615
  194.7 4.7 %mlp_grad.3 = (bf16[192,1536]{1,0:T(8,128)(2,1)S(1)}, bf16[192,1536]{1,0:T(8,128)(2,1)S(1)}, bf16[192,1536]{1,0:T(8,128)(2,1)S(1)}, bf16[192,1536]{1,0:T(8,128)(2,1)S(1)}, f32[8,192]{1,0:T(8,128)S(1)}) custom-call(s32[4]{0:T(128)S(1)} %pad_add_fusion.refs_0_.place_ref, bf16[256,768]{1,0:T(8,128)(2,1)S(1)} %get-tuple-element.251.refs_1_, ...), custom_call_target="tpu_custom_call" | custom-call | flops 603979776 | bytes 3938304 | tf_op jit(solution)/shard_map/mlp_grad/pallas_call | solution.py:94
  199.4 5.4 %collective-permute-done.71.refs_4_ = bf16[192,768]{1,0:T(8,128)(2,1)S(1)} collective-permute-done((bf16[192,768]{1,0:T(8,128)(2,1)S(1)}, bf16[192,768]{1,0:T(8,128)(2,1)S(1)}, u32[]{:S(2)}, u32[]{:S(2)}) %collective-permute-start.71) | collective-permute-done | bytes 294944 | tf_op jit(solution)/shard_map/ppermute | solution.py:615
  212.4 3.3 %collective-permute-done.68.refs_4_ = bf16[64,768]{1,0:T(8,128)(2,1)S(1)} collective-permute-done((bf16[64,768]{1,0:T(8,128)(2,1)S(1)}, bf16[64,768]{1,0:T(8,128)(2,1)S(1)}, u32[]{:S(2)}, u32[]{:S(2)}) %collective-permute-start.68) | collective-permute-done | bytes 98336 | tf_op jit(solution)/shard_map/ppermute | solution.py:615
  224.8 3.4 %attention_back.3 = (bf16[256,768]{1,0:T(8,128)(2,1)S(1)}, bf16[256,576]{1,0:T(8,128)(2,1)S(1)}, f32[64,768]{1,0:T(8,128)S(1)}, f32[64,768]{1,0:T(8,128)S(1)}, bf16[128,768]{1,0:T(8,128)(2,1)S(1)}) custom-call(bf16[64,768]{1,0:T(8,128)(2,1)S(1)} %get-tuple-element.274.refs_0_, bf16[64,768]{1,0:T(8,128)(2,1)S(1)} %collective-permute-done.72.refs_1_, ...), custom_call_target="tpu_custom_call" | custom-call | flops 704643072 | bytes 3145728 | tf_op jit(solution)/shard_map/attention_back/pallas_call | solution.py:94
  228.2 2.8 collective-permute-start.77
  231.9 6.0 %collective-permute-done.49.refs_4_ = bf16[64,768]{1,0:T(8,128)(2,1)S(1)} collective-permute-done((bf16[64,768]{1,0:T(8,128)(2,1)S(1)}, bf16[64,768]{1,0:T(8,128)(2,1)S(1)}, u32[]{:S(2)}, u32[]{:S(2)}) %collective-permute-start.49) | collective-permute-done | bytes 98336 | tf_op jit(solution)/shard_map/ppermute | solution.py:615
  238.3 4.6 %attention_grad.3 = (bf16[208,768]{1,0:T(8,128)(2,1)S(1)}, bf16[208,768]{1,0:T(8,128)(2,1)S(1)}, bf16[208,768]{1,0:T(8,128)(2,1)S(1)}, bf16[208,768]{1,0:T(8,128)(2,1)S(1)}, f32[8,192]{1,0:T(8,128)}) custom-call(s32[4]{0:T(128)S(1)} %pad_add_fusion.refs_0_.place_ref, bf16[256,768]{1,0:T(8,128)(2,1)S(1)} %get-tuple-element.276.refs_1_, ...), custom_call_target="tpu_custom_call" | custom-call | flops 352321536 | bytes 2476032 | tf_op jit(solution)/shard_map/attention_grad/pallas_call | solution.py:94
  261.2 5.4 %collective-permute-done.84.refs_3_ = bf16[208,768]{1,0:T(8,128)(2,1)} collective-permute-done((bf16[208,768]{1,0:T(8,128)(2,1)}, bf16[208,768]{1,0:T(8,128)(2,1)}, u32[]{:S(2)}, u32[]{:S(2)}) %collective-permute-start.84) | collective-permute-done | bytes 319520 | tf_op jit(solution)/shard_map/ppermute | solution.py:615
  286.5 3.4 %collective-permute-start.87 = (bf16[112,768]{1,0:T(8,128)(2,1)S(1)}, bf16[112,768]{1,0:T(8,128)(2,1)S(1)}, u32[]{:S(2)}, u32[]{:S(2)}) collective-permute-start(bf16[112,768]{1,0:T(8,128)(2,1)S(1)} %copy-done.13), channel_id=1, source_target_pairs={{0,4},{1,5},{2,6},{3,7},{4,2},{5,3},{6,0},{7,1},{8,12},{9,13},{10,... | collective-permute-start | bytes 516104 | tf_op jit(solution)/shard_map/ppermute | solution.py:615
  296.7 3.7 %collective-permute-done.87.refs_3_ = bf16[112,768]{1,0:T(8,128)(2,1)S(1)} collective-permute-done((bf16[112,768]{1,0:T(8,128)(2,1)S(1)}, bf16[112,768]{1,0:T(8,128)(2,1)S(1)}, u32[]{:S(2)}, u32[]{:S(2)}) %collective-permute-start.87) | collective-permute-done | bytes 172064 | tf_op jit(solution)/shard_map/ppermute | solution.py:615
  305.2 3.3 %collective-permute-done.101 = f32[1,768]{1,0:T(1,128)S(1)} collective-permute-done((f32[1,768]{1,0:T(1,128)S(1)}, f32[1,768]{1,0:T(1,128)S(1)}, u32[]{:S(2)}, u32[]{:S(2)}) %collective-permute-start.101) | collective-permute-done | bytes 3104 | tf_op jit(solution)/shard_map/ppermute | solution.py:615
  (342 shorter events, 174.4 us)
Async XLA Ops:
  21.4 13.1 %collective-permute-start.13 = (bf16[96,1536]{1,0:T(8,128)(2,1)S(1)}, bf16[96,1536]{1,0:T(8,128)(2,1)S(1)}, u32[]{:S(2)}, u32[]{:S(2)}) collective-permute-start(bf16[96,1536]{1,0:T(8,128)(2,1)S(1)} %pack_mlp.1), channel_id=1, source_target_pairs={{0,0},{1,1},{2,2},{3,3},{4,6},{5,7},{6,4},{7,5},{8,8},{9,9},{10,10... | collective-permute-start | bytes 884744 | tf_op jit(solution)/shard_map/ppermute | solution.py:615
  22.1 12.4 %collective-permute-start.14 = (bf16[96,1536]{1,0:T(8,128)(2,1)S(1)}, bf16[96,1536]{1,0:T(8,128)(2,1)S(1)}, u32[]{:S(2)}, u32[]{:S(2)}) collective-permute-start(bf16[96,1536]{1,0:T(8,128)(2,1)S(1)} %pack_mlp.1), channel_id=1, source_target_pairs={{0,6},{1,7},{2,4},{3,5},{4,0},{5,1},{6,2},{7,3},{8,14},{9,15},{10,... | collective-permute-start | bytes 884744 | tf_op jit(solution)/shard_map/ppermute | solution.py:615
  31.0 18.0 %collective-permute-start.7 = (bf16[2,112,768]{2,1,0:T(8,128)(2,1)S(1)}, bf16[2,112,768]{2,1,0:T(8,128)(2,1)S(1)}, u32[]{:S(2)}, u32[]{:S(2)}) collective-permute-start(bf16[2,112,768]{2,1,0:T(8,128)(2,1)S(1)} %couple.5.refs_0_), channel_id=1, source_target_pairs={{0,8},{1,9},{2,10},{3,11},{4,12},{5,13},{6,14},{7,15},{8,0},{9,1},... | collective-permute-start | bytes 1032200 | tf_op jit(solution)/shard_map/ppermute | solution.py:615
  32.2 17.6 %collective-permute-start.8 = (bf16[2,112,768]{2,1,0:T(8,128)(2,1)S(1)}, bf16[2,112,768]{2,1,0:T(8,128)(2,1)S(1)}, u32[]{:S(2)}, u32[]{:S(2)}) collective-permute-start(bf16[2,112,768]{2,1,0:T(8,128)(2,1)S(1)} %couple.5.refs_0_), channel_id=1, source_target_pairs={{0,16},{1,17},{2,18},{3,19},{4,20},{5,21},{6,22},{7,23},{8,24},{9,... | collective-permute-start | bytes 1032200 | tf_op jit(solution)/shard_map/ppermute | solution.py:615
  33.6 16.9 %collective-permute-start.9 = (bf16[2,112,768]{2,1,0:T(8,128)(2,1)S(1)}, bf16[2,112,768]{2,1,0:T(8,128)(2,1)S(1)}, u32[]{:S(2)}, u32[]{:S(2)}) collective-permute-start(bf16[2,112,768]{2,1,0:T(8,128)(2,1)S(1)} %couple.5.refs_0_), channel_id=1, source_target_pairs={{0,24},{1,25},{2,26},{3,27},{4,28},{5,29},{6,30},{7,31},{8,16},{9,... | collective-permute-start | bytes 1032200 | tf_op jit(solution)/shard_map/ppermute | solution.py:615
  53.4 16.0 %collective-permute-start.22 = (bf16[2,96,1536]{2,1,0:T(8,128)(2,1)S(1)}, bf16[2,96,1536]{2,1,0:T(8,128)(2,1)S(1)}, u32[]{:S(2)}, u32[]{:S(2)}) collective-permute-start(bf16[2,96,1536]{2,1,0:T(8,128)(2,1)S(1)} %couple.6.refs_0_), channel_id=1, source_target_pairs={{0,8},{1,9},{2,10},{3,11},{4,12},{5,13},{6,14},{7,15},{8,0},{9,1},... | collective-permute-start | bytes 1769480 | tf_op jit(solution)/shard_map/ppermute | solution.py:615
  54.1 15.3 %collective-permute-start.23 = (bf16[2,96,1536]{2,1,0:T(8,128)(2,1)S(1)}, bf16[2,96,1536]{2,1,0:T(8,128)(2,1)S(1)}, u32[]{:S(2)}, u32[]{:S(2)}) collective-permute-start(bf16[2,96,1536]{2,1,0:T(8,128)(2,1)S(1)} %couple.6.refs_0_), channel_id=1, source_target_pairs={{0,16},{1,17},{2,18},{3,19},{4,20},{5,21},{6,22},{7,23},{8,24},{9,... | collective-permute-start | bytes 1769480 | tf_op jit(solution)/shard_map/ppermute | solution.py:615
  69.6 22.0 %collective-permute-start.29 = (bf16[2,96,1536]{2,1,0:T(8,128)(2,1)S(1)}, bf16[2,96,1536]{2,1,0:T(8,128)(2,1)S(1)}, u32[]{:S(2)}, u32[]{:S(2)}) collective-permute-start(bf16[2,96,1536]{2,1,0:T(8,128)(2,1)S(1)} %couple.6.refs_0_), channel_id=1, source_target_pairs={{0,24},{1,25},{2,26},{3,27},{4,28},{5,29},{6,30},{7,31},{8,16},{9,... | collective-permute-start | bytes 1769480 | tf_op jit(solution)/shard_map/ppermute | solution.py:615
  72.0 18.8 %collective-permute-start.30 = (bf16[96,2304]{1,0:T(8,128)(2,1)S(1)}, bf16[96,2304]{1,0:T(8,128)(2,1)S(1)}, u32[]{:S(2)}, u32[]{:S(2)}) collective-permute-start(bf16[96,2304]{1,0:T(8,128)(2,1)S(1)} %pack_block.1), channel_id=1, source_target_pairs={{0,0},{1,1},{2,2},{3,3},{4,6},{5,7},{6,4},{7,5},{8,8},{9,9},{10,10... | collective-permute-start | bytes 1327112 | tf_op jit(solution)/shard_map/ppermute | solution.py:615
  72.7 18.1 %collective-permute-start.31 = (bf16[96,2304]{1,0:T(8,128)(2,1)S(1)}, bf16[96,2304]{1,0:T(8,128)(2,1)S(1)}, u32[]{:S(2)}, u32[]{:S(2)}) collective-permute-start(bf16[96,2304]{1,0:T(8,128)(2,1)S(1)} %pack_block.1), channel_id=1, source_target_pairs={{0,6},{1,7},{2,4},{3,5},{4,0},{5,1},{6,2},{7,3},{8,14},{9,15},{10,... | collective-permute-start | bytes 1327112 | tf_op jit(solution)/shard_map/ppermute | solution.py:615
  91.6 12.5 %collective-permute-start.33 = (bf16[2,96,768]{2,1,0:T(8,128)(2,1)S(1)}, bf16[2,96,768]{2,1,0:T(8,128)(2,1)S(1)}, u32[]{:S(2)}, u32[]{:S(2)}) collective-permute-start(bf16[2,96,768]{2,1,0:T(8,128)(2,1)S(1)} %get-tuple-element.198.refs_0_), channel_id=1, source_target_pairs={{0,8},{1,9},{2,10},{3,11},{4,12},{5,13},{6,14},{7,15},{8,0},{9,1},... | collective-permute-start | bytes 884744 | tf_op jit(solution)/shard_map/ppermute | solution.py:615
  110.3 17.7 %collective-permute-start.40 = (bf16[2,96,1536]{2,1,0:T(8,128)(2,1)S(1)}, bf16[2,96,1536]{2,1,0:T(8,128)(2,1)S(1)}, u32[]{:S(2)}, u32[]{:S(2)}) collective-permute-start(bf16[2,96,1536]{2,1,0:T(8,128)(2,1)S(1)} %get-tuple-element.213.refs_0_), channel_id=1, source_target_pairs={{0,8},{1,9},{2,10},{3,11},{4,12},{5,13},{6,14},{7,15},{8,0},{9,1},... | collective-permute-start | bytes 1769480 | tf_op jit(solution)/shard_map/ppermute | solution.py:615
  111.6 16.4 %collective-permute-start.41 = (bf16[2,96,1536]{2,1,0:T(8,128)(2,1)S(1)}, bf16[2,96,1536]{2,1,0:T(8,128)(2,1)S(1)}, u32[]{:S(2)}, u32[]{:S(2)}) collective-permute-start(bf16[2,96,1536]{2,1,0:T(8,128)(2,1)S(1)} %get-tuple-element.213.refs_0_), channel_id=1, source_target_pairs={{0,16},{1,17},{2,18},{3,19},{4,20},{5,21},{6,22},{7,23},{8,24},{9,... | collective-permute-start | bytes 1769480 | tf_op jit(solution)/shard_map/ppermute | solution.py:615
  128.2 16.5 %collective-permute-start.47 = (bf16[2,96,1536]{2,1,0:T(8,128)(2,1)S(1)}, bf16[2,96,1536]{2,1,0:T(8,128)(2,1)S(1)}, u32[]{:S(2)}, u32[]{:S(2)}) collective-permute-start(bf16[2,96,1536]{2,1,0:T(8,128)(2,1)S(1)} %get-tuple-element.213.refs_0_), channel_id=1, source_target_pairs={{0,24},{1,25},{2,26},{3,27},{4,28},{5,29},{6,30},{7,31},{8,16},{9,... | collective-permute-start | bytes 1769480 | tf_op jit(solution)/shard_map/ppermute | solution.py:615
  154.5 18.2 %collective-permute-start.64 = (bf16[192,1536]{1,0:T(8,128)(2,1)S(1)}, bf16[192,1536]{1,0:T(8,128)(2,1)S(1)}, u32[]{:S(2)}, u32[]{:S(2)}) collective-permute-start(bf16[192,1536]{1,0:T(8,128)(2,1)S(1)} %get-tuple-element.257), channel_id=1, source_target_pairs={{0,8},{1,9},{2,10},{3,11},{4,12},{5,13},{6,14},{7,15},{8,0},{9,1},... | collective-permute-start | bytes 1769480 | tf_op jit(solution)/shard_map/ppermute | solution.py:615
  155.2 17.5 %collective-permute-start.65 = (bf16[192,1536]{1,0:T(8,128)(2,1)S(1)}, bf16[192,1536]{1,0:T(8,128)(2,1)S(1)}, u32[]{:S(2)}, u32[]{:S(2)}) collective-permute-start(bf16[192,1536]{1,0:T(8,128)(2,1)S(1)} %get-tuple-element.258), channel_id=1, source_target_pairs={{0,16},{1,17},{2,18},{3,19},{4,20},{5,21},{6,22},{7,23},{8,24},{9,... | collective-permute-start | bytes 1769480 | tf_op jit(solution)/shard_map/ppermute | solution.py:615
  172.7 16.5 %collective-permute-start.66 = (bf16[192,1536]{1,0:T(8,128)(2,1)S(1)}, bf16[192,1536]{1,0:T(8,128)(2,1)S(1)}, u32[]{:S(2)}, u32[]{:S(2)}) collective-permute-start(bf16[192,1536]{1,0:T(8,128)(2,1)S(1)} %get-tuple-element.259), channel_id=1, source_target_pairs={{0,24},{1,25},{2,26},{3,27},{4,28},{5,29},{6,30},{7,31},{8,16},{9,... | collective-permute-start | bytes 1769480 | tf_op jit(solution)/shard_map/ppermute | solution.py:615
  190.9 13.9 %collective-permute-start.71 = (bf16[192,768]{1,0:T(8,128)(2,1)S(1)}, bf16[192,768]{1,0:T(8,128)(2,1)S(1)}, u32[]{:S(2)}, u32[]{:S(2)}) collective-permute-start(bf16[192,768]{1,0:T(8,128)(2,1)S(1)} %get-tuple-element.273), channel_id=1, source_target_pairs={{0,24},{1,25},{2,26},{3,27},{4,28},{5,29},{6,30},{7,31},{8,16},{9,... | collective-permute-start | bytes 884744 | tf_op jit(solution)/shard_map/ppermute | solution.py:615
  194.6 15.9 %collective-permute-start.67 = (bf16[128,768]{1,0:T(8,128)(2,1)S(1)}, bf16[128,768]{1,0:T(8,128)(2,1)S(1)}, u32[]{:S(2)}, u32[]{:S(2)}) collective-permute-start(bf16[128,768]{1,0:T(8,128)(2,1)S(1)} %get-tuple-element.262), channel_id=1, source_target_pairs={{0,4},{1,5},{2,6},{3,7},{4,0},{5,1},{6,2},{7,3},{8,12},{9,13},{10,... | collective-permute-start | bytes 589832 | tf_op jit(solution)/shard_map/ppermute | solution.py:615
  204.8 23.4 %collective-permute-start.75 = (bf16[192,1536]{1,0:T(8,128)(2,1)S(1)}, bf16[192,1536]{1,0:T(8,128)(2,1)S(1)}, u32[]{:S(2)}, u32[]{:S(2)}) collective-permute-start(bf16[192,1536]{1,0:T(8,128)(2,1)S(1)} %get-tuple-element.286), channel_id=1, source_target_pairs={{0,8},{1,9},{2,10},{3,11},{4,12},{5,13},{6,14},{7,15},{8,0},{9,1},... | collective-permute-start | bytes 1769480 | tf_op jit(solution)/shard_map/ppermute | solution.py:615
  205.8 22.4 %collective-permute-start.76 = (bf16[192,1536]{1,0:T(8,128)(2,1)S(1)}, bf16[192,1536]{1,0:T(8,128)(2,1)S(1)}, u32[]{:S(2)}, u32[]{:S(2)}) collective-permute-start(bf16[192,1536]{1,0:T(8,128)(2,1)S(1)} %get-tuple-element.288), channel_id=1, source_target_pairs={{0,16},{1,17},{2,18},{3,19},{4,20},{5,21},{6,22},{7,23},{8,24},{9,... | collective-permute-start | bytes 1769480 | tf_op jit(solution)/shard_map/ppermute | solution.py:615
  209.8 21.1 %collective-permute-start.79 = (bf16[96,2304]{1,0:T(8,128)(2,1)S(1)}, bf16[96,2304]{1,0:T(8,128)(2,1)S(1)}, u32[]{:S(2)}, u32[]{:S(2)}) collective-permute-start(bf16[96,2304]{1,0:T(8,128)(2,1)S(1)} %get-tuple-element.295), channel_id=1, source_target_pairs={{0,0},{1,1},{2,2},{3,3},{4,6},{5,7},{6,4},{7,5},{8,8},{9,9},{10,10... | collective-permute-start | bytes 1327112 | tf_op jit(solution)/shard_map/ppermute | solution.py:615
  228.2 17.0 %collective-permute-start.77 = (bf16[192,1536]{1,0:T(8,128)(2,1)S(1)}, bf16[192,1536]{1,0:T(8,128)(2,1)S(1)}, u32[]{:S(2)}, u32[]{:S(2)}) collective-permute-start(bf16[192,1536]{1,0:T(8,128)(2,1)S(1)} %get-tuple-element.289), channel_id=1, source_target_pairs={{0,24},{1,25},{2,26},{3,27},{4,28},{5,29},{6,30},{7,31},{8,16},{9,... | collective-permute-start | bytes 1769480 | tf_op jit(solution)/shard_map/ppermute | solution.py:615
  231.7 13.5 %collective-permute-start.78 = (bf16[96,2304]{1,0:T(8,128)(2,1)S(1)}, bf16[96,2304]{1,0:T(8,128)(2,1)S(1)}, u32[]{:S(2)}, u32[]{:S(2)}) collective-permute-start(bf16[96,2304]{1,0:T(8,128)(2,1)S(1)} %get-tuple-element.291), channel_id=1, source_target_pairs={{0,4},{1,5},{2,6},{3,7},{4,2},{5,3},{6,0},{7,1},{8,12},{9,13},{10,... | collective-permute-start | bytes 1327112 | tf_op jit(solution)/shard_map/ppermute | solution.py:615
  248.8 12.4 %collective-permute-start.83 = (bf16[208,768]{1,0:T(8,128)(2,1)}, bf16[208,768]{1,0:T(8,128)(2,1)}, u32[]{:S(2)}, u32[]{:S(2)}) collective-permute-start(bf16[208,768]{1,0:T(8,128)(2,1)} %copy-done.10), channel_id=1, source_target_pairs={{0,8},{1,9},{2,10},{3,11},{4,12},{5,13},{6,14},{7,15},{8,0},{9,1},... | collective-permute-start | bytes 958472 | tf_op jit(solution)/shard_map/ppermute | solution.py:615
  250.4 16.2 %collective-permute-start.84 = (bf16[208,768]{1,0:T(8,128)(2,1)}, bf16[208,768]{1,0:T(8,128)(2,1)}, u32[]{:S(2)}, u32[]{:S(2)}) collective-permute-start(bf16[208,768]{1,0:T(8,128)(2,1)} %copy-done.9), channel_id=1, source_target_pairs={{0,16},{1,17},{2,18},{3,19},{4,20},{5,21},{6,22},{7,23},{8,24},{9,... | collective-permute-start | bytes 958472 | tf_op jit(solution)/shard_map/ppermute | solution.py:615
  251.2 15.3 %collective-permute-start.85 = (bf16[208,768]{1,0:T(8,128)(2,1)}, bf16[208,768]{1,0:T(8,128)(2,1)}, u32[]{:S(2)}, u32[]{:S(2)}) collective-permute-start(bf16[208,768]{1,0:T(8,128)(2,1)} %copy-done.8), channel_id=1, source_target_pairs={{0,24},{1,25},{2,26},{3,27},{4,28},{5,29},{6,30},{7,31},{8,16},{9,... | collective-permute-start | bytes 958472 | tf_op jit(solution)/shard_map/ppermute | solution.py:615
  258.7 19.9 %collective-permute-start.88 = (bf16[96,1536]{1,0:T(8,128)(2,1)}, bf16[96,1536]{1,0:T(8,128)(2,1)S(1)}, u32[]{:S(2)}, u32[]{:S(2)}) collective-permute-start(bf16[96,1536]{1,0:T(8,128)(2,1)} %get-tuple-element.310), channel_id=1, source_target_pairs={{0,0},{1,1},{2,2},{3,3},{4,6},{5,7},{6,4},{7,5},{8,8},{9,9},{10,10... | collective-permute-start | bytes 884744 | tf_op jit(solution)/shard_map/ppermute | solution.py:615
  260.4 18.2 %collective-permute-start.89 = (bf16[96,1536]{1,0:T(8,128)(2,1)S(1)}, bf16[96,1536]{1,0:T(8,128)(2,1)S(1)}, u32[]{:S(2)}, u32[]{:S(2)}) collective-permute-start(bf16[96,1536]{1,0:T(8,128)(2,1)S(1)} %get-tuple-element.311), channel_id=1, source_target_pairs={{0,4},{1,5},{2,6},{3,7},{4,2},{5,3},{6,0},{7,1},{8,12},{9,13},{10,... | collective-permute-start | bytes 884744 | tf_op jit(solution)/shard_map/ppermute | solution.py:615
  274.8 25.7 %collective-permute-start.50 = (bf16[64,768]{1,0:T(8,128)(2,1)}, bf16[64,768]{1,0:T(8,128)(2,1)S(1)}, u32[]{:S(2)}, u32[]{:S(2)}) collective-permute-start(bf16[64,768]{1,0:T(8,128)(2,1)} %copy-done.16), channel_id=1, source_target_pairs={{0,0},{1,1},{2,4},{3,5},{4,2},{5,3},{6,6},{7,7},{8,8},{9,9},{10,12... | collective-permute-start | bytes 294920 | tf_op jit(solution)/shard_map/ppermute | solution.py:615
  276.4 24.0 %collective-permute-start.82 = (f32[64,768]{1,0:T(8,128)}, f32[64,768]{1,0:T(8,128)S(1)}, u32[]{:S(2)}, u32[]{:S(2)}) collective-permute-start(f32[64,768]{1,0:T(8,128)} %copy-done.11), channel_id=1, source_target_pairs={{0,0},{1,1},{2,4},{3,5},{4,2},{5,3},{6,6},{7,7},{8,8},{9,9},{10,12... | collective-permute-start | bytes 589832 | tf_op jit(solution)/shard_map/ppermute | solution.py:615
  286.5 14.0 %collective-permute-start.87 = (bf16[112,768]{1,0:T(8,128)(2,1)S(1)}, bf16[112,768]{1,0:T(8,128)(2,1)S(1)}, u32[]{:S(2)}, u32[]{:S(2)}) collective-permute-start(bf16[112,768]{1,0:T(8,128)(2,1)S(1)} %copy-done.13), channel_id=1, source_target_pairs={{0,4},{1,5},{2,6},{3,7},{4,2},{5,3},{6,0},{7,1},{8,12},{9,13},{10,... | collective-permute-start | bytes 516104 | tf_op jit(solution)/shard_map/ppermute | solution.py:615
  (95 other events, 633.8 us)

commit v4 on v3

--- a/solution.py
+++ b/solution.py
@@ -988,7 +988,7 @@
         )
         after = (grad_attention[0],)
         if layer == 0:
-            after = after + tuple(given_mlp[0][3:]) + tuple(near_packs[upper][1] for upper in range(1, layers))
+            after = after + (output,) + tuple(given_mlp[0][3:]) + tuple(near_packs[upper][1] for upper in range(1, layers))
         if layer == 0:
             height = 2 * shard + 16
             if n_chips > 8:
@@ -1065,7 +1065,7 @@
     sigmoid_cond = jax.nn.sigmoid(cond_full)
     grad_condition = cond_total * sigmoid_cond * (1.0 + cond_full * (1.0 - sigmoid_cond))
 
-    grad_tokens = move(flow, swap_core_half)
+    grad_tokens = move(gate(flow, cond_mine), swap_core_half)
     output, grad_tokens, grad_qkv, grad_out, grad_up, grad_down, vec = call(
         finish_kernel,
         [

time: 315 us -> 311 us (0.987)
  starting transfers between devices: 137 us -> 130 us
    ppermute x102, starting transfers between devices: 137 us -> 130 us  [move(): return lax.ppermute(values, AXES, [(i, target(i)) for i in range(n_all)])]
    unnamed x55 -> x49, local copies, waits for them, and re-layouts: 10.2 us -> 8.2 us
  transfers between devices with their start and end apart: 102 -> 102, of which waited for: 39 -> 41; matrix products, arithmetic and copies ran while one was open for 4% -> 5% of each run, Pallas kernels for 19% -> 20%
where the time goes in v4:
time: 311 us; the launch traced here: 305 us
  starting transfers between devices  130 us (42%)
  waiting for transfers between devices  84.2 us (27%)
  Pallas kernels  63.5 us (20%)
  local copies, waits for them, and re-layouts  16.4 us (5%)
  other arithmetic  6.57 us (2%)
    ppermute x102, starting transfers between devices, move(): return lax.ppermute(values, AXES, [(i, target(i)) for i in range(n_all)])  130 us
    ppermute x102, waiting for transfers between devices, move(): return lax.ppermute(values, AXES, [(i, target(i)) for i in range(n_all)])  84.2 us
    pallas_call x37, Pallas kernels, call(): pl.pallas_call(run, out_shape=out_shape, in_specs=in_specs, out_specs=out...  59.6 us
    unnamed x49, local copies, waits for them, and re-layouts  8.2 us
  transfers between devices with their start and end apart: 102, of which 41 were waited for; matrix products, arithmetic and copies ran while one was open for 5% of the time, Pallas kernels for 20%

profile of v4, /device:TPU:0, one launch (start us, length us, event | category | flops | bytes accessed | tf_op | source)
XLA Modules:
  0.0 305.5 jit_solution(16905057177696704750)
XLA Ops:
  3.8 2.9 collective-permute-start.2
  22.1 3.6 %collective-permute-start.14 = (bf16[96,1536]{1,0:T(8,128)(2,1)S(1)}, bf16[96,1536]{1,0:T(8,128)(2,1)S(1)}, u32[]{:S(2)}, u32[]{:S(2)}) collective-permute-start(bf16[96,1536]{1,0:T(8,128)(2,1)S(1)} %pack_mlp.1), channel_id=1, source_target_pairs={{0,6},{1,7},{2,4},{3,5},{4,0},{5,1},{6,2},{7,3},{8,14},{9,15},{10,... | collective-permute-start | bytes 884744 | tf_op jit(solution)/shard_map/ppermute | solution.py:615
  35.2 8.2 %collective-permute-start.15 = (f32[2,2,6,192]{3,2,1,0:T(8,128)S(1)}, f32[2,2,6,192]{3,2,1,0:T(8,128)S(1)}, u32[]{:S(2)}, u32[]{:S(2)}) collective-permute-start(f32[2,2,6,192]{3,2,1,0:T(8,128)S(1)} %fusion.9), channel_id=1, source_target_pairs={{0,4},{1,5},{2,6},{3,7},{4,0},{5,1},{6,2},{7,3},{8,12},{9,13},{10,... | collective-permute-start | bytes 55304 | tf_op jit(solution)/shard_map/ppermute | solution.py:615
  45.0 4.0 %collective-permute-start.18 = (f32[2,6,192]{2,1,0:T(8,128)S(1)}, f32[2,6,192]{2,1,0:T(8,128)S(1)}, u32[]{:S(2)}, u32[]{:S(2)}) collective-permute-start(f32[2,6,192]{2,1,0:T(8,128)S(1)} %get-tuple-element.376), channel_id=1, source_target_pairs={{0,3},{1,2},{2,1},{3,0},{4,7},{5,6},{6,5},{7,4},{8,11},{9,10},{10,... | collective-permute-start | bytes 27656 | tf_op jit(solution)/shard_map/ppermute | solution.py:615
  56.9 5.7 %collective-permute-start.19 = (bf16[64,768]{1,0:T(8,128)(2,1)S(1)}, bf16[64,768]{1,0:T(8,128)(2,1)S(1)}, u32[]{:S(2)}, u32[]{:S(2)}) collective-permute-start(bf16[64,768]{1,0:T(8,128)(2,1)S(1)} %get-tuple-element.182.refs_0_), channel_id=1, source_target_pairs={{0,1},{1,0},{2,3},{3,2},{4,5},{5,4},{6,7},{7,6},{8,9},{9,8},{10,11... | collective-permute-start | bytes 294920 | tf_op jit(solution)/shard_map/ppermute | solution.py:615
  72.7 3.6 %collective-permute-start.31 = (bf16[96,2304]{1,0:T(8,128)(2,1)S(1)}, bf16[96,2304]{1,0:T(8,128)(2,1)S(1)}, u32[]{:S(2)}, u32[]{:S(2)}) collective-permute-start(bf16[96,2304]{1,0:T(8,128)(2,1)S(1)} %pack_block.1), channel_id=1, source_target_pairs={{0,6},{1,7},{2,4},{3,5},{4,0},{5,1},{6,2},{7,3},{8,14},{9,15},{10,... | collective-permute-start | bytes 1327112 | tf_op jit(solution)/shard_map/ppermute | solution.py:615
  76.3 5.1 %collective-permute-start.25 = (bf16[64,768]{1,0:T(8,128)(2,1)S(1)}, bf16[64,768]{1,0:T(8,128)(2,1)S(1)}, u32[]{:S(2)}, u32[]{:S(2)}) collective-permute-start(bf16[64,768]{1,0:T(8,128)(2,1)S(1)} %add_convert_fusion.7), channel_id=1, source_target_pairs={{0,1},{1,0},{2,3},{3,2},{4,5},{5,4},{6,7},{7,6},{8,9},{9,8},{10,11... | collective-permute-start | bytes 294920 | tf_op jit(solution)/shard_map/ppermute | solution.py:615
  81.4 6.0 %collective-permute-done.25.refs_4_ = bf16[64,768]{1,0:T(8,128)(2,1)S(1)} collective-permute-done((bf16[64,768]{1,0:T(8,128)(2,1)S(1)}, bf16[64,768]{1,0:T(8,128)(2,1)S(1)}, u32[]{:S(2)}, u32[]{:S(2)}) %collective-permute-start.25) | collective-permute-done | bytes 98336 | tf_op jit(solution)/shard_map/ppermute | solution.py:615
  93.6 5.9 %collective-permute-start.27 = (bf16[64,768]{1,0:T(8,128)(2,1)S(1)}, bf16[64,768]{1,0:T(8,128)(2,1)S(1)}, u32[]{:S(2)}, u32[]{:S(2)}) collective-permute-start(bf16[64,768]{1,0:T(8,128)(2,1)S(1)} %get-tuple-element.192.refs_0_), channel_id=1, source_target_pairs={{0,4},{1,5},{2,6},{3,7},{4,0},{5,1},{6,2},{7,3},{8,12},{9,13},{10,... | collective-permute-start | bytes 294920 | tf_op jit(solution)/shard_map/ppermute | solution.py:615
  104.1 5.4 %collective-permute-start.35 = (bf16[128,768]{1,0:T(8,128)(2,1)S(1)}, bf16[128,768]{1,0:T(8,128)(2,1)S(1)}, u32[]{:S(2)}, u32[]{:S(2)}) collective-permute-start(bf16[128,768]{1,0:T(8,128)(2,1)S(1)} %get-tuple-element.201), channel_id=1, source_target_pairs={{0,4},{1,5},{2,6},{3,7},{4,0},{5,1},{6,2},{7,3},{8,12},{9,13},{10,... | collective-permute-start | bytes 589832 | tf_op jit(solution)/shard_map/ppermute | solution.py:615
  115.9 2.8 collective-permute-done.36.refs_4_
  121.4 2.8 collective-permute-done.37.refs_1_
  131.9 3.0 collective-permute-done.43.refs_4_
  138.2 3.2 %collective-permute-done.44.refs_1_ = bf16[64,768]{1,0:T(8,128)(2,1)S(1)} collective-permute-done((bf16[64,768]{1,0:T(8,128)(2,1)S(1)}, bf16[64,768]{1,0:T(8,128)(2,1)S(1)}, u32[]{:S(2)}, u32[]{:S(2)}) %collective-permute-start.44) | collective-permute-done | bytes 98336 | tf_op jit(solution)/shard_map/ppermute | solution.py:615
  149.8 4.7 %mlp_grad.2 = (bf16[192,1536]{1,0:T(8,128)(2,1)S(1)}, bf16[192,1536]{1,0:T(8,128)(2,1)S(1)}, bf16[192,1536]{1,0:T(8,128)(2,1)S(1)}, bf16[192,1536]{1,0:T(8,128)(2,1)S(1)}, f32[8,192]{1,0:T(8,128)S(1)}) custom-call(s32[4]{0:T(128)S(1)} %pad_add_fusion.refs_0_.place_ref, bf16[256,768]{1,0:T(8,128)(2,1)S(1)} %get-tuple-element.222.refs_1_, ...), custom_call_target="tpu_custom_call" | custom-call | flops 603979776 | bytes 3938304 | tf_op jit(solution)/shard_map/mlp_grad/pallas_call | solution.py:94
  158.8 2.9 collective-permute-done.55.refs_4_
  164.7 2.9 collective-permute-done.56.refs_1_
  168.9 3.6 %attention_back.2 = (bf16[256,768]{1,0:T(8,128)(2,1)S(1)}, bf16[256,576]{1,0:T(8,128)(2,1)S(1)}, f32[64,768]{1,0:T(8,128)S(1)}, f32[64,768]{1,0:T(8,128)S(1)}, bf16[128,768]{1,0:T(8,128)(2,1)S(1)}) custom-call(bf16[64,768]{1,0:T(8,128)(2,1)S(1)} %get-tuple-element.233.refs_0_, bf16[64,768]{1,0:T(8,128)(2,1)S(1)} %collective-permute-done.56.refs_1_, ...), custom_call_target="tpu_custom_call" | custom-call | flops 704643072 | bytes 3145728 | tf_op jit(solution)/shard_map/attention_back/pallas_call | solution.py:94
  175.9 3.2 %attention_grad.2 = (bf16[192,768]{1,0:T(8,128)(2,1)S(1)}, bf16[192,768]{1,0:T(8,128)(2,1)S(1)}, bf16[192,768]{1,0:T(8,128)(2,1)S(1)}, bf16[192,768]{1,0:T(8,128)(2,1)S(1)}, f32[8,192]{1,0:T(8,128)S(1)}) custom-call(s32[4]{0:T(128)S(1)} %pad_add_fusion.refs_0_.place_ref, bf16[256,768]{1,0:T(8,128)(2,1)S(1)} %get-tuple-element.235.refs_1_, ...), custom_call_target="tpu_custom_call" | custom-call | flops 352321536 | bytes 2371584 | tf_op jit(solution)/shard_map/attention_grad/pallas_call | solution.py:94
  181.6 3.1 %collective-permute-done.61.refs_1_ = bf16[64,768]{1,0:T(8,128)(2,1)S(1)} collective-permute-done((bf16[64,768]{1,0:T(8,128)(2,1)S(1)}, bf16[64,768]{1,0:T(8,128)(2,1)S(1)}, u32[]{:S(2)}, u32[]{:S(2)}) %collective-permute-start.61) | collective-permute-done | bytes 98336 | tf_op jit(solution)/shard_map/ppermute | solution.py:615
  184.7 4.5 %collective-permute-done.66.refs_8_ = bf16[192,1536]{1,0:T(8,128)(2,1)S(1)} collective-permute-done((bf16[192,1536]{1,0:T(8,128)(2,1)S(1)}, bf16[192,1536]{1,0:T(8,128)(2,1)S(1)}, u32[]{:S(2)}, u32[]{:S(2)}) %collective-permute-start.66) | collective-permute-done | bytes 589856 | tf_op jit(solution)/shard_map/ppermute | solution.py:615
  194.7 4.7 %mlp_grad.3 = (bf16[192,1536]{1,0:T(8,128)(2,1)S(1)}, bf16[192,1536]{1,0:T(8,128)(2,1)S(1)}, bf16[192,1536]{1,0:T(8,128)(2,1)S(1)}, bf16[192,1536]{1,0:T(8,128)(2,1)S(1)}, f32[8,192]{1,0:T(8,128)S(1)}) custom-call(s32[4]{0:T(128)S(1)} %pad_add_fusion.refs_0_.place_ref, bf16[256,768]{1,0:T(8,128)(2,1)S(1)} %get-tuple-element.251.refs_1_, ...), custom_call_target="tpu_custom_call" | custom-call | flops 603979776 | bytes 3938304 | tf_op jit(solution)/shard_map/mlp_grad/pallas_call | solution.py:94
  199.4 5.4 %collective-permute-done.71.refs_4_ = bf16[192,768]{1,0:T(8,128)(2,1)S(1)} collective-permute-done((bf16[192,768]{1,0:T(8,128)(2,1)S(1)}, bf16[192,768]{1,0:T(8,128)(2,1)S(1)}, u32[]{:S(2)}, u32[]{:S(2)}) %collective-permute-start.71) | collective-permute-done | bytes 294944 | tf_op jit(solution)/shard_map/ppermute | solution.py:615
  207.1 2.7 sum_parts.3
  212.4 3.2 %collective-permute-done.68.refs_4_ = bf16[64,768]{1,0:T(8,128)(2,1)S(1)} collective-permute-done((bf16[64,768]{1,0:T(8,128)(2,1)S(1)}, bf16[64,768]{1,0:T(8,128)(2,1)S(1)}, u32[]{:S(2)}, u32[]{:S(2)}) %collective-permute-start.68) | collective-permute-done | bytes 98336 | tf_op jit(solution)/shard_map/ppermute | solution.py:615
  224.8 3.4 %attention_back.3 = (bf16[256,768]{1,0:T(8,128)(2,1)S(1)}, bf16[256,576]{1,0:T(8,128)(2,1)S(1)}, f32[64,768]{1,0:T(8,128)S(1)}, f32[64,768]{1,0:T(8,128)S(1)}, bf16[128,768]{1,0:T(8,128)(2,1)S(1)}) custom-call(bf16[64,768]{1,0:T(8,128)(2,1)S(1)} %get-tuple-element.274.refs_0_, bf16[64,768]{1,0:T(8,128)(2,1)S(1)} %collective-permute-done.72.refs_1_, ...), custom_call_target="tpu_custom_call" | custom-call | flops 704643072 | bytes 3145728 | tf_op jit(solution)/shard_map/attention_back/pallas_call | solution.py:94
  228.2 2.7 collective-permute-start.77
  231.9 5.9 %collective-permute-done.49.refs_4_ = bf16[64,768]{1,0:T(8,128)(2,1)S(1)} collective-permute-done((bf16[64,768]{1,0:T(8,128)(2,1)S(1)}, bf16[64,768]{1,0:T(8,128)(2,1)S(1)}, u32[]{:S(2)}, u32[]{:S(2)}) %collective-permute-start.49) | collective-permute-done | bytes 98336 | tf_op jit(solution)/shard_map/ppermute | solution.py:615
  239.0 4.6 %attention_grad.3 = (bf16[208,768]{1,0:T(8,128)(2,1)S(1)}, bf16[208,768]{1,0:T(8,128)(2,1)S(1)}, bf16[208,768]{1,0:T(8,128)(2,1)S(1)}, bf16[208,768]{1,0:T(8,128)(2,1)S(1)}, f32[8,192]{1,0:T(8,128)}) custom-call(s32[4]{0:T(128)S(1)} %pad_add_fusion.refs_0_.place_ref, bf16[256,768]{1,0:T(8,128)(2,1)S(1)} %get-tuple-element.276.refs_1_, ...), custom_call_target="tpu_custom_call" | custom-call | flops 352321536 | bytes 2476032 | tf_op jit(solution)/shard_map/attention_grad/pallas_call | solution.py:94
  244.3 3.0 collective-permute-done.78.refs_7_
  277.2 6.3 %collective-permute-done.89.refs_5_ = bf16[96,1536]{1,0:T(8,128)(2,1)S(1)} collective-permute-done((bf16[96,1536]{1,0:T(8,128)(2,1)}, bf16[96,1536]{1,0:T(8,128)(2,1)S(1)}, u32[]{:S(2)}, u32[]{:S(2)}) %collective-permute-start.89) | collective-permute-done | bytes 294944 | tf_op jit(solution)/shard_map/ppermute | solution.py:615
  292.0 2.8 copy.77
  (336 shorter events, 171.5 us)
Async XLA Ops:
  21.4 13.1 %collective-permute-start.13 = (bf16[96,1536]{1,0:T(8,128)(2,1)S(1)}, bf16[96,1536]{1,0:T(8,128)(2,1)S(1)}, u32[]{:S(2)}, u32[]{:S(2)}) collective-permute-start(bf16[96,1536]{1,0:T(8,128)(2,1)S(1)} %pack_mlp.1), channel_id=1, source_target_pairs={{0,0},{1,1},{2,2},{3,3},{4,6},{5,7},{6,4},{7,5},{8,8},{9,9},{10,10... | collective-permute-start | bytes 884744 | tf_op jit(solution)/shard_map/ppermute | solution.py:615
  22.1 12.4 %collective-permute-start.14 = (bf16[96,1536]{1,0:T(8,128)(2,1)S(1)}, bf16[96,1536]{1,0:T(8,128)(2,1)S(1)}, u32[]{:S(2)}, u32[]{:S(2)}) collective-permute-start(bf16[96,1536]{1,0:T(8,128)(2,1)S(1)} %pack_mlp.1), channel_id=1, source_target_pairs={{0,6},{1,7},{2,4},{3,5},{4,0},{5,1},{6,2},{7,3},{8,14},{9,15},{10,... | collective-permute-start | bytes 884744 | tf_op jit(solution)/shard_map/ppermute | solution.py:615
  31.0 18.0 %collective-permute-start.7 = (bf16[2,112,768]{2,1,0:T(8,128)(2,1)S(1)}, bf16[2,112,768]{2,1,0:T(8,128)(2,1)S(1)}, u32[]{:S(2)}, u32[]{:S(2)}) collective-permute-start(bf16[2,112,768]{2,1,0:T(8,128)(2,1)S(1)} %couple.5.refs_0_), channel_id=1, source_target_pairs={{0,8},{1,9},{2,10},{3,11},{4,12},{5,13},{6,14},{7,15},{8,0},{9,1},... | collective-permute-start | bytes 1032200 | tf_op jit(solution)/shard_map/ppermute | solution.py:615
  32.2 17.6 %collective-permute-start.8 = (bf16[2,112,768]{2,1,0:T(8,128)(2,1)S(1)}, bf16[2,112,768]{2,1,0:T(8,128)(2,1)S(1)}, u32[]{:S(2)}, u32[]{:S(2)}) collective-permute-start(bf16[2,112,768]{2,1,0:T(8,128)(2,1)S(1)} %couple.5.refs_0_), channel_id=1, source_target_pairs={{0,16},{1,17},{2,18},{3,19},{4,20},{5,21},{6,22},{7,23},{8,24},{9,... | collective-permute-start | bytes 1032200 | tf_op jit(solution)/shard_map/ppermute | solution.py:615
  33.6 16.9 %collective-permute-start.9 = (bf16[2,112,768]{2,1,0:T(8,128)(2,1)S(1)}, bf16[2,112,768]{2,1,0:T(8,128)(2,1)S(1)}, u32[]{:S(2)}, u32[]{:S(2)}) collective-permute-start(bf16[2,112,768]{2,1,0:T(8,128)(2,1)S(1)} %couple.5.refs_0_), channel_id=1, source_target_pairs={{0,24},{1,25},{2,26},{3,27},{4,28},{5,29},{6,30},{7,31},{8,16},{9,... | collective-permute-start | bytes 1032200 | tf_op jit(solution)/shard_map/ppermute | solution.py:615
  53.4 16.0 %collective-permute-start.22 = (bf16[2,96,1536]{2,1,0:T(8,128)(2,1)S(1)}, bf16[2,96,1536]{2,1,0:T(8,128)(2,1)S(1)}, u32[]{:S(2)}, u32[]{:S(2)}) collective-permute-start(bf16[2,96,1536]{2,1,0:T(8,128)(2,1)S(1)} %couple.6.refs_0_), channel_id=1, source_target_pairs={{0,8},{1,9},{2,10},{3,11},{4,12},{5,13},{6,14},{7,15},{8,0},{9,1},... | collective-permute-start | bytes 1769480 | tf_op jit(solution)/shard_map/ppermute | solution.py:615
  54.1 15.3 %collective-permute-start.23 = (bf16[2,96,1536]{2,1,0:T(8,128)(2,1)S(1)}, bf16[2,96,1536]{2,1,0:T(8,128)(2,1)S(1)}, u32[]{:S(2)}, u32[]{:S(2)}) collective-permute-start(bf16[2,96,1536]{2,1,0:T(8,128)(2,1)S(1)} %couple.6.refs_0_), channel_id=1, source_target_pairs={{0,16},{1,17},{2,18},{3,19},{4,20},{5,21},{6,22},{7,23},{8,24},{9,... | collective-permute-start | bytes 1769480 | tf_op jit(solution)/shard_map/ppermute | solution.py:615
  69.6 22.0 %collective-permute-start.29 = (bf16[2,96,1536]{2,1,0:T(8,128)(2,1)S(1)}, bf16[2,96,1536]{2,1,0:T(8,128)(2,1)S(1)}, u32[]{:S(2)}, u32[]{:S(2)}) collective-permute-start(bf16[2,96,1536]{2,1,0:T(8,128)(2,1)S(1)} %couple.6.refs_0_), channel_id=1, source_target_pairs={{0,24},{1,25},{2,26},{3,27},{4,28},{5,29},{6,30},{7,31},{8,16},{9,... | collective-permute-start | bytes 1769480 | tf_op jit(solution)/shard_map/ppermute | solution.py:615
  72.0 18.7 %collective-permute-start.30 = (bf16[96,2304]{1,0:T(8,128)(2,1)S(1)}, bf16[96,2304]{1,0:T(8,128)(2,1)S(1)}, u32[]{:S(2)}, u32[]{:S(2)}) collective-permute-start(bf16[96,2304]{1,0:T(8,128)(2,1)S(1)} %pack_block.1), channel_id=1, source_target_pairs={{0,0},{1,1},{2,2},{3,3},{4,6},{5,7},{6,4},{7,5},{8,8},{9,9},{10,10... | collective-permute-start | bytes 1327112 | tf_op jit(solution)/shard_map/ppermute | solution.py:615
  72.7 18.1 %collective-permute-start.31 = (bf16[96,2304]{1,0:T(8,128)(2,1)S(1)}, bf16[96,2304]{1,0:T(8,128)(2,1)S(1)}, u32[]{:S(2)}, u32[]{:S(2)}) collective-permute-start(bf16[96,2304]{1,0:T(8,128)(2,1)S(1)} %pack_block.1), channel_id=1, source_target_pairs={{0,6},{1,7},{2,4},{3,5},{4,0},{5,1},{6,2},{7,3},{8,14},{9,15},{10,... | collective-permute-start | bytes 1327112 | tf_op jit(solution)/shard_map/ppermute | solution.py:615
  88.2 11.3 %collective-permute-start.26 = (bf16[64,768]{1,0:T(8,128)(2,1)S(1)}, bf16[64,768]{1,0:T(8,128)(2,1)S(1)}, u32[]{:S(2)}, u32[]{:S(2)}) collective-permute-start(bf16[64,768]{1,0:T(8,128)(2,1)S(1)} %get-tuple-element.192.refs_0_), channel_id=1, source_target_pairs={{0,1},{1,0},{2,3},{3,2},{4,5},{5,4},{6,7},{7,6},{8,9},{9,8},{10,11... | collective-permute-start | bytes 294920 | tf_op jit(solution)/shard_map/ppermute | solution.py:615
  91.6 12.5 %collective-permute-start.33 = (bf16[2,96,768]{2,1,0:T(8,128)(2,1)S(1)}, bf16[2,96,768]{2,1,0:T(8,128)(2,1)S(1)}, u32[]{:S(2)}, u32[]{:S(2)}) collective-permute-start(bf16[2,96,768]{2,1,0:T(8,128)(2,1)S(1)} %get-tuple-element.198.refs_0_), channel_id=1, source_target_pairs={{0,8},{1,9},{2,10},{3,11},{4,12},{5,13},{6,14},{7,15},{8,0},{9,1},... | collective-permute-start | bytes 884744 | tf_op jit(solution)/shard_map/ppermute | solution.py:615
  110.3 17.7 %collective-permute-start.40 = (bf16[2,96,1536]{2,1,0:T(8,128)(2,1)S(1)}, bf16[2,96,1536]{2,1,0:T(8,128)(2,1)S(1)}, u32[]{:S(2)}, u32[]{:S(2)}) collective-permute-start(bf16[2,96,1536]{2,1,0:T(8,128)(2,1)S(1)} %get-tuple-element.213.refs_0_), channel_id=1, source_target_pairs={{0,8},{1,9},{2,10},{3,11},{4,12},{5,13},{6,14},{7,15},{8,0},{9,1},... | collective-permute-start | bytes 1769480 | tf_op jit(solution)/shard_map/ppermute | solution.py:615
  111.6 16.4 %collective-permute-start.41 = (bf16[2,96,1536]{2,1,0:T(8,128)(2,1)S(1)}, bf16[2,96,1536]{2,1,0:T(8,128)(2,1)S(1)}, u32[]{:S(2)}, u32[]{:S(2)}) collective-permute-start(bf16[2,96,1536]{2,1,0:T(8,128)(2,1)S(1)} %get-tuple-element.213.refs_0_), channel_id=1, source_target_pairs={{0,16},{1,17},{2,18},{3,19},{4,20},{5,21},{6,22},{7,23},{8,24},{9,... | collective-permute-start | bytes 1769480 | tf_op jit(solution)/shard_map/ppermute | solution.py:615
  128.2 16.5 %collective-permute-start.47 = (bf16[2,96,1536]{2,1,0:T(8,128)(2,1)S(1)}, bf16[2,96,1536]{2,1,0:T(8,128)(2,1)S(1)}, u32[]{:S(2)}, u32[]{:S(2)}) collective-permute-start(bf16[2,96,1536]{2,1,0:T(8,128)(2,1)S(1)} %get-tuple-element.213.refs_0_), channel_id=1, source_target_pairs={{0,24},{1,25},{2,26},{3,27},{4,28},{5,29},{6,30},{7,31},{8,16},{9,... | collective-permute-start | bytes 1769480 | tf_op jit(solution)/shard_map/ppermute | solution.py:615
  154.5 18.2 %collective-permute-start.64 = (bf16[192,1536]{1,0:T(8,128)(2,1)S(1)}, bf16[192,1536]{1,0:T(8,128)(2,1)S(1)}, u32[]{:S(2)}, u32[]{:S(2)}) collective-permute-start(bf16[192,1536]{1,0:T(8,128)(2,1)S(1)} %get-tuple-element.257), channel_id=1, source_target_pairs={{0,8},{1,9},{2,10},{3,11},{4,12},{5,13},{6,14},{7,15},{8,0},{9,1},... | collective-permute-start | bytes 1769480 | tf_op jit(solution)/shard_map/ppermute | solution.py:615
  155.2 17.5 %collective-permute-start.65 = (bf16[192,1536]{1,0:T(8,128)(2,1)S(1)}, bf16[192,1536]{1,0:T(8,128)(2,1)S(1)}, u32[]{:S(2)}, u32[]{:S(2)}) collective-permute-start(bf16[192,1536]{1,0:T(8,128)(2,1)S(1)} %get-tuple-element.258), channel_id=1, source_target_pairs={{0,16},{1,17},{2,18},{3,19},{4,20},{5,21},{6,22},{7,23},{8,24},{9,... | collective-permute-start | bytes 1769480 | tf_op jit(solution)/shard_map/ppermute | solution.py:615
  172.8 16.5 %collective-permute-start.66 = (bf16[192,1536]{1,0:T(8,128)(2,1)S(1)}, bf16[192,1536]{1,0:T(8,128)(2,1)S(1)}, u32[]{:S(2)}, u32[]{:S(2)}) collective-permute-start(bf16[192,1536]{1,0:T(8,128)(2,1)S(1)} %get-tuple-element.259), channel_id=1, source_target_pairs={{0,24},{1,25},{2,26},{3,27},{4,28},{5,29},{6,30},{7,31},{8,16},{9,... | collective-permute-start | bytes 1769480 | tf_op jit(solution)/shard_map/ppermute | solution.py:615
  190.9 13.8 %collective-permute-start.71 = (bf16[192,768]{1,0:T(8,128)(2,1)S(1)}, bf16[192,768]{1,0:T(8,128)(2,1)S(1)}, u32[]{:S(2)}, u32[]{:S(2)}) collective-permute-start(bf16[192,768]{1,0:T(8,128)(2,1)S(1)} %get-tuple-element.273), channel_id=1, source_target_pairs={{0,24},{1,25},{2,26},{3,27},{4,28},{5,29},{6,30},{7,31},{8,16},{9,... | collective-permute-start | bytes 884744 | tf_op jit(solution)/shard_map/ppermute | solution.py:615
  194.6 15.9 %collective-permute-start.67 = (bf16[128,768]{1,0:T(8,128)(2,1)S(1)}, bf16[128,768]{1,0:T(8,128)(2,1)S(1)}, u32[]{:S(2)}, u32[]{:S(2)}) collective-permute-start(bf16[128,768]{1,0:T(8,128)(2,1)S(1)} %get-tuple-element.262), channel_id=1, source_target_pairs={{0,4},{1,5},{2,6},{3,7},{4,0},{5,1},{6,2},{7,3},{8,12},{9,13},{10,... | collective-permute-start | bytes 589832 | tf_op jit(solution)/shard_map/ppermute | solution.py:615
  204.8 23.4 %collective-permute-start.75 = (bf16[192,1536]{1,0:T(8,128)(2,1)S(1)}, bf16[192,1536]{1,0:T(8,128)(2,1)S(1)}, u32[]{:S(2)}, u32[]{:S(2)}) collective-permute-start(bf16[192,1536]{1,0:T(8,128)(2,1)S(1)} %get-tuple-element.286), channel_id=1, source_target_pairs={{0,8},{1,9},{2,10},{3,11},{4,12},{5,13},{6,14},{7,15},{8,0},{9,1},... | collective-permute-start | bytes 1769480 | tf_op jit(solution)/shard_map/ppermute | solution.py:615
  205.8 22.4 %collective-permute-start.76 = (bf16[192,1536]{1,0:T(8,128)(2,1)S(1)}, bf16[192,1536]{1,0:T(8,128)(2,1)S(1)}, u32[]{:S(2)}, u32[]{:S(2)}) collective-permute-start(bf16[192,1536]{1,0:T(8,128)(2,1)S(1)} %get-tuple-element.288), channel_id=1, source_target_pairs={{0,16},{1,17},{2,18},{3,19},{4,20},{5,21},{6,22},{7,23},{8,24},{9,... | collective-permute-start | bytes 1769480 | tf_op jit(solution)/shard_map/ppermute | solution.py:615
  209.8 21.1 %collective-permute-start.79 = (bf16[96,2304]{1,0:T(8,128)(2,1)S(1)}, bf16[96,2304]{1,0:T(8,128)(2,1)S(1)}, u32[]{:S(2)}, u32[]{:S(2)}) collective-permute-start(bf16[96,2304]{1,0:T(8,128)(2,1)S(1)} %get-tuple-element.295), channel_id=1, source_target_pairs={{0,0},{1,1},{2,2},{3,3},{4,6},{5,7},{6,4},{7,5},{8,8},{9,9},{10,10... | collective-permute-start | bytes 1327112 | tf_op jit(solution)/shard_map/ppermute | solution.py:615
  228.2 19.1 %collective-permute-start.77 = (bf16[192,1536]{1,0:T(8,128)(2,1)S(1)}, bf16[192,1536]{1,0:T(8,128)(2,1)S(1)}, u32[]{:S(2)}, u32[]{:S(2)}) collective-permute-start(bf16[192,1536]{1,0:T(8,128)(2,1)S(1)} %get-tuple-element.289), channel_id=1, source_target_pairs={{0,24},{1,25},{2,26},{3,27},{4,28},{5,29},{6,30},{7,31},{8,16},{9,... | collective-permute-start | bytes 1769480 | tf_op jit(solution)/shard_map/ppermute | solution.py:615
  231.7 15.6 %collective-permute-start.78 = (bf16[96,2304]{1,0:T(8,128)(2,1)S(1)}, bf16[96,2304]{1,0:T(8,128)(2,1)S(1)}, u32[]{:S(2)}, u32[]{:S(2)}) collective-permute-start(bf16[96,2304]{1,0:T(8,128)(2,1)S(1)} %get-tuple-element.291), channel_id=1, source_target_pairs={{0,4},{1,5},{2,6},{3,7},{4,2},{5,3},{6,0},{7,1},{8,12},{9,13},{10,... | collective-permute-start | bytes 1327112 | tf_op jit(solution)/shard_map/ppermute | solution.py:615
  250.8 15.9 %collective-permute-start.83 = (bf16[208,768]{1,0:T(8,128)(2,1)}, bf16[208,768]{1,0:T(8,128)(2,1)}, u32[]{:S(2)}, u32[]{:S(2)}) collective-permute-start(bf16[208,768]{1,0:T(8,128)(2,1)} %copy-done.10), channel_id=1, source_target_pairs={{0,8},{1,9},{2,10},{3,11},{4,12},{5,13},{6,14},{7,15},{8,0},{9,1},... | collective-permute-start | bytes 958472 | tf_op jit(solution)/shard_map/ppermute | solution.py:615
  251.2 15.4 %collective-permute-start.84 = (bf16[208,768]{1,0:T(8,128)(2,1)}, bf16[208,768]{1,0:T(8,128)(2,1)}, u32[]{:S(2)}, u32[]{:S(2)}) collective-permute-start(bf16[208,768]{1,0:T(8,128)(2,1)} %copy-done.9), channel_id=1, source_target_pairs={{0,16},{1,17},{2,18},{3,19},{4,20},{5,21},{6,22},{7,23},{8,24},{9,... | collective-permute-start | bytes 958472 | tf_op jit(solution)/shard_map/ppermute | solution.py:615
  252.6 15.7 %collective-permute-start.85 = (bf16[208,768]{1,0:T(8,128)(2,1)}, bf16[208,768]{1,0:T(8,128)(2,1)}, u32[]{:S(2)}, u32[]{:S(2)}) collective-permute-start(bf16[208,768]{1,0:T(8,128)(2,1)} %copy-done.8), channel_id=1, source_target_pairs={{0,24},{1,25},{2,26},{3,27},{4,28},{5,29},{6,30},{7,31},{8,16},{9,... | collective-permute-start | bytes 958472 | tf_op jit(solution)/shard_map/ppermute | solution.py:615
  264.0 13.2 %collective-permute-start.88 = (bf16[96,1536]{1,0:T(8,128)(2,1)}, bf16[96,1536]{1,0:T(8,128)(2,1)S(1)}, u32[]{:S(2)}, u32[]{:S(2)}) collective-permute-start(bf16[96,1536]{1,0:T(8,128)(2,1)} %get-tuple-element.310), channel_id=1, source_target_pairs={{0,0},{1,1},{2,2},{3,3},{4,6},{5,7},{6,4},{7,5},{8,8},{9,9},{10,10... | collective-permute-start | bytes 884744 | tf_op jit(solution)/shard_map/ppermute | solution.py:615
  265.6 17.9 %collective-permute-start.89 = (bf16[96,1536]{1,0:T(8,128)(2,1)}, bf16[96,1536]{1,0:T(8,128)(2,1)S(1)}, u32[]{:S(2)}, u32[]{:S(2)}) collective-permute-start(bf16[96,1536]{1,0:T(8,128)(2,1)} %get-tuple-element.311), channel_id=1, source_target_pairs={{0,4},{1,5},{2,6},{3,7},{4,2},{5,3},{6,0},{7,1},{8,12},{9,13},{10,... | collective-permute-start | bytes 884744 | tf_op jit(solution)/shard_map/ppermute | solution.py:615
  275.2 21.2 %collective-permute-start.82 = (f32[64,768]{1,0:T(8,128)S(1)}, f32[64,768]{1,0:T(8,128)S(1)}, u32[]{:S(2)}, u32[]{:S(2)}) collective-permute-start(f32[64,768]{1,0:T(8,128)S(1)} %get-tuple-element.299), channel_id=1, source_target_pairs={{0,0},{1,1},{2,4},{3,5},{4,2},{5,3},{6,6},{7,7},{8,8},{9,9},{10,12... | collective-permute-start | bytes 589832 | tf_op jit(solution)/shard_map/ppermute | solution.py:615
  275.9 19.6 %collective-permute-start.86 = (bf16[112,768]{1,0:T(8,128)(2,1)S(1)}, bf16[112,768]{1,0:T(8,128)(2,1)S(1)}, u32[]{:S(2)}, u32[]{:S(2)}) collective-permute-start(bf16[112,768]{1,0:T(8,128)(2,1)S(1)} %get-tuple-element.307), channel_id=1, source_target_pairs={{0,0},{1,1},{2,2},{3,3},{4,6},{5,7},{6,4},{7,5},{8,8},{9,9},{10,10... | collective-permute-start | bytes 516104 | tf_op jit(solution)/shard_map/ppermute | solution.py:615
  (92 other events, 605.6 us)

commit v5 on v4

--- a/solution.py
+++ b/solution.py
@@ -1059,8 +1059,7 @@
     cond_total = jnp.where(
         core == 0, jnp.stack([cond_mine, cond_sent], axis=1), jnp.stack([cond_sent, cond_mine], axis=1)
     ).reshape(1, D)
-    cond_total = gate(cond_total, *near_attention)
-    cond_total = cond_total + xor(cond_total, PARITY)
+    cond_total = gate(cond_total + xor(cond_total, PARITY), *near_attention)
     cond_total = cond_total + xor(cond_total, HALF)
     sigmoid_cond = jax.nn.sigmoid(cond_full)
     grad_condition = cond_total * sigmoid_cond * (1.0 + cond_full * (1.0 - sigmoid_cond))

time: 311 us -> 308 us (level)
  waiting for transfers between devices: 84.2 us -> 80.5 us
    ppermute x102, waiting for transfers between devices: 84.2 us -> 80.5 us  [move(): return lax.ppermute(values, AXES, [(i, target(i)) for i in range(n_all)])]
  transfers between devices with their start and end apart: 102 -> 102, of which waited for: 41 -> 38; matrix products, arithmetic and copies ran while one was open for 5% -> 5% of each run, Pallas kernels for 20% -> 20%
where the time goes in v5:
time: 308 us; the launch traced here: 303 us
  starting transfers between devices  131 us (43%)
  waiting for transfers between devices  80.5 us (26%)
  Pallas kernels  63.5 us (21%)
  local copies, waits for them, and re-layouts  16.4 us (5%)
  other arithmetic  6.57 us (2%)
    ppermute x102, starting transfers between devices, move(): return lax.ppermute(values, AXES, [(i, target(i)) for i in range(n_all)])  131 us
    ppermute x102, waiting for transfers between devices, move(): return lax.ppermute(values, AXES, [(i, target(i)) for i in range(n_all)])  80.5 us
    pallas_call x37, Pallas kernels, call(): pl.pallas_call(run, out_shape=out_shape, in_specs=in_specs, out_specs=out...  59.6 us
    unnamed x49, local copies, waits for them, and re-layouts  8.2 us
  transfers between devices with their start and end apart: 102, of which 38 were waited for; matrix products, arithmetic and copies ran while one was open for 5% of the time, Pallas kernels for 20%

profile of v5, /device:TPU:0, one launch (start us, length us, event | category | flops | bytes accessed | tf_op | source)
XLA Modules:
  0.0 302.7 jit_solution(13687730022531601848)
XLA Ops:
  3.8 2.9 collective-permute-start.2
  22.1 3.6 %collective-permute-start.14 = (bf16[96,1536]{1,0:T(8,128)(2,1)S(1)}, bf16[96,1536]{1,0:T(8,128)(2,1)S(1)}, u32[]{:S(2)}, u32[]{:S(2)}) collective-permute-start(bf16[96,1536]{1,0:T(8,128)(2,1)S(1)} %pack_mlp.1), channel_id=1, source_target_pairs={{0,6},{1,7},{2,4},{3,5},{4,0},{5,1},{6,2},{7,3},{8,14},{9,15},{10,... | collective-permute-start | bytes 884744 | tf_op jit(solution)/shard_map/ppermute | solution.py:615
  35.2 8.2 %collective-permute-start.15 = (f32[2,2,6,192]{3,2,1,0:T(8,128)S(1)}, f32[2,2,6,192]{3,2,1,0:T(8,128)S(1)}, u32[]{:S(2)}, u32[]{:S(2)}) collective-permute-start(f32[2,2,6,192]{3,2,1,0:T(8,128)S(1)} %fusion.9), channel_id=1, source_target_pairs={{0,4},{1,5},{2,6},{3,7},{4,0},{5,1},{6,2},{7,3},{8,12},{9,13},{10,... | collective-permute-start | bytes 55304 | tf_op jit(solution)/shard_map/ppermute | solution.py:615
  45.0 4.0 %collective-permute-start.18 = (f32[2,6,192]{2,1,0:T(8,128)S(1)}, f32[2,6,192]{2,1,0:T(8,128)S(1)}, u32[]{:S(2)}, u32[]{:S(2)}) collective-permute-start(f32[2,6,192]{2,1,0:T(8,128)S(1)} %get-tuple-element.376), channel_id=1, source_target_pairs={{0,3},{1,2},{2,1},{3,0},{4,7},{5,6},{6,5},{7,4},{8,11},{9,10},{10,... | collective-permute-start | bytes 27656 | tf_op jit(solution)/shard_map/ppermute | solution.py:615
  56.9 5.7 %collective-permute-start.19 = (bf16[64,768]{1,0:T(8,128)(2,1)S(1)}, bf16[64,768]{1,0:T(8,128)(2,1)S(1)}, u32[]{:S(2)}, u32[]{:S(2)}) collective-permute-start(bf16[64,768]{1,0:T(8,128)(2,1)S(1)} %get-tuple-element.182.refs_0_), channel_id=1, source_target_pairs={{0,1},{1,0},{2,3},{3,2},{4,5},{5,4},{6,7},{7,6},{8,9},{9,8},{10,11... | collective-permute-start | bytes 294920 | tf_op jit(solution)/shard_map/ppermute | solution.py:615
  72.7 3.6 %collective-permute-start.31 = (bf16[96,2304]{1,0:T(8,128)(2,1)S(1)}, bf16[96,2304]{1,0:T(8,128)(2,1)S(1)}, u32[]{:S(2)}, u32[]{:S(2)}) collective-permute-start(bf16[96,2304]{1,0:T(8,128)(2,1)S(1)} %pack_block.1), channel_id=1, source_target_pairs={{0,6},{1,7},{2,4},{3,5},{4,0},{5,1},{6,2},{7,3},{8,14},{9,15},{10,... | collective-permute-start | bytes 1327112 | tf_op jit(solution)/shard_map/ppermute | solution.py:615
  76.3 5.1 %collective-permute-start.25 = (bf16[64,768]{1,0:T(8,128)(2,1)S(1)}, bf16[64,768]{1,0:T(8,128)(2,1)S(1)}, u32[]{:S(2)}, u32[]{:S(2)}) collective-permute-start(bf16[64,768]{1,0:T(8,128)(2,1)S(1)} %add_convert_fusion.7), channel_id=1, source_target_pairs={{0,1},{1,0},{2,3},{3,2},{4,5},{5,4},{6,7},{7,6},{8,9},{9,8},{10,11... | collective-permute-start | bytes 294920 | tf_op jit(solution)/shard_map/ppermute | solution.py:615
  81.4 6.0 %collective-permute-done.25.refs_4_ = bf16[64,768]{1,0:T(8,128)(2,1)S(1)} collective-permute-done((bf16[64,768]{1,0:T(8,128)(2,1)S(1)}, bf16[64,768]{1,0:T(8,128)(2,1)S(1)}, u32[]{:S(2)}, u32[]{:S(2)}) %collective-permute-start.25) | collective-permute-done | bytes 98336 | tf_op jit(solution)/shard_map/ppermute | solution.py:615
  93.6 5.9 %collective-permute-start.27 = (bf16[64,768]{1,0:T(8,128)(2,1)S(1)}, bf16[64,768]{1,0:T(8,128)(2,1)S(1)}, u32[]{:S(2)}, u32[]{:S(2)}) collective-permute-start(bf16[64,768]{1,0:T(8,128)(2,1)S(1)} %get-tuple-element.192.refs_0_), channel_id=1, source_target_pairs={{0,4},{1,5},{2,6},{3,7},{4,0},{5,1},{6,2},{7,3},{8,12},{9,13},{10,... | collective-permute-start | bytes 294920 | tf_op jit(solution)/shard_map/ppermute | solution.py:615
  104.1 5.4 %collective-permute-start.35 = (bf16[128,768]{1,0:T(8,128)(2,1)S(1)}, bf16[128,768]{1,0:T(8,128)(2,1)S(1)}, u32[]{:S(2)}, u32[]{:S(2)}) collective-permute-start(bf16[128,768]{1,0:T(8,128)(2,1)S(1)} %get-tuple-element.201), channel_id=1, source_target_pairs={{0,4},{1,5},{2,6},{3,7},{4,0},{5,1},{6,2},{7,3},{8,12},{9,13},{10,... | collective-permute-start | bytes 589832 | tf_op jit(solution)/shard_map/ppermute | solution.py:615
  115.9 2.8 collective-permute-done.36.refs_4_
  121.4 2.8 collective-permute-done.37.refs_1_
  131.9 3.0 collective-permute-done.43.refs_4_
  138.2 3.2 %collective-permute-done.44.refs_1_ = bf16[64,768]{1,0:T(8,128)(2,1)S(1)} collective-permute-done((bf16[64,768]{1,0:T(8,128)(2,1)S(1)}, bf16[64,768]{1,0:T(8,128)(2,1)S(1)}, u32[]{:S(2)}, u32[]{:S(2)}) %collective-permute-start.44) | collective-permute-done | bytes 98336 | tf_op jit(solution)/shard_map/ppermute | solution.py:615
  149.8 4.7 %mlp_grad.2 = (bf16[192,1536]{1,0:T(8,128)(2,1)S(1)}, bf16[192,1536]{1,0:T(8,128)(2,1)S(1)}, bf16[192,1536]{1,0:T(8,128)(2,1)S(1)}, bf16[192,1536]{1,0:T(8,128)(2,1)S(1)}, f32[8,192]{1,0:T(8,128)S(1)}) custom-call(s32[4]{0:T(128)S(1)} %pad_add_fusion.refs_0_.place_ref, bf16[256,768]{1,0:T(8,128)(2,1)S(1)} %get-tuple-element.222.refs_1_, ...), custom_call_target="tpu_custom_call" | custom-call | flops 603979776 | bytes 3938304 | tf_op jit(solution)/shard_map/mlp_grad/pallas_call | solution.py:94
  158.8 2.9 collective-permute-done.55.refs_4_
  164.7 2.9 collective-permute-done.56.refs_1_
  168.9 3.6 %attention_back.2 = (bf16[256,768]{1,0:T(8,128)(2,1)S(1)}, bf16[256,576]{1,0:T(8,128)(2,1)S(1)}, f32[64,768]{1,0:T(8,128)S(1)}, f32[64,768]{1,0:T(8,128)S(1)}, bf16[128,768]{1,0:T(8,128)(2,1)S(1)}) custom-call(bf16[64,768]{1,0:T(8,128)(2,1)S(1)} %get-tuple-element.233.refs_0_, bf16[64,768]{1,0:T(8,128)(2,1)S(1)} %collective-permute-done.56.refs_1_, ...), custom_call_target="tpu_custom_call" | custom-call | flops 704643072 | bytes 3145728 | tf_op jit(solution)/shard_map/attention_back/pallas_call | solution.py:94
  175.9 3.2 %attention_grad.2 = (bf16[192,768]{1,0:T(8,128)(2,1)S(1)}, bf16[192,768]{1,0:T(8,128)(2,1)S(1)}, bf16[192,768]{1,0:T(8,128)(2,1)S(1)}, bf16[192,768]{1,0:T(8,128)(2,1)S(1)}, f32[8,192]{1,0:T(8,128)S(1)}) custom-call(s32[4]{0:T(128)S(1)} %pad_add_fusion.refs_0_.place_ref, bf16[256,768]{1,0:T(8,128)(2,1)S(1)} %get-tuple-element.235.refs_1_, ...), custom_call_target="tpu_custom_call" | custom-call | flops 352321536 | bytes 2371584 | tf_op jit(solution)/shard_map/attention_grad/pallas_call | solution.py:94
  181.6 3.1 %collective-permute-done.61.refs_1_ = bf16[64,768]{1,0:T(8,128)(2,1)S(1)} collective-permute-done((bf16[64,768]{1,0:T(8,128)(2,1)S(1)}, bf16[64,768]{1,0:T(8,128)(2,1)S(1)}, u32[]{:S(2)}, u32[]{:S(2)}) %collective-permute-start.61) | collective-permute-done | bytes 98336 | tf_op jit(solution)/shard_map/ppermute | solution.py:615
  184.7 4.5 %collective-permute-done.66.refs_8_ = bf16[192,1536]{1,0:T(8,128)(2,1)S(1)} collective-permute-done((bf16[192,1536]{1,0:T(8,128)(2,1)S(1)}, bf16[192,1536]{1,0:T(8,128)(2,1)S(1)}, u32[]{:S(2)}, u32[]{:S(2)}) %collective-permute-start.66) | collective-permute-done | bytes 589856 | tf_op jit(solution)/shard_map/ppermute | solution.py:615
  194.7 4.7 %mlp_grad.3 = (bf16[192,1536]{1,0:T(8,128)(2,1)S(1)}, bf16[192,1536]{1,0:T(8,128)(2,1)S(1)}, bf16[192,1536]{1,0:T(8,128)(2,1)S(1)}, bf16[192,1536]{1,0:T(8,128)(2,1)S(1)}, f32[8,192]{1,0:T(8,128)S(1)}) custom-call(s32[4]{0:T(128)S(1)} %pad_add_fusion.refs_0_.place_ref, bf16[256,768]{1,0:T(8,128)(2,1)S(1)} %get-tuple-element.251.refs_1_, ...), custom_call_target="tpu_custom_call" | custom-call | flops 603979776 | bytes 3938304 | tf_op jit(solution)/shard_map/mlp_grad/pallas_call | solution.py:94
  199.4 5.4 %collective-permute-done.71.refs_4_ = bf16[192,768]{1,0:T(8,128)(2,1)S(1)} collective-permute-done((bf16[192,768]{1,0:T(8,128)(2,1)S(1)}, bf16[192,768]{1,0:T(8,128)(2,1)S(1)}, u32[]{:S(2)}, u32[]{:S(2)}) %collective-permute-start.71) | collective-permute-done | bytes 294944 | tf_op jit(solution)/shard_map/ppermute | solution.py:615
  207.1 2.7 sum_parts.3
  212.4 3.2 %collective-permute-done.68.refs_4_ = bf16[64,768]{1,0:T(8,128)(2,1)S(1)} collective-permute-done((bf16[64,768]{1,0:T(8,128)(2,1)S(1)}, bf16[64,768]{1,0:T(8,128)(2,1)S(1)}, u32[]{:S(2)}, u32[]{:S(2)}) %collective-permute-start.68) | collective-permute-done | bytes 98336 | tf_op jit(solution)/shard_map/ppermute | solution.py:615
  224.8 3.4 %attention_back.3 = (bf16[256,768]{1,0:T(8,128)(2,1)S(1)}, bf16[256,576]{1,0:T(8,128)(2,1)S(1)}, f32[64,768]{1,0:T(8,128)S(1)}, f32[64,768]{1,0:T(8,128)S(1)}, bf16[128,768]{1,0:T(8,128)(2,1)S(1)}) custom-call(bf16[64,768]{1,0:T(8,128)(2,1)S(1)} %get-tuple-element.274.refs_0_, bf16[64,768]{1,0:T(8,128)(2,1)S(1)} %collective-permute-done.72.refs_1_, ...), custom_call_target="tpu_custom_call" | custom-call | flops 704643072 | bytes 3145728 | tf_op jit(solution)/shard_map/attention_back/pallas_call | solution.py:94
  228.2 2.7 collective-permute-start.77
  231.9 5.9 %collective-permute-done.49.refs_4_ = bf16[64,768]{1,0:T(8,128)(2,1)S(1)} collective-permute-done((bf16[64,768]{1,0:T(8,128)(2,1)S(1)}, bf16[64,768]{1,0:T(8,128)(2,1)S(1)}, u32[]{:S(2)}, u32[]{:S(2)}) %collective-permute-start.49) | collective-permute-done | bytes 98336 | tf_op jit(solution)/shard_map/ppermute | solution.py:615
  239.0 4.6 %attention_grad.3 = (bf16[208,768]{1,0:T(8,128)(2,1)S(1)}, bf16[208,768]{1,0:T(8,128)(2,1)S(1)}, bf16[208,768]{1,0:T(8,128)(2,1)S(1)}, bf16[208,768]{1,0:T(8,128)(2,1)S(1)}, f32[8,192]{1,0:T(8,128)}) custom-call(s32[4]{0:T(128)S(1)} %pad_add_fusion.refs_0_.place_ref, bf16[256,768]{1,0:T(8,128)(2,1)S(1)} %get-tuple-element.276.refs_1_, ...), custom_call_target="tpu_custom_call" | custom-call | flops 352321536 | bytes 2476032 | tf_op jit(solution)/shard_map/attention_grad/pallas_call | solution.py:94
  244.3 3.0 %collective-permute-done.78.refs_7_ = bf16[96,2304]{1,0:T(8,128)(2,1)S(1)} collective-permute-done((bf16[96,2304]{1,0:T(8,128)(2,1)S(1)}, bf16[96,2304]{1,0:T(8,128)(2,1)S(1)}, u32[]{:S(2)}, u32[]{:S(2)}) %collective-permute-start.78) | collective-permute-done | bytes 442400 | tf_op jit(solution)/shard_map/ppermute | solution.py:615
  277.2 6.3 %collective-permute-done.89.refs_5_ = bf16[96,1536]{1,0:T(8,128)(2,1)S(1)} collective-permute-done((bf16[96,1536]{1,0:T(8,128)(2,1)}, bf16[96,1536]{1,0:T(8,128)(2,1)S(1)}, u32[]{:S(2)}, u32[]{:S(2)}) %collective-permute-start.89) | collective-permute-done | bytes 294944 | tf_op jit(solution)/shard_map/ppermute | solution.py:615
  291.8 2.8 copy.77
  (336 shorter events, 168.7 us)
Async XLA Ops:
  21.4 13.1 %collective-permute-start.13 = (bf16[96,1536]{1,0:T(8,128)(2,1)S(1)}, bf16[96,1536]{1,0:T(8,128)(2,1)S(1)}, u32[]{:S(2)}, u32[]{:S(2)}) collective-permute-start(bf16[96,1536]{1,0:T(8,128)(2,1)S(1)} %pack_mlp.1), channel_id=1, source_target_pairs={{0,0},{1,1},{2,2},{3,3},{4,6},{5,7},{6,4},{7,5},{8,8},{9,9},{10,10... | collective-permute-start | bytes 884744 | tf_op jit(solution)/shard_map/ppermute | solution.py:615
  22.1 12.4 %collective-permute-start.14 = (bf16[96,1536]{1,0:T(8,128)(2,1)S(1)}, bf16[96,1536]{1,0:T(8,128)(2,1)S(1)}, u32[]{:S(2)}, u32[]{:S(2)}) collective-permute-start(bf16[96,1536]{1,0:T(8,128)(2,1)S(1)} %pack_mlp.1), channel_id=1, source_target_pairs={{0,6},{1,7},{2,4},{3,5},{4,0},{5,1},{6,2},{7,3},{8,14},{9,15},{10,... | collective-permute-start | bytes 884744 | tf_op jit(solution)/shard_map/ppermute | solution.py:615
  31.0 18.0 %collective-permute-start.7 = (bf16[2,112,768]{2,1,0:T(8,128)(2,1)S(1)}, bf16[2,112,768]{2,1,0:T(8,128)(2,1)S(1)}, u32[]{:S(2)}, u32[]{:S(2)}) collective-permute-start(bf16[2,112,768]{2,1,0:T(8,128)(2,1)S(1)} %couple.5.refs_0_), channel_id=1, source_target_pairs={{0,8},{1,9},{2,10},{3,11},{4,12},{5,13},{6,14},{7,15},{8,0},{9,1},... | collective-permute-start | bytes 1032200 | tf_op jit(solution)/shard_map/ppermute | solution.py:615
  32.2 17.6 %collective-permute-start.8 = (bf16[2,112,768]{2,1,0:T(8,128)(2,1)S(1)}, bf16[2,112,768]{2,1,0:T(8,128)(2,1)S(1)}, u32[]{:S(2)}, u32[]{:S(2)}) collective-permute-start(bf16[2,112,768]{2,1,0:T(8,128)(2,1)S(1)} %couple.5.refs_0_), channel_id=1, source_target_pairs={{0,16},{1,17},{2,18},{3,19},{4,20},{5,21},{6,22},{7,23},{8,24},{9,... | collective-permute-start | bytes 1032200 | tf_op jit(solution)/shard_map/ppermute | solution.py:615
  33.6 16.9 %collective-permute-start.9 = (bf16[2,112,768]{2,1,0:T(8,128)(2,1)S(1)}, bf16[2,112,768]{2,1,0:T(8,128)(2,1)S(1)}, u32[]{:S(2)}, u32[]{:S(2)}) collective-permute-start(bf16[2,112,768]{2,1,0:T(8,128)(2,1)S(1)} %couple.5.refs_0_), channel_id=1, source_target_pairs={{0,24},{1,25},{2,26},{3,27},{4,28},{5,29},{6,30},{7,31},{8,16},{9,... | collective-permute-start | bytes 1032200 | tf_op jit(solution)/shard_map/ppermute | solution.py:615
  53.4 16.0 %collective-permute-start.22 = (bf16[2,96,1536]{2,1,0:T(8,128)(2,1)S(1)}, bf16[2,96,1536]{2,1,0:T(8,128)(2,1)S(1)}, u32[]{:S(2)}, u32[]{:S(2)}) collective-permute-start(bf16[2,96,1536]{2,1,0:T(8,128)(2,1)S(1)} %couple.6.refs_0_), channel_id=1, source_target_pairs={{0,8},{1,9},{2,10},{3,11},{4,12},{5,13},{6,14},{7,15},{8,0},{9,1},... | collective-permute-start | bytes 1769480 | tf_op jit(solution)/shard_map/ppermute | solution.py:615
  54.1 15.3 %collective-permute-start.23 = (bf16[2,96,1536]{2,1,0:T(8,128)(2,1)S(1)}, bf16[2,96,1536]{2,1,0:T(8,128)(2,1)S(1)}, u32[]{:S(2)}, u32[]{:S(2)}) collective-permute-start(bf16[2,96,1536]{2,1,0:T(8,128)(2,1)S(1)} %couple.6.refs_0_), channel_id=1, source_target_pairs={{0,16},{1,17},{2,18},{3,19},{4,20},{5,21},{6,22},{7,23},{8,24},{9,... | collective-permute-start | bytes 1769480 | tf_op jit(solution)/shard_map/ppermute | solution.py:615
  69.6 22.0 %collective-permute-start.29 = (bf16[2,96,1536]{2,1,0:T(8,128)(2,1)S(1)}, bf16[2,96,1536]{2,1,0:T(8,128)(2,1)S(1)}, u32[]{:S(2)}, u32[]{:S(2)}) collective-permute-start(bf16[2,96,1536]{2,1,0:T(8,128)(2,1)S(1)} %couple.6.refs_0_), channel_id=1, source_target_pairs={{0,24},{1,25},{2,26},{3,27},{4,28},{5,29},{6,30},{7,31},{8,16},{9,... | collective-permute-start | bytes 1769480 | tf_op jit(solution)/shard_map/ppermute | solution.py:615
  72.0 18.7 %collective-permute-start.30 = (bf16[96,2304]{1,0:T(8,128)(2,1)S(1)}, bf16[96,2304]{1,0:T(8,128)(2,1)S(1)}, u32[]{:S(2)}, u32[]{:S(2)}) collective-permute-start(bf16[96,2304]{1,0:T(8,128)(2,1)S(1)} %pack_block.1), channel_id=1, source_target_pairs={{0,0},{1,1},{2,2},{3,3},{4,6},{5,7},{6,4},{7,5},{8,8},{9,9},{10,10... | collective-permute-start | bytes 1327112 | tf_op jit(solution)/shard_map/ppermute | solution.py:615
  72.7 18.1 %collective-permute-start.31 = (bf16[96,2304]{1,0:T(8,128)(2,1)S(1)}, bf16[96,2304]{1,0:T(8,128)(2,1)S(1)}, u32[]{:S(2)}, u32[]{:S(2)}) collective-permute-start(bf16[96,2304]{1,0:T(8,128)(2,1)S(1)} %pack_block.1), channel_id=1, source_target_pairs={{0,6},{1,7},{2,4},{3,5},{4,0},{5,1},{6,2},{7,3},{8,14},{9,15},{10,... | collective-permute-start | bytes 1327112 | tf_op jit(solution)/shard_map/ppermute | solution.py:615
  88.2 11.3 %collective-permute-start.26 = (bf16[64,768]{1,0:T(8,128)(2,1)S(1)}, bf16[64,768]{1,0:T(8,128)(2,1)S(1)}, u32[]{:S(2)}, u32[]{:S(2)}) collective-permute-start(bf16[64,768]{1,0:T(8,128)(2,1)S(1)} %get-tuple-element.192.refs_0_), channel_id=1, source_target_pairs={{0,1},{1,0},{2,3},{3,2},{4,5},{5,4},{6,7},{7,6},{8,9},{9,8},{10,11... | collective-permute-start | bytes 294920 | tf_op jit(solution)/shard_map/ppermute | solution.py:615
  91.6 12.5 %collective-permute-start.33 = (bf16[2,96,768]{2,1,0:T(8,128)(2,1)S(1)}, bf16[2,96,768]{2,1,0:T(8,128)(2,1)S(1)}, u32[]{:S(2)}, u32[]{:S(2)}) collective-permute-start(bf16[2,96,768]{2,1,0:T(8,128)(2,1)S(1)} %get-tuple-element.198.refs_0_), channel_id=1, source_target_pairs={{0,8},{1,9},{2,10},{3,11},{4,12},{5,13},{6,14},{7,15},{8,0},{9,1},... | collective-permute-start | bytes 884744 | tf_op jit(solution)/shard_map/ppermute | solution.py:615
  110.3 17.7 %collective-permute-start.40 = (bf16[2,96,1536]{2,1,0:T(8,128)(2,1)S(1)}, bf16[2,96,1536]{2,1,0:T(8,128)(2,1)S(1)}, u32[]{:S(2)}, u32[]{:S(2)}) collective-permute-start(bf16[2,96,1536]{2,1,0:T(8,128)(2,1)S(1)} %get-tuple-element.213.refs_0_), channel_id=1, source_target_pairs={{0,8},{1,9},{2,10},{3,11},{4,12},{5,13},{6,14},{7,15},{8,0},{9,1},... | collective-permute-start | bytes 1769480 | tf_op jit(solution)/shard_map/ppermute | solution.py:615
  111.6 16.4 %collective-permute-start.41 = (bf16[2,96,1536]{2,1,0:T(8,128)(2,1)S(1)}, bf16[2,96,1536]{2,1,0:T(8,128)(2,1)S(1)}, u32[]{:S(2)}, u32[]{:S(2)}) collective-permute-start(bf16[2,96,1536]{2,1,0:T(8,128)(2,1)S(1)} %get-tuple-element.213.refs_0_), channel_id=1, source_target_pairs={{0,16},{1,17},{2,18},{3,19},{4,20},{5,21},{6,22},{7,23},{8,24},{9,... | collective-permute-start | bytes 1769480 | tf_op jit(solution)/shard_map/ppermute | solution.py:615
  128.2 16.5 %collective-permute-start.47 = (bf16[2,96,1536]{2,1,0:T(8,128)(2,1)S(1)}, bf16[2,96,1536]{2,1,0:T(8,128)(2,1)S(1)}, u32[]{:S(2)}, u32[]{:S(2)}) collective-permute-start(bf16[2,96,1536]{2,1,0:T(8,128)(2,1)S(1)} %get-tuple-element.213.refs_0_), channel_id=1, source_target_pairs={{0,24},{1,25},{2,26},{3,27},{4,28},{5,29},{6,30},{7,31},{8,16},{9,... | collective-permute-start | bytes 1769480 | tf_op jit(solution)/shard_map/ppermute | solution.py:615
  154.5 18.2 %collective-permute-start.64 = (bf16[192,1536]{1,0:T(8,128)(2,1)S(1)}, bf16[192,1536]{1,0:T(8,128)(2,1)S(1)}, u32[]{:S(2)}, u32[]{:S(2)}) collective-permute-start(bf16[192,1536]{1,0:T(8,128)(2,1)S(1)} %get-tuple-element.257), channel_id=1, source_target_pairs={{0,8},{1,9},{2,10},{3,11},{4,12},{5,13},{6,14},{7,15},{8,0},{9,1},... | collective-permute-start | bytes 1769480 | tf_op jit(solution)/shard_map/ppermute | solution.py:615
  155.2 17.5 %collective-permute-start.65 = (bf16[192,1536]{1,0:T(8,128)(2,1)S(1)}, bf16[192,1536]{1,0:T(8,128)(2,1)S(1)}, u32[]{:S(2)}, u32[]{:S(2)}) collective-permute-start(bf16[192,1536]{1,0:T(8,128)(2,1)S(1)} %get-tuple-element.258), channel_id=1, source_target_pairs={{0,16},{1,17},{2,18},{3,19},{4,20},{5,21},{6,22},{7,23},{8,24},{9,... | collective-permute-start | bytes 1769480 | tf_op jit(solution)/shard_map/ppermute | solution.py:615
  172.8 16.5 %collective-permute-start.66 = (bf16[192,1536]{1,0:T(8,128)(2,1)S(1)}, bf16[192,1536]{1,0:T(8,128)(2,1)S(1)}, u32[]{:S(2)}, u32[]{:S(2)}) collective-permute-start(bf16[192,1536]{1,0:T(8,128)(2,1)S(1)} %get-tuple-element.259), channel_id=1, source_target_pairs={{0,24},{1,25},{2,26},{3,27},{4,28},{5,29},{6,30},{7,31},{8,16},{9,... | collective-permute-start | bytes 1769480 | tf_op jit(solution)/shard_map/ppermute | solution.py:615
  190.9 13.8 %collective-permute-start.71 = (bf16[192,768]{1,0:T(8,128)(2,1)S(1)}, bf16[192,768]{1,0:T(8,128)(2,1)S(1)}, u32[]{:S(2)}, u32[]{:S(2)}) collective-permute-start(bf16[192,768]{1,0:T(8,128)(2,1)S(1)} %get-tuple-element.273), channel_id=1, source_target_pairs={{0,24},{1,25},{2,26},{3,27},{4,28},{5,29},{6,30},{7,31},{8,16},{9,... | collective-permute-start | bytes 884744 | tf_op jit(solution)/shard_map/ppermute | solution.py:615
  194.6 15.9 %collective-permute-start.67 = (bf16[128,768]{1,0:T(8,128)(2,1)S(1)}, bf16[128,768]{1,0:T(8,128)(2,1)S(1)}, u32[]{:S(2)}, u32[]{:S(2)}) collective-permute-start(bf16[128,768]{1,0:T(8,128)(2,1)S(1)} %get-tuple-element.262), channel_id=1, source_target_pairs={{0,4},{1,5},{2,6},{3,7},{4,0},{5,1},{6,2},{7,3},{8,12},{9,13},{10,... | collective-permute-start | bytes 589832 | tf_op jit(solution)/shard_map/ppermute | solution.py:615
  204.8 23.4 %collective-permute-start.75 = (bf16[192,1536]{1,0:T(8,128)(2,1)S(1)}, bf16[192,1536]{1,0:T(8,128)(2,1)S(1)}, u32[]{:S(2)}, u32[]{:S(2)}) collective-permute-start(bf16[192,1536]{1,0:T(8,128)(2,1)S(1)} %get-tuple-element.286), channel_id=1, source_target_pairs={{0,8},{1,9},{2,10},{3,11},{4,12},{5,13},{6,14},{7,15},{8,0},{9,1},... | collective-permute-start | bytes 1769480 | tf_op jit(solution)/shard_map/ppermute | solution.py:615
  205.8 22.4 %collective-permute-start.76 = (bf16[192,1536]{1,0:T(8,128)(2,1)S(1)}, bf16[192,1536]{1,0:T(8,128)(2,1)S(1)}, u32[]{:S(2)}, u32[]{:S(2)}) collective-permute-start(bf16[192,1536]{1,0:T(8,128)(2,1)S(1)} %get-tuple-element.288), channel_id=1, source_target_pairs={{0,16},{1,17},{2,18},{3,19},{4,20},{5,21},{6,22},{7,23},{8,24},{9,... | collective-permute-start | bytes 1769480 | tf_op jit(solution)/shard_map/ppermute | solution.py:615
  209.8 21.1 %collective-permute-start.79 = (bf16[96,2304]{1,0:T(8,128)(2,1)S(1)}, bf16[96,2304]{1,0:T(8,128)(2,1)S(1)}, u32[]{:S(2)}, u32[]{:S(2)}) collective-permute-start(bf16[96,2304]{1,0:T(8,128)(2,1)S(1)} %get-tuple-element.295), channel_id=1, source_target_pairs={{0,0},{1,1},{2,2},{3,3},{4,6},{5,7},{6,4},{7,5},{8,8},{9,9},{10,10... | collective-permute-start | bytes 1327112 | tf_op jit(solution)/shard_map/ppermute | solution.py:615
  228.2 19.1 %collective-permute-start.77 = (bf16[192,1536]{1,0:T(8,128)(2,1)S(1)}, bf16[192,1536]{1,0:T(8,128)(2,1)S(1)}, u32[]{:S(2)}, u32[]{:S(2)}) collective-permute-start(bf16[192,1536]{1,0:T(8,128)(2,1)S(1)} %get-tuple-element.289), channel_id=1, source_target_pairs={{0,24},{1,25},{2,26},{3,27},{4,28},{5,29},{6,30},{7,31},{8,16},{9,... | collective-permute-start | bytes 1769480 | tf_op jit(solution)/shard_map/ppermute | solution.py:615
  231.7 15.6 %collective-permute-start.78 = (bf16[96,2304]{1,0:T(8,128)(2,1)S(1)}, bf16[96,2304]{1,0:T(8,128)(2,1)S(1)}, u32[]{:S(2)}, u32[]{:S(2)}) collective-permute-start(bf16[96,2304]{1,0:T(8,128)(2,1)S(1)} %get-tuple-element.291), channel_id=1, source_target_pairs={{0,4},{1,5},{2,6},{3,7},{4,2},{5,3},{6,0},{7,1},{8,12},{9,13},{10,... | collective-permute-start | bytes 1327112 | tf_op jit(solution)/shard_map/ppermute | solution.py:615
  250.8 15.9 %collective-permute-start.83 = (bf16[208,768]{1,0:T(8,128)(2,1)}, bf16[208,768]{1,0:T(8,128)(2,1)}, u32[]{:S(2)}, u32[]{:S(2)}) collective-permute-start(bf16[208,768]{1,0:T(8,128)(2,1)} %copy-done.10), channel_id=1, source_target_pairs={{0,8},{1,9},{2,10},{3,11},{4,12},{5,13},{6,14},{7,15},{8,0},{9,1},... | collective-permute-start | bytes 958472 | tf_op jit(solution)/shard_map/ppermute | solution.py:615
  251.2 15.4 %collective-permute-start.84 = (bf16[208,768]{1,0:T(8,128)(2,1)}, bf16[208,768]{1,0:T(8,128)(2,1)}, u32[]{:S(2)}, u32[]{:S(2)}) collective-permute-start(bf16[208,768]{1,0:T(8,128)(2,1)} %copy-done.9), channel_id=1, source_target_pairs={{0,16},{1,17},{2,18},{3,19},{4,20},{5,21},{6,22},{7,23},{8,24},{9,... | collective-permute-start | bytes 958472 | tf_op jit(solution)/shard_map/ppermute | solution.py:615
  252.6 15.7 %collective-permute-start.85 = (bf16[208,768]{1,0:T(8,128)(2,1)}, bf16[208,768]{1,0:T(8,128)(2,1)}, u32[]{:S(2)}, u32[]{:S(2)}) collective-permute-start(bf16[208,768]{1,0:T(8,128)(2,1)} %copy-done.8), channel_id=1, source_target_pairs={{0,24},{1,25},{2,26},{3,27},{4,28},{5,29},{6,30},{7,31},{8,16},{9,... | collective-permute-start | bytes 958472 | tf_op jit(solution)/shard_map/ppermute | solution.py:615
  264.0 13.2 %collective-permute-start.88 = (bf16[96,1536]{1,0:T(8,128)(2,1)}, bf16[96,1536]{1,0:T(8,128)(2,1)S(1)}, u32[]{:S(2)}, u32[]{:S(2)}) collective-permute-start(bf16[96,1536]{1,0:T(8,128)(2,1)} %get-tuple-element.310), channel_id=1, source_target_pairs={{0,0},{1,1},{2,2},{3,3},{4,6},{5,7},{6,4},{7,5},{8,8},{9,9},{10,10... | collective-permute-start | bytes 884744 | tf_op jit(solution)/shard_map/ppermute | solution.py:615
  265.6 17.9 %collective-permute-start.89 = (bf16[96,1536]{1,0:T(8,128)(2,1)}, bf16[96,1536]{1,0:T(8,128)(2,1)S(1)}, u32[]{:S(2)}, u32[]{:S(2)}) collective-permute-start(bf16[96,1536]{1,0:T(8,128)(2,1)} %get-tuple-element.311), channel_id=1, source_target_pairs={{0,4},{1,5},{2,6},{3,7},{4,2},{5,3},{6,0},{7,1},{8,12},{9,13},{10,... | collective-permute-start | bytes 884744 | tf_op jit(solution)/shard_map/ppermute | solution.py:615
  275.2 22.9 %collective-permute-start.82 = (f32[64,768]{1,0:T(8,128)S(1)}, f32[64,768]{1,0:T(8,128)S(1)}, u32[]{:S(2)}, u32[]{:S(2)}) collective-permute-start(f32[64,768]{1,0:T(8,128)S(1)} %get-tuple-element.299), channel_id=1, source_target_pairs={{0,0},{1,1},{2,4},{3,5},{4,2},{5,3},{6,6},{7,7},{8,8},{9,9},{10,12... | collective-permute-start | bytes 589832 | tf_op jit(solution)/shard_map/ppermute | solution.py:615
  275.9 19.6 %collective-permute-start.86 = (bf16[112,768]{1,0:T(8,128)(2,1)S(1)}, bf16[112,768]{1,0:T(8,128)(2,1)S(1)}, u32[]{:S(2)}, u32[]{:S(2)}) collective-permute-start(bf16[112,768]{1,0:T(8,128)(2,1)S(1)} %get-tuple-element.307), channel_id=1, source_target_pairs={{0,0},{1,1},{2,2},{3,3},{4,6},{5,7},{6,4},{7,5},{8,8},{9,9},{10,10... | collective-permute-start | bytes 516104 | tf_op jit(solution)/shard_map/ppermute | solution.py:615
  (92 other events, 601.0 us)

commit v6 on v4

--- a/solution.py
+++ b/solution.py
@@ -1059,9 +1059,8 @@
     cond_total = jnp.where(
         core == 0, jnp.stack([cond_mine, cond_sent], axis=1), jnp.stack([cond_sent, cond_mine], axis=1)
     ).reshape(1, D)
-    cond_total = gate(cond_total, *near_attention)
     cond_total = cond_total + xor(cond_total, PARITY)
-    cond_total = cond_total + xor(cond_total, HALF)
+    cond_total = gate(cond_total + xor(cond_total, HALF), *near_attention)
     sigmoid_cond = jax.nn.sigmoid(cond_full)
     grad_condition = cond_total * sigmoid_cond * (1.0 + cond_full * (1.0 - sigmoid_cond))
 

time: 311 us -> 316 us (1.016)
  starting transfers between devices: 130 us -> 136 us
    ppermute x102, starting transfers between devices: 130 us -> 136 us  [move(): return lax.ppermute(values, AXES, [(i, target(i)) for i in range(n_all)])]
    unnamed x49 -> x47, local copies, waits for them, and re-layouts: 8.2 us -> 7.23 us
  transfers between devices with their start and end apart: 102 -> 102, of which waited for: 41 -> 40; matrix products, arithmetic and copies ran while one was open for 5% -> 4% of each run, Pallas kernels for 20% -> 19%
where the time goes in v6:
time: 316 us; the launch traced here: 310 us
  starting transfers between devices  136 us (43%)
  waiting for transfers between devices  82.8 us (26%)
  Pallas kernels  63.5 us (20%)
  local copies, waits for them, and re-layouts  15.5 us (5%)
  other arithmetic  6.57 us (2%)
  matrix products  3.7 us (1%)
    ppermute x102, starting transfers between devices, move(): return lax.ppermute(values, AXES, [(i, target(i)) for i in range(n_all)])  136 us
    ppermute x102, waiting for transfers between devices, move(): return lax.ppermute(values, AXES, [(i, target(i)) for i in range(n_all)])  82.8 us
    pallas_call x37, Pallas kernels, call(): pl.pallas_call(run, out_shape=out_shape, in_specs=in_specs, out_specs=out...  59.6 us
    unnamed x47, local copies, waits for them, and re-layouts  7.23 us
  transfers between devices with their start and end apart: 102, of which 40 were waited for; matrix products, arithmetic and copies ran while one was open for 4% of the time, Pallas kernels for 19%

profile of v6, /device:TPU:0, one launch (start us, length us, event | category | flops | bytes accessed | tf_op | source)
XLA Modules:
  0.0 310.5 jit_solution(2364889030442325243)
XLA Ops:
  3.8 2.9 collective-permute-start.2
  22.1 3.6 %collective-permute-start.14 = (bf16[96,1536]{1,0:T(8,128)(2,1)S(1)}, bf16[96,1536]{1,0:T(8,128)(2,1)S(1)}, u32[]{:S(2)}, u32[]{:S(2)}) collective-permute-start(bf16[96,1536]{1,0:T(8,128)(2,1)S(1)} %pack_mlp.1), channel_id=1, source_target_pairs={{0,6},{1,7},{2,4},{3,5},{4,0},{5,1},{6,2},{7,3},{8,14},{9,15},{10,... | collective-permute-start | bytes 884744 | tf_op jit(solution)/shard_map/ppermute | solution.py:615
  35.2 8.2 %collective-permute-start.15 = (f32[2,2,6,192]{3,2,1,0:T(8,128)S(1)}, f32[2,2,6,192]{3,2,1,0:T(8,128)S(1)}, u32[]{:S(2)}, u32[]{:S(2)}) collective-permute-start(f32[2,2,6,192]{3,2,1,0:T(8,128)S(1)} %fusion.9), channel_id=1, source_target_pairs={{0,4},{1,5},{2,6},{3,7},{4,0},{5,1},{6,2},{7,3},{8,12},{9,13},{10,... | collective-permute-start | bytes 55304 | tf_op jit(solution)/shard_map/ppermute | solution.py:615
  45.0 4.0 %collective-permute-start.18 = (f32[2,6,192]{2,1,0:T(8,128)S(1)}, f32[2,6,192]{2,1,0:T(8,128)S(1)}, u32[]{:S(2)}, u32[]{:S(2)}) collective-permute-start(f32[2,6,192]{2,1,0:T(8,128)S(1)} %get-tuple-element.376), channel_id=1, source_target_pairs={{0,3},{1,2},{2,1},{3,0},{4,7},{5,6},{6,5},{7,4},{8,11},{9,10},{10,... | collective-permute-start | bytes 27656 | tf_op jit(solution)/shard_map/ppermute | solution.py:615
  56.9 5.7 %collective-permute-start.19 = (bf16[64,768]{1,0:T(8,128)(2,1)S(1)}, bf16[64,768]{1,0:T(8,128)(2,1)S(1)}, u32[]{:S(2)}, u32[]{:S(2)}) collective-permute-start(bf16[64,768]{1,0:T(8,128)(2,1)S(1)} %get-tuple-element.182.refs_0_), channel_id=1, source_target_pairs={{0,1},{1,0},{2,3},{3,2},{4,5},{5,4},{6,7},{7,6},{8,9},{9,8},{10,11... | collective-permute-start | bytes 294920 | tf_op jit(solution)/shard_map/ppermute | solution.py:615
  72.7 3.6 %collective-permute-start.31 = (bf16[96,2304]{1,0:T(8,128)(2,1)S(1)}, bf16[96,2304]{1,0:T(8,128)(2,1)S(1)}, u32[]{:S(2)}, u32[]{:S(2)}) collective-permute-start(bf16[96,2304]{1,0:T(8,128)(2,1)S(1)} %pack_block.1), channel_id=1, source_target_pairs={{0,6},{1,7},{2,4},{3,5},{4,0},{5,1},{6,2},{7,3},{8,14},{9,15},{10,... | collective-permute-start | bytes 1327112 | tf_op jit(solution)/shard_map/ppermute | solution.py:615
  76.3 5.1 %collective-permute-start.25 = (bf16[64,768]{1,0:T(8,128)(2,1)S(1)}, bf16[64,768]{1,0:T(8,128)(2,1)S(1)}, u32[]{:S(2)}, u32[]{:S(2)}) collective-permute-start(bf16[64,768]{1,0:T(8,128)(2,1)S(1)} %add_convert_fusion.7), channel_id=1, source_target_pairs={{0,1},{1,0},{2,3},{3,2},{4,5},{5,4},{6,7},{7,6},{8,9},{9,8},{10,11... | collective-permute-start | bytes 294920 | tf_op jit(solution)/shard_map/ppermute | solution.py:615
  81.4 6.0 %collective-permute-done.25.refs_4_ = bf16[64,768]{1,0:T(8,128)(2,1)S(1)} collective-permute-done((bf16[64,768]{1,0:T(8,128)(2,1)S(1)}, bf16[64,768]{1,0:T(8,128)(2,1)S(1)}, u32[]{:S(2)}, u32[]{:S(2)}) %collective-permute-start.25) | collective-permute-done | bytes 98336 | tf_op jit(solution)/shard_map/ppermute | solution.py:615
  93.6 5.9 %collective-permute-start.27 = (bf16[64,768]{1,0:T(8,128)(2,1)S(1)}, bf16[64,768]{1,0:T(8,128)(2,1)S(1)}, u32[]{:S(2)}, u32[]{:S(2)}) collective-permute-start(bf16[64,768]{1,0:T(8,128)(2,1)S(1)} %get-tuple-element.192.refs_0_), channel_id=1, source_target_pairs={{0,4},{1,5},{2,6},{3,7},{4,0},{5,1},{6,2},{7,3},{8,12},{9,13},{10,... | collective-permute-start | bytes 294920 | tf_op jit(solution)/shard_map/ppermute | solution.py:615
  104.1 5.4 %collective-permute-start.35 = (bf16[128,768]{1,0:T(8,128)(2,1)S(1)}, bf16[128,768]{1,0:T(8,128)(2,1)S(1)}, u32[]{:S(2)}, u32[]{:S(2)}) collective-permute-start(bf16[128,768]{1,0:T(8,128)(2,1)S(1)} %get-tuple-element.201), channel_id=1, source_target_pairs={{0,4},{1,5},{2,6},{3,7},{4,0},{5,1},{6,2},{7,3},{8,12},{9,13},{10,... | collective-permute-start | bytes 589832 | tf_op jit(solution)/shard_map/ppermute | solution.py:615
  115.9 2.8 collective-permute-done.36.refs_4_
  121.4 2.8 collective-permute-done.37.refs_1_
  131.9 3.0 collective-permute-done.43.refs_4_
  138.2 3.2 %collective-permute-done.44.refs_1_ = bf16[64,768]{1,0:T(8,128)(2,1)S(1)} collective-permute-done((bf16[64,768]{1,0:T(8,128)(2,1)S(1)}, bf16[64,768]{1,0:T(8,128)(2,1)S(1)}, u32[]{:S(2)}, u32[]{:S(2)}) %collective-permute-start.44) | collective-permute-done | bytes 98336 | tf_op jit(solution)/shard_map/ppermute | solution.py:615
  149.8 4.7 %mlp_grad.2 = (bf16[192,1536]{1,0:T(8,128)(2,1)S(1)}, bf16[192,1536]{1,0:T(8,128)(2,1)S(1)}, bf16[192,1536]{1,0:T(8,128)(2,1)S(1)}, bf16[192,1536]{1,0:T(8,128)(2,1)S(1)}, f32[8,192]{1,0:T(8,128)S(1)}) custom-call(s32[4]{0:T(128)S(1)} %pad_add_fusion.refs_0_.place_ref, bf16[256,768]{1,0:T(8,128)(2,1)S(1)} %get-tuple-element.222.refs_1_, ...), custom_call_target="tpu_custom_call" | custom-call | flops 603979776 | bytes 3938304 | tf_op jit(solution)/shard_map/mlp_grad/pallas_call | solution.py:94
  158.8 2.9 collective-permute-done.55.refs_4_
  164.7 2.9 collective-permute-done.56.refs_1_
  168.9 3.6 %attention_back.2 = (bf16[256,768]{1,0:T(8,128)(2,1)S(1)}, bf16[256,576]{1,0:T(8,128)(2,1)S(1)}, f32[64,768]{1,0:T(8,128)S(1)}, f32[64,768]{1,0:T(8,128)S(1)}, bf16[128,768]{1,0:T(8,128)(2,1)S(1)}) custom-call(bf16[64,768]{1,0:T(8,128)(2,1)S(1)} %get-tuple-element.233.refs_0_, bf16[64,768]{1,0:T(8,128)(2,1)S(1)} %collective-permute-done.56.refs_1_, ...), custom_call_target="tpu_custom_call" | custom-call | flops 704643072 | bytes 3145728 | tf_op jit(solution)/shard_map/attention_back/pallas_call | solution.py:94
  175.9 3.2 %attention_grad.2 = (bf16[192,768]{1,0:T(8,128)(2,1)S(1)}, bf16[192,768]{1,0:T(8,128)(2,1)S(1)}, bf16[192,768]{1,0:T(8,128)(2,1)S(1)}, bf16[192,768]{1,0:T(8,128)(2,1)S(1)}, f32[8,192]{1,0:T(8,128)S(1)}) custom-call(s32[4]{0:T(128)S(1)} %pad_add_fusion.refs_0_.place_ref, bf16[256,768]{1,0:T(8,128)(2,1)S(1)} %get-tuple-element.235.refs_1_, ...), custom_call_target="tpu_custom_call" | custom-call | flops 352321536 | bytes 2371584 | tf_op jit(solution)/shard_map/attention_grad/pallas_call | solution.py:94
  181.6 3.1 collective-permute-done.61.refs_1_
  184.7 4.5 %collective-permute-done.66.refs_8_ = bf16[192,1536]{1,0:T(8,128)(2,1)S(1)} collective-permute-done((bf16[192,1536]{1,0:T(8,128)(2,1)S(1)}, bf16[192,1536]{1,0:T(8,128)(2,1)S(1)}, u32[]{:S(2)}, u32[]{:S(2)}) %collective-permute-start.66) | collective-permute-done | bytes 589856 | tf_op jit(solution)/shard_map/ppermute | solution.py:615
  194.7 4.7 %mlp_grad.3 = (bf16[192,1536]{1,0:T(8,128)(2,1)S(1)}, bf16[192,1536]{1,0:T(8,128)(2,1)S(1)}, bf16[192,1536]{1,0:T(8,128)(2,1)S(1)}, bf16[192,1536]{1,0:T(8,128)(2,1)S(1)}, f32[8,192]{1,0:T(8,128)S(1)}) custom-call(s32[4]{0:T(128)S(1)} %pad_add_fusion.refs_0_.place_ref, bf16[256,768]{1,0:T(8,128)(2,1)S(1)} %get-tuple-element.251.refs_1_, ...), custom_call_target="tpu_custom_call" | custom-call | flops 603979776 | bytes 3938304 | tf_op jit(solution)/shard_map/mlp_grad/pallas_call | solution.py:94
  199.4 5.4 %collective-permute-done.71.refs_4_ = bf16[192,768]{1,0:T(8,128)(2,1)S(1)} collective-permute-done((bf16[192,768]{1,0:T(8,128)(2,1)S(1)}, bf16[192,768]{1,0:T(8,128)(2,1)S(1)}, u32[]{:S(2)}, u32[]{:S(2)}) %collective-permute-start.71) | collective-permute-done | bytes 294944 | tf_op jit(solution)/shard_map/ppermute | solution.py:615
  207.1 2.7 sum_parts.3
  212.4 3.2 %collective-permute-done.68.refs_4_ = bf16[64,768]{1,0:T(8,128)(2,1)S(1)} collective-permute-done((bf16[64,768]{1,0:T(8,128)(2,1)S(1)}, bf16[64,768]{1,0:T(8,128)(2,1)S(1)}, u32[]{:S(2)}, u32[]{:S(2)}) %collective-permute-start.68) | collective-permute-done | bytes 98336 | tf_op jit(solution)/shard_map/ppermute | solution.py:615
  224.8 3.4 %attention_back.3 = (bf16[256,768]{1,0:T(8,128)(2,1)S(1)}, bf16[256,576]{1,0:T(8,128)(2,1)S(1)}, f32[64,768]{1,0:T(8,128)S(1)}, f32[64,768]{1,0:T(8,128)S(1)}, bf16[128,768]{1,0:T(8,128)(2,1)S(1)}) custom-call(bf16[64,768]{1,0:T(8,128)(2,1)S(1)} %get-tuple-element.274.refs_0_, bf16[64,768]{1,0:T(8,128)(2,1)S(1)} %collective-permute-done.72.refs_1_, ...), custom_call_target="tpu_custom_call" | custom-call | flops 704643072 | bytes 3145728 | tf_op jit(solution)/shard_map/attention_back/pallas_call | solution.py:94
  231.9 5.9 %collective-permute-done.49.refs_4_ = bf16[64,768]{1,0:T(8,128)(2,1)S(1)} collective-permute-done((bf16[64,768]{1,0:T(8,128)(2,1)S(1)}, bf16[64,768]{1,0:T(8,128)(2,1)S(1)}, u32[]{:S(2)}, u32[]{:S(2)}) %collective-permute-start.49) | collective-permute-done | bytes 98336 | tf_op jit(solution)/shard_map/ppermute | solution.py:615
  239.0 4.6 %attention_grad.3 = (bf16[208,768]{1,0:T(8,128)(2,1)S(1)}, bf16[208,768]{1,0:T(8,128)(2,1)S(1)}, bf16[208,768]{1,0:T(8,128)(2,1)S(1)}, bf16[208,768]{1,0:T(8,128)(2,1)S(1)}, f32[8,192]{1,0:T(8,128)}) custom-call(s32[4]{0:T(128)S(1)} %pad_add_fusion.refs_0_.place_ref, bf16[256,768]{1,0:T(8,128)(2,1)S(1)} %get-tuple-element.276.refs_1_, ...), custom_call_target="tpu_custom_call" | custom-call | flops 352321536 | bytes 2476032 | tf_op jit(solution)/shard_map/attention_grad/pallas_call | solution.py:94
  244.3 3.0 collective-permute-done.78.refs_7_
  275.9 5.3 %collective-permute-done.89.refs_5_ = bf16[96,1536]{1,0:T(8,128)(2,1)S(1)} collective-permute-done((bf16[96,1536]{1,0:T(8,128)(2,1)}, bf16[96,1536]{1,0:T(8,128)(2,1)S(1)}, u32[]{:S(2)}, u32[]{:S(2)}) %collective-permute-start.89) | collective-permute-done | bytes 294944 | tf_op jit(solution)/shard_map/ppermute | solution.py:615
  293.0 5.1 %collective-permute-start.100 = (f32[1,768]{1,0:T(1,128)S(1)}, f32[1,768]{1,0:T(1,128)S(1)}, u32[]{:S(2)}, u32[]{:S(2)}) collective-permute-start(f32[1,768]{1,0:T(1,128)S(1)} %select_n.138), channel_id=1, source_target_pairs={{0,1},{1,0},{2,3},{3,2},{4,5},{5,4},{6,7},{7,6},{8,9},{9,8},{10,11... | collective-permute-start | bytes 9224 | tf_op jit(solution)/shard_map/ppermute | solution.py:615
  302.4 2.8 copy.77
  (335 shorter events, 175.2 us)
Async XLA Ops:
  21.4 13.1 %collective-permute-start.13 = (bf16[96,1536]{1,0:T(8,128)(2,1)S(1)}, bf16[96,1536]{1,0:T(8,128)(2,1)S(1)}, u32[]{:S(2)}, u32[]{:S(2)}) collective-permute-start(bf16[96,1536]{1,0:T(8,128)(2,1)S(1)} %pack_mlp.1), channel_id=1, source_target_pairs={{0,0},{1,1},{2,2},{3,3},{4,6},{5,7},{6,4},{7,5},{8,8},{9,9},{10,10... | collective-permute-start | bytes 884744 | tf_op jit(solution)/shard_map/ppermute | solution.py:615
  22.1 12.4 %collective-permute-start.14 = (bf16[96,1536]{1,0:T(8,128)(2,1)S(1)}, bf16[96,1536]{1,0:T(8,128)(2,1)S(1)}, u32[]{:S(2)}, u32[]{:S(2)}) collective-permute-start(bf16[96,1536]{1,0:T(8,128)(2,1)S(1)} %pack_mlp.1), channel_id=1, source_target_pairs={{0,6},{1,7},{2,4},{3,5},{4,0},{5,1},{6,2},{7,3},{8,14},{9,15},{10,... | collective-permute-start | bytes 884744 | tf_op jit(solution)/shard_map/ppermute | solution.py:615
  31.0 18.0 %collective-permute-start.7 = (bf16[2,112,768]{2,1,0:T(8,128)(2,1)S(1)}, bf16[2,112,768]{2,1,0:T(8,128)(2,1)S(1)}, u32[]{:S(2)}, u32[]{:S(2)}) collective-permute-start(bf16[2,112,768]{2,1,0:T(8,128)(2,1)S(1)} %couple.5.refs_0_), channel_id=1, source_target_pairs={{0,8},{1,9},{2,10},{3,11},{4,12},{5,13},{6,14},{7,15},{8,0},{9,1},... | collective-permute-start | bytes 1032200 | tf_op jit(solution)/shard_map/ppermute | solution.py:615
  32.2 17.6 %collective-permute-start.8 = (bf16[2,112,768]{2,1,0:T(8,128)(2,1)S(1)}, bf16[2,112,768]{2,1,0:T(8,128)(2,1)S(1)}, u32[]{:S(2)}, u32[]{:S(2)}) collective-permute-start(bf16[2,112,768]{2,1,0:T(8,128)(2,1)S(1)} %couple.5.refs_0_), channel_id=1, source_target_pairs={{0,16},{1,17},{2,18},{3,19},{4,20},{5,21},{6,22},{7,23},{8,24},{9,... | collective-permute-start | bytes 1032200 | tf_op jit(solution)/shard_map/ppermute | solution.py:615
  33.6 16.9 %collective-permute-start.9 = (bf16[2,112,768]{2,1,0:T(8,128)(2,1)S(1)}, bf16[2,112,768]{2,1,0:T(8,128)(2,1)S(1)}, u32[]{:S(2)}, u32[]{:S(2)}) collective-permute-start(bf16[2,112,768]{2,1,0:T(8,128)(2,1)S(1)} %couple.5.refs_0_), channel_id=1, source_target_pairs={{0,24},{1,25},{2,26},{3,27},{4,28},{5,29},{6,30},{7,31},{8,16},{9,... | collective-permute-start | bytes 1032200 | tf_op jit(solution)/shard_map/ppermute | solution.py:615
  53.4 16.0 %collective-permute-start.22 = (bf16[2,96,1536]{2,1,0:T(8,128)(2,1)S(1)}, bf16[2,96,1536]{2,1,0:T(8,128)(2,1)S(1)}, u32[]{:S(2)}, u32[]{:S(2)}) collective-permute-start(bf16[2,96,1536]{2,1,0:T(8,128)(2,1)S(1)} %couple.6.refs_0_), channel_id=1, source_target_pairs={{0,8},{1,9},{2,10},{3,11},{4,12},{5,13},{6,14},{7,15},{8,0},{9,1},... | collective-permute-start | bytes 1769480 | tf_op jit(solution)/shard_map/ppermute | solution.py:615
  54.1 15.3 %collective-permute-start.23 = (bf16[2,96,1536]{2,1,0:T(8,128)(2,1)S(1)}, bf16[2,96,1536]{2,1,0:T(8,128)(2,1)S(1)}, u32[]{:S(2)}, u32[]{:S(2)}) collective-permute-start(bf16[2,96,1536]{2,1,0:T(8,128)(2,1)S(1)} %couple.6.refs_0_), channel_id=1, source_target_pairs={{0,16},{1,17},{2,18},{3,19},{4,20},{5,21},{6,22},{7,23},{8,24},{9,... | collective-permute-start | bytes 1769480 | tf_op jit(solution)/shard_map/ppermute | solution.py:615
  69.6 22.0 %collective-permute-start.29 = (bf16[2,96,1536]{2,1,0:T(8,128)(2,1)S(1)}, bf16[2,96,1536]{2,1,0:T(8,128)(2,1)S(1)}, u32[]{:S(2)}, u32[]{:S(2)}) collective-permute-start(bf16[2,96,1536]{2,1,0:T(8,128)(2,1)S(1)} %couple.6.refs_0_), channel_id=1, source_target_pairs={{0,24},{1,25},{2,26},{3,27},{4,28},{5,29},{6,30},{7,31},{8,16},{9,... | collective-permute-start | bytes 1769480 | tf_op jit(solution)/shard_map/ppermute | solution.py:615
  72.0 18.7 %collective-permute-start.30 = (bf16[96,2304]{1,0:T(8,128)(2,1)S(1)}, bf16[96,2304]{1,0:T(8,128)(2,1)S(1)}, u32[]{:S(2)}, u32[]{:S(2)}) collective-permute-start(bf16[96,2304]{1,0:T(8,128)(2,1)S(1)} %pack_block.1), channel_id=1, source_target_pairs={{0,0},{1,1},{2,2},{3,3},{4,6},{5,7},{6,4},{7,5},{8,8},{9,9},{10,10... | collective-permute-start | bytes 1327112 | tf_op jit(solution)/shard_map/ppermute | solution.py:615
  72.7 18.1 %collective-permute-start.31 = (bf16[96,2304]{1,0:T(8,128)(2,1)S(1)}, bf16[96,2304]{1,0:T(8,128)(2,1)S(1)}, u32[]{:S(2)}, u32[]{:S(2)}) collective-permute-start(bf16[96,2304]{1,0:T(8,128)(2,1)S(1)} %pack_block.1), channel_id=1, source_target_pairs={{0,6},{1,7},{2,4},{3,5},{4,0},{5,1},{6,2},{7,3},{8,14},{9,15},{10,... | collective-permute-start | bytes 1327112 | tf_op jit(solution)/shard_map/ppermute | solution.py:615
  91.6 12.5 %collective-permute-start.33 = (bf16[2,96,768]{2,1,0:T(8,128)(2,1)S(1)}, bf16[2,96,768]{2,1,0:T(8,128)(2,1)S(1)}, u32[]{:S(2)}, u32[]{:S(2)}) collective-permute-start(bf16[2,96,768]{2,1,0:T(8,128)(2,1)S(1)} %get-tuple-element.198.refs_0_), channel_id=1, source_target_pairs={{0,8},{1,9},{2,10},{3,11},{4,12},{5,13},{6,14},{7,15},{8,0},{9,1},... | collective-permute-start | bytes 884744 | tf_op jit(solution)/shard_map/ppermute | solution.py:615
  110.3 17.7 %collective-permute-start.40 = (bf16[2,96,1536]{2,1,0:T(8,128)(2,1)S(1)}, bf16[2,96,1536]{2,1,0:T(8,128)(2,1)S(1)}, u32[]{:S(2)}, u32[]{:S(2)}) collective-permute-start(bf16[2,96,1536]{2,1,0:T(8,128)(2,1)S(1)} %get-tuple-element.213.refs_0_), channel_id=1, source_target_pairs={{0,8},{1,9},{2,10},{3,11},{4,12},{5,13},{6,14},{7,15},{8,0},{9,1},... | collective-permute-start | bytes 1769480 | tf_op jit(solution)/shard_map/ppermute | solution.py:615
  111.6 16.4 %collective-permute-start.41 = (bf16[2,96,1536]{2,1,0:T(8,128)(2,1)S(1)}, bf16[2,96,1536]{2,1,0:T(8,128)(2,1)S(1)}, u32[]{:S(2)}, u32[]{:S(2)}) collective-permute-start(bf16[2,96,1536]{2,1,0:T(8,128)(2,1)S(1)} %get-tuple-element.213.refs_0_), channel_id=1, source_target_pairs={{0,16},{1,17},{2,18},{3,19},{4,20},{5,21},{6,22},{7,23},{8,24},{9,... | collective-permute-start | bytes 1769480 | tf_op jit(solution)/shard_map/ppermute | solution.py:615
  128.2 16.5 %collective-permute-start.47 = (bf16[2,96,1536]{2,1,0:T(8,128)(2,1)S(1)}, bf16[2,96,1536]{2,1,0:T(8,128)(2,1)S(1)}, u32[]{:S(2)}, u32[]{:S(2)}) collective-permute-start(bf16[2,96,1536]{2,1,0:T(8,128)(2,1)S(1)} %get-tuple-element.213.refs_0_), channel_id=1, source_target_pairs={{0,24},{1,25},{2,26},{3,27},{4,28},{5,29},{6,30},{7,31},{8,16},{9,... | collective-permute-start | bytes 1769480 | tf_op jit(solution)/shard_map/ppermute | solution.py:615
  154.5 18.2 %collective-permute-start.64 = (bf16[192,1536]{1,0:T(8,128)(2,1)S(1)}, bf16[192,1536]{1,0:T(8,128)(2,1)S(1)}, u32[]{:S(2)}, u32[]{:S(2)}) collective-permute-start(bf16[192,1536]{1,0:T(8,128)(2,1)S(1)} %get-tuple-element.257), channel_id=1, source_target_pairs={{0,8},{1,9},{2,10},{3,11},{4,12},{5,13},{6,14},{7,15},{8,0},{9,1},... | collective-permute-start | bytes 1769480 | tf_op jit(solution)/shard_map/ppermute | solution.py:615
  155.2 17.5 %collective-permute-start.65 = (bf16[192,1536]{1,0:T(8,128)(2,1)S(1)}, bf16[192,1536]{1,0:T(8,128)(2,1)S(1)}, u32[]{:S(2)}, u32[]{:S(2)}) collective-permute-start(bf16[192,1536]{1,0:T(8,128)(2,1)S(1)} %get-tuple-element.258), channel_id=1, source_target_pairs={{0,16},{1,17},{2,18},{3,19},{4,20},{5,21},{6,22},{7,23},{8,24},{9,... | collective-permute-start | bytes 1769480 | tf_op jit(solution)/shard_map/ppermute | solution.py:615
  172.8 16.5 %collective-permute-start.66 = (bf16[192,1536]{1,0:T(8,128)(2,1)S(1)}, bf16[192,1536]{1,0:T(8,128)(2,1)S(1)}, u32[]{:S(2)}, u32[]{:S(2)}) collective-permute-start(bf16[192,1536]{1,0:T(8,128)(2,1)S(1)} %get-tuple-element.259), channel_id=1, source_target_pairs={{0,24},{1,25},{2,26},{3,27},{4,28},{5,29},{6,30},{7,31},{8,16},{9,... | collective-permute-start | bytes 1769480 | tf_op jit(solution)/shard_map/ppermute | solution.py:615
  190.9 13.8 %collective-permute-start.71 = (bf16[192,768]{1,0:T(8,128)(2,1)S(1)}, bf16[192,768]{1,0:T(8,128)(2,1)S(1)}, u32[]{:S(2)}, u32[]{:S(2)}) collective-permute-start(bf16[192,768]{1,0:T(8,128)(2,1)S(1)} %get-tuple-element.273), channel_id=1, source_target_pairs={{0,24},{1,25},{2,26},{3,27},{4,28},{5,29},{6,30},{7,31},{8,16},{9,... | collective-permute-start | bytes 884744 | tf_op jit(solution)/shard_map/ppermute | solution.py:615
  194.6 15.9 %collective-permute-start.67 = (bf16[128,768]{1,0:T(8,128)(2,1)S(1)}, bf16[128,768]{1,0:T(8,128)(2,1)S(1)}, u32[]{:S(2)}, u32[]{:S(2)}) collective-permute-start(bf16[128,768]{1,0:T(8,128)(2,1)S(1)} %get-tuple-element.262), channel_id=1, source_target_pairs={{0,4},{1,5},{2,6},{3,7},{4,0},{5,1},{6,2},{7,3},{8,12},{9,13},{10,... | collective-permute-start | bytes 589832 | tf_op jit(solution)/shard_map/ppermute | solution.py:615
  204.8 23.4 %collective-permute-start.75 = (bf16[192,1536]{1,0:T(8,128)(2,1)S(1)}, bf16[192,1536]{1,0:T(8,128)(2,1)S(1)}, u32[]{:S(2)}, u32[]{:S(2)}) collective-permute-start(bf16[192,1536]{1,0:T(8,128)(2,1)S(1)} %get-tuple-element.286), channel_id=1, source_target_pairs={{0,8},{1,9},{2,10},{3,11},{4,12},{5,13},{6,14},{7,15},{8,0},{9,1},... | collective-permute-start | bytes 1769480 | tf_op jit(solution)/shard_map/ppermute | solution.py:615
  205.8 22.4 %collective-permute-start.76 = (bf16[192,1536]{1,0:T(8,128)(2,1)S(1)}, bf16[192,1536]{1,0:T(8,128)(2,1)S(1)}, u32[]{:S(2)}, u32[]{:S(2)}) collective-permute-start(bf16[192,1536]{1,0:T(8,128)(2,1)S(1)} %get-tuple-element.288), channel_id=1, source_target_pairs={{0,16},{1,17},{2,18},{3,19},{4,20},{5,21},{6,22},{7,23},{8,24},{9,... | collective-permute-start | bytes 1769480 | tf_op jit(solution)/shard_map/ppermute | solution.py:615
  209.8 21.1 %collective-permute-start.79 = (bf16[96,2304]{1,0:T(8,128)(2,1)S(1)}, bf16[96,2304]{1,0:T(8,128)(2,1)S(1)}, u32[]{:S(2)}, u32[]{:S(2)}) collective-permute-start(bf16[96,2304]{1,0:T(8,128)(2,1)S(1)} %get-tuple-element.295), channel_id=1, source_target_pairs={{0,0},{1,1},{2,2},{3,3},{4,6},{5,7},{6,4},{7,5},{8,8},{9,9},{10,10... | collective-permute-start | bytes 1327112 | tf_op jit(solution)/shard_map/ppermute | solution.py:615
  228.2 19.1 %collective-permute-start.77 = (bf16[192,1536]{1,0:T(8,128)(2,1)S(1)}, bf16[192,1536]{1,0:T(8,128)(2,1)S(1)}, u32[]{:S(2)}, u32[]{:S(2)}) collective-permute-start(bf16[192,1536]{1,0:T(8,128)(2,1)S(1)} %get-tuple-element.289), channel_id=1, source_target_pairs={{0,24},{1,25},{2,26},{3,27},{4,28},{5,29},{6,30},{7,31},{8,16},{9,... | collective-permute-start | bytes 1769480 | tf_op jit(solution)/shard_map/ppermute | solution.py:615
  231.7 15.6 %collective-permute-start.78 = (bf16[96,2304]{1,0:T(8,128)(2,1)S(1)}, bf16[96,2304]{1,0:T(8,128)(2,1)S(1)}, u32[]{:S(2)}, u32[]{:S(2)}) collective-permute-start(bf16[96,2304]{1,0:T(8,128)(2,1)S(1)} %get-tuple-element.291), channel_id=1, source_target_pairs={{0,4},{1,5},{2,6},{3,7},{4,2},{5,3},{6,0},{7,1},{8,12},{9,13},{10,... | collective-permute-start | bytes 1327112 | tf_op jit(solution)/shard_map/ppermute | solution.py:615
  250.8 16.0 %collective-permute-start.83 = (bf16[208,768]{1,0:T(8,128)(2,1)}, bf16[208,768]{1,0:T(8,128)(2,1)}, u32[]{:S(2)}, u32[]{:S(2)}) collective-permute-start(bf16[208,768]{1,0:T(8,128)(2,1)} %copy-done.10), channel_id=1, source_target_pairs={{0,8},{1,9},{2,10},{3,11},{4,12},{5,13},{6,14},{7,15},{8,0},{9,1},... | collective-permute-start | bytes 958472 | tf_op jit(solution)/shard_map/ppermute | solution.py:615
  251.2 15.6 %collective-permute-start.84 = (bf16[208,768]{1,0:T(8,128)(2,1)}, bf16[208,768]{1,0:T(8,128)(2,1)}, u32[]{:S(2)}, u32[]{:S(2)}) collective-permute-start(bf16[208,768]{1,0:T(8,128)(2,1)} %copy-done.9), channel_id=1, source_target_pairs={{0,16},{1,17},{2,18},{3,19},{4,20},{5,21},{6,22},{7,23},{8,24},{9,... | collective-permute-start | bytes 958472 | tf_op jit(solution)/shard_map/ppermute | solution.py:615
  252.6 15.7 %collective-permute-start.85 = (bf16[208,768]{1,0:T(8,128)(2,1)}, bf16[208,768]{1,0:T(8,128)(2,1)}, u32[]{:S(2)}, u32[]{:S(2)}) collective-permute-start(bf16[208,768]{1,0:T(8,128)(2,1)} %copy-done.8), channel_id=1, source_target_pairs={{0,24},{1,25},{2,26},{3,27},{4,28},{5,29},{6,30},{7,31},{8,16},{9,... | collective-permute-start | bytes 958472 | tf_op jit(solution)/shard_map/ppermute | solution.py:615
  264.0 11.8 %collective-permute-start.88 = (bf16[96,1536]{1,0:T(8,128)(2,1)}, bf16[96,1536]{1,0:T(8,128)(2,1)S(1)}, u32[]{:S(2)}, u32[]{:S(2)}) collective-permute-start(bf16[96,1536]{1,0:T(8,128)(2,1)} %get-tuple-element.310), channel_id=1, source_target_pairs={{0,0},{1,1},{2,2},{3,3},{4,6},{5,7},{6,4},{7,5},{8,8},{9,9},{10,10... | collective-permute-start | bytes 884744 | tf_op jit(solution)/shard_map/ppermute | solution.py:615
  265.8 15.4 %collective-permute-start.89 = (bf16[96,1536]{1,0:T(8,128)(2,1)}, bf16[96,1536]{1,0:T(8,128)(2,1)S(1)}, u32[]{:S(2)}, u32[]{:S(2)}) collective-permute-start(bf16[96,1536]{1,0:T(8,128)(2,1)} %get-tuple-element.311), channel_id=1, source_target_pairs={{0,4},{1,5},{2,6},{3,7},{4,2},{5,3},{6,0},{7,1},{8,12},{9,13},{10,... | collective-permute-start | bytes 884744 | tf_op jit(solution)/shard_map/ppermute | solution.py:615
  286.2 19.6 %collective-permute-start.82 = (f32[64,768]{1,0:T(8,128)S(1)}, f32[64,768]{1,0:T(8,128)S(1)}, u32[]{:S(2)}, u32[]{:S(2)}) collective-permute-start(f32[64,768]{1,0:T(8,128)S(1)} %get-tuple-element.299), channel_id=1, source_target_pairs={{0,0},{1,1},{2,4},{3,5},{4,2},{5,3},{6,6},{7,7},{8,8},{9,9},{10,12... | collective-permute-start | bytes 589832 | tf_op jit(solution)/shard_map/ppermute | solution.py:615
  289.3 16.5 %collective-permute-start.86 = (bf16[112,768]{1,0:T(8,128)(2,1)S(1)}, bf16[112,768]{1,0:T(8,128)(2,1)S(1)}, u32[]{:S(2)}, u32[]{:S(2)}) collective-permute-start(bf16[112,768]{1,0:T(8,128)(2,1)S(1)} %get-tuple-element.307), channel_id=1, source_target_pairs={{0,0},{1,1},{2,2},{3,3},{4,6},{5,7},{6,4},{7,5},{8,8},{9,9},{10,10... | collective-permute-start | bytes 516104 | tf_op jit(solution)/shard_map/ppermute | solution.py:615
  290.0 15.8 %collective-permute-start.87 = (bf16[112,768]{1,0:T(8,128)(2,1)S(1)}, bf16[112,768]{1,0:T(8,128)(2,1)S(1)}, u32[]{:S(2)}, u32[]{:S(2)}) collective-permute-start(bf16[112,768]{1,0:T(8,128)(2,1)S(1)} %get-tuple-element.308), channel_id=1, source_target_pairs={{0,4},{1,5},{2,6},{3,7},{4,2},{5,3},{6,0},{7,1},{8,12},{9,13},{10,... | collective-permute-start | bytes 516104 | tf_op jit(solution)/shard_map/ppermute | solution.py:615
  (91 other events, 611.0 us)
